TPU v7x, 256 devices: a whole 4x4x8 slice. The times are simulated.
256 devices in a mesh: pairs: 8 (over y, core), proj: 32 (over x, z).
Axes of the slice: x: 4, y: 4, z: 8, core: 2. Of those that a mesh axis runs over, the one named last changes fastest.
Arguments:
- q_fact: bfloat16 [98304, 32], P(('pairs', 'proj')), parts along dimension 0, may hold values from -6 to 6
- p_fact: bfloat16 [147456, 32], P(('pairs', 'proj')), parts along dimension 0, may hold values from -6 to 6
- q_cot: bfloat16 [98304, 2048], P(('pairs', 'proj')), parts along dimension 0, may hold values from -0.796875 to 0.796875
- p_cot: bfloat16 [147456, 2048], P(('pairs', 'proj')), parts along dimension 0, may hold values from -0.796875 to 0.796875
- passage_of: int32 [3072], P('pairs'), parts along dimension 0, may hold values from 0 to 383, each once
- projection: bfloat16 [32768, 4096], P('proj'), may hold values from -0.03125 to 0.03125
Outputs:
- features: float32 [3072, 4096], P(('pairs', 'proj')), parts along dimension 0
There are 8 independent parts, one for each index of `pairs`. A program takes and returns all parts, laid end to end along the dimension named above; an argument that names none is the same for every part. Nothing has to cross between parts.
Inputs may be any that keep to these rules, and one draw needn't show every extreme that they name: `passage_of`: each passage belongs to exactly one pair.
All inputs are finite; a program needn't handle non-finite values.
Results may differ from a plain program's by a relative error of at most 0.01.
Values may be sent and summed in bfloat16 or wider, within the bound.
No kernel may reach another device: no remote copies, remote signals or barrier semaphores. Data moves between devices by JAX's collectives and lax.ppermute only.
A program may use at most 64 MiB of HBM per device.

v0:
```python
import jax
import jax.numpy as jnp
from jax import lax
from jax.sharding import PartitionSpec as P

KV = 1024
R = 16
QLEN = 32
PLEN = 48


def slab_grads(cols, fact, length):
    cot3 = cols.reshape(-1, length, cols.shape[1])
    fact3 = fact.reshape(-1, length, fact.shape[1])
    grads = jnp.einsum("sta,str->sar", cot3, fact3, preferred_element_type=jnp.float32)
    return grads.reshape(grads.shape[0], -1).astype(jnp.bfloat16)


def local(q_fact, p_fact, q_cot, p_cot, passage_of, projection):
    rank = R
    q_cols, p_cols = (
        lax.all_to_all(q_cot, "proj", split_axis=1, concat_axis=0, tiled=True),
        lax.all_to_all(p_cot, "proj", split_axis=1, concat_axis=0, tiled=True),
    )
    q_all, p_all = (
        lax.all_gather(q_fact, "proj", axis=0, tiled=True),
        lax.all_gather(p_fact, "proj", axis=0, tiled=True),
    )
    width = q_cols.shape[1]
    layer_now = lax.axis_index("proj") * width // KV
    q_use = lax.dynamic_slice_in_dim(q_all, layer_now * rank, rank, 1)
    p_use = lax.dynamic_slice_in_dim(p_all, layer_now * rank, rank, 1)
    q_grad = slab_grads(q_cols, q_use, QLEN)
    p_grad = slab_grads(p_cols, p_use, PLEN)
    picked = jnp.take(p_grad, passage_of, axis=0)
    pair_grad = (q_grad.astype(jnp.float32) + picked.astype(jnp.float32)).astype(jnp.bfloat16)
    return lax.psum_scatter(
        jnp.dot(pair_grad, projection, preferred_element_type=jnp.float32),
        "proj",
        scatter_dimension=0,
        tiled=True,
    )


def solution(mesh):
    placed = (
        P(("pairs", "proj"), None),
        P(("pairs", "proj"), None),
        P(("pairs", "proj"), None),
        P(("pairs", "proj"), None),
        P("pairs"),
        P("proj", None),
    )
    return jax.shard_map(
        local, mesh=mesh, in_specs=placed, out_specs=P(("pairs", "proj"), None), check_vma=False
    )
```

profile of v0, /device:TPU:14, one launch (start us, length us, event | category | flops | bytes accessed | tf_op | source)
XLA Modules:
  0.0 383.5 jit_solution(8394632654484499471)
XLA Ops:
  6.5 2.6 copy.20
  9.1 11.6 %all-to-all-start = ((bf16[384,32,64]{0,2,1:T(8,128)(2,1)}), bf16[384,32,64]{0,2,1:T(8,128)(2,1)S(1)}, u32[]{:S(2)}, u32[]{:S(2)}) async-start(bf16[384,32,64]{0,2,1:T(8,128)(2,1)} %bitcast), calls=%async_computation | async-start | bytes 3145728 | tf_op jit(solution)/shard_map/all_to_all | solution.py:22
  20.7 0.0 all-gather.3.cloned.1.call-start
  20.8 0.7 all-gather.3.cloned.1.call-update
  21.5 4.4 %copy.25 = bf16[576,2048]{0,1:T(8,128)(2,1)} copy(bf16[576,2048]{1,0:T(8,128)(2,1)} %param.9) | data formatting | bytes 4718592 | tf_op args[3]
  25.9 33.0 %all-to-all-done = bf16[384,32,64]{0,2,1:T(8,128)(2,1)S(1)} async-done(((bf16[384,32,64]{0,2,1:T(8,128)(2,1)}), bf16[384,32,64]{0,2,1:T(8,128)(2,1)S(1)}, u32[]{:S(2)}, u32[]{:S(2)}) %all-to-all-start) | async-done | bytes 1572896 | tf_op jit(solution)/shard_map/all_to_all | solution.py:22
  58.9 0.0 copy-start
  58.9 0.0 copy-start.7
  58.9 1.2 copy-done
  60.1 8.0 %all-to-all-start.1 = ((bf16[576,32,64]{0,2,1:T(8,128)(2,1)}), bf16[576,32,64]{0,2,1:T(8,128)(2,1)}, u32[]{:S(2)}, u32[]{:S(2)}) async-start(bf16[576,32,64]{0,2,1:T(8,128)(2,1)} %bitcast.6), calls=%async_computation.1 | async-start | bytes 5242880 | tf_op jit(solution)/shard_map/all_to_all | solution.py:23
  68.0 0.0 copy-start.8
  68.1 0.0 copy-done.7
  68.1 105.3 %all_gather.6 = bf16[12288,32]{0,1:T(8,128)(2,1)S(1)} all-gather(bf16[384,32]{0,1:T(8,128)(2,1)S(1)} %copy-done.7), channel_id=1, replica_groups=mesh['pairs'=8,'proj'=32] {'proj'}, dimensions={0}, use_global_device_ids=true | all-gather | bytes 811008 | tf_op jit(solution)/shard_map/all_gather | solution.py:26
  173.4 2.4 reshape.31
  175.8 0.0 copy-done.8
  175.8 0.0 all-gather.3.cloned.1.call-done
  175.9 1.7 copy.24
  177.6 1.6 reshape.46
  179.2 2.5 reshape.33
  181.8 3.1 copy.21
  184.8 4.4 %convert_bitcast_fusion = f32[384,64,16]{1,2,0:T(8,128)} fusion(bf16[384,32,64]{2,1,0:T(8,128)(2,1)S(1)} %bitcast.26, bf16[384,32,16]{1,0,2:T(8,128)(2,1)} %reshape.31), kind=kOutput, calls=%fused_computation.1 | convolution fusion | flops 25952256 | bytes 3538944 | tf_op jit(solution)/shard_map/sta,str->sar/dot_general | solution.py:15
  189.2 2.4 copy.23
  191.6 1.6 copy.30
  193.2 0.0 all-to-all-done.1
  193.2 0.0 copy-start.1
  193.2 6.0 %copy.26 = bf16[32,576,64]{2,1,0:T(8,128)(2,1)} copy(bf16[32,576,64]{1,2,0:T(8,128)(2,1)} %bitcast.7) | data formatting | bytes 4718592 | tf_op jit(solution)/shard_map/all_to_all | solution.py:23
  199.2 0.0 copy-done.1
  199.2 3.8 fusion.3
  203.0 1.4 copy.28
  204.4 0.3 copy.29
  204.7 0.0 copy-start.2
  204.7 2.1 gather_fusion
  206.8 0.0 copy-done.2
  206.8 8.9 %fusion.6 = f32[384,4096]{1,0:T(8,128)} fusion(bf16[1024,4096]{1,0:T(8,128)(2,1)} %param.11, f32[384,1024]{1,0:T(8,128)S(1)} %copy-done.2, bf16[384,1024]{1,0:T(8,128)(2,1)S(1)} %gather_fusion, pred[384]{0:T(512)(128)(4,1)S(1)} %compare_and_fusion), kind=kOutput, calls=%fused_computation.8 | convolution fusion | flops 3222798336 | bytes 17039744 | tf_op jit(solution)/shard_map/dot_general | solution.py:38
  215.7 0.0 copy-start.9
  215.7 103.5 %fusion = f32[16,4096]{1,0:T(8,128)S(1)} fusion(f32[384,4096]{1,0:T(8,128)} %fusion.6), kind=kCustom, calls=%all-reduce-scatter | all-reduce-scatter fusion | flops 2097153 | bytes 6554624
  319.3 1.9 collective-permute-start
  321.2 4.0 %collective-permute-start.1 = (f32[16,4096]{1,0:T(8,128)S(1)}, f32[16,4096]{1,0:T(8,128)S(1)}, u32[]{:S(2)}, u32[]{:S(2)}) collective-permute-start(f32[16,4096]{1,0:T(8,128)S(1)} %fusion), channel_id=1, source_target_pairs={{0,2},{1,3},{2,4},{3,5},{4,6},{5,7},{6,8},{7,9},{8,10},{9,11},{10,... | collective-permute-start | bytes 786440
  325.2 1.3 collective-permute-start.7
  326.5 1.9 collective-permute-start.2
  328.5 1.9 collective-permute-start.3
  330.4 17.2 %collective-permute-done.7 = f32[12,4096]{1,0:T(8,128)S(1)} collective-permute-done((f32[12,4096]{1,0:T(8,128)S(1)}, f32[12,4096]{1,0:T(8,128)S(1)}, u32[]{:S(2)}, u32[]{:S(2)}) %collective-permute-start.7) | collective-permute-done | bytes 196640
  347.5 1.9 collective-permute-start.4
  349.5 0.0 collective-permute-done
  349.5 1.9 collective-permute-start.5
  351.4 0.0 collective-permute-done.1
  351.4 1.9 collective-permute-start.6
  353.3 0.0 copy-done.9
  353.4 0.6 dynamic-slice.4
  354.6 0.0 collective-permute-done.2
  354.6 0.0 copy-start.3
  354.6 0.0 collective-permute-done.3
  354.6 0.0 copy-start.4
  354.6 7.9 %collective-permute-done.4 = f32[16,4096]{1,0:T(8,128)S(1)} collective-permute-done((f32[16,4096]{1,0:T(8,128)S(1)}, f32[16,4096]{1,0:T(8,128)S(1)}, u32[]{:S(2)}, u32[]{:S(2)}) %collective-permute-start.4) | collective-permute-done | bytes 262176
  362.5 0.0 copy-start.5
  362.5 0.0 collective-permute-done.5
  362.5 0.0 copy-done.3
  362.5 0.0 copy-done.4
  362.5 0.7 copy-done.5
  363.2 0.0 copy-start.6
  363.2 0.7 copy-done.6
  363.9 1.2 collective-permute-done.6
  365.1 10.8 %concatenate = f32[140,4096]{1,0:T(8,128)S(1)} concatenate(f32[12,4096]{1,0:T(8,128)S(1)} %collective-permute-done.7, f32[16,4096]{1,0:T(8,128)} %collective-permute-done.6, f32[16,4096]{1,0:T(8,128)} %copy-done.6, f32[16,4096]{1,0:T(8,128)} %copy-done.5, f32[16,4096]{1,0:T(8,128)} %copy-done.4, f32[16,4096]{1,0:T(8,128)} %copy-done.3, f32[16,4096]{1,0:T(8,128)S(1)} %collective-permute-done.1, ...), dimensions={0} | concatenate | bytes 4587520
  375.9 0.7 constant_dynamic-slice_fusion
  (6 shorter events, 0.1 us)
Async XLA Ops:
  9.1 49.8 %all-to-all-start = ((bf16[384,32,64]{0,2,1:T(8,128)(2,1)}), bf16[384,32,64]{0,2,1:T(8,128)(2,1)S(1)}, u32[]{:S(2)}, u32[]{:S(2)}) async-start(bf16[384,32,64]{0,2,1:T(8,128)(2,1)} %bitcast), calls=%async_computation | async-start | bytes 3145728 | tf_op jit(solution)/shard_map/all_to_all | solution.py:22
  20.7 155.1 %all-gather.3.cloned.1.call-start = ((), (), s32[]{:S(2)}) async-start(), calls=%async_computation.2 | async-start | bytes 1351680 | tf_op jit(solution)/shard_map/all_gather | solution.py:27
  58.9 1.2 copy-start
  58.9 9.2 %copy-start.7 = (bf16[384,32]{0,1:T(8,128)(2,1)S(1)}, bf16[384,32]{0,1:T(8,128)(2,1)}, u32[]{:S(2)}) copy-start(bf16[384,32]{0,1:T(8,128)(2,1)} %param.6) | copy-start | bytes 73732
  60.1 133.2 %all-to-all-start.1 = ((bf16[576,32,64]{0,2,1:T(8,128)(2,1)}), bf16[576,32,64]{0,2,1:T(8,128)(2,1)}, u32[]{:S(2)}, u32[]{:S(2)}) async-start(bf16[576,32,64]{0,2,1:T(8,128)(2,1)} %bitcast.6), calls=%async_computation.1 | async-start | bytes 5242880 | tf_op jit(solution)/shard_map/all_to_all | solution.py:23
  68.0 107.8 %copy-start.8 = (s32[384]{0:T(512)S(1)}, s32[384]{0:T(512)}, u32[]{:S(2)}) copy-start(s32[384]{0:T(512)} %param.10) | copy-start | bytes 4612
  193.2 6.0 %copy-start.1 = (bf16[384,48,16]{1,0,2:T(8,128)(2,1)S(1)}, bf16[384,48,16]{1,0,2:T(8,128)(2,1)}, u32[]{:S(2)}) copy-start(bf16[384,48,16]{1,0,2:T(8,128)(2,1)} %reshape.33) | copy-start | bytes 1769476
  204.7 2.1 copy-start.2
  215.7 137.6 %copy-start.9 = (u32[256]{0:T(256)S(1)}, u32[256]{0:T(256)}, u32[]{:S(2)}) copy-start(u32[256]{0:T(256)} %constant.48) | copy-start | bytes 3076
  319.3 30.2 %collective-permute-start = (f32[16,4096]{1,0:T(8,128)S(1)}, f32[16,4096]{1,0:T(8,128)S(1)}, u32[]{:S(2)}, u32[]{:S(2)}) collective-permute-start(f32[16,4096]{1,0:T(8,128)S(1)} %fusion), channel_id=1, source_target_pairs={{0,1},{1,2},{2,3},{3,4},{4,5},{5,6},{6,7},{7,8},{8,9},{9,10},{10,1... | collective-permute-start | bytes 786440
  321.2 30.2 %collective-permute-start.1 = (f32[16,4096]{1,0:T(8,128)S(1)}, f32[16,4096]{1,0:T(8,128)S(1)}, u32[]{:S(2)}, u32[]{:S(2)}) collective-permute-start(f32[16,4096]{1,0:T(8,128)S(1)} %fusion), channel_id=1, source_target_pairs={{0,2},{1,3},{2,4},{3,5},{4,6},{5,7},{6,8},{7,9},{8,10},{9,11},{10,... | collective-permute-start | bytes 786440
  325.2 22.3 %collective-permute-start.7 = (f32[12,4096]{1,0:T(8,128)S(1)}, f32[12,4096]{1,0:T(8,128)S(1)}, u32[]{:S(2)}, u32[]{:S(2)}) collective-permute-start(f32[12,4096]{1,0:T(8,128)S(1)} %slice.2), channel_id=1, source_target_pairs={{0,8},{1,9},{2,10},{3,11},{4,12},{5,13},{6,14},{7,15},{8,16},{9,17... | collective-permute-start | bytes 589832
  326.5 28.1 %collective-permute-start.2 = (f32[16,4096]{1,0:T(8,128)S(1)}, f32[16,4096]{1,0:T(8,128)S(1)}, u32[]{:S(2)}, u32[]{:S(2)}) collective-permute-start(f32[16,4096]{1,0:T(8,128)S(1)} %fusion), channel_id=1, source_target_pairs={{0,3},{1,4},{2,5},{3,6},{4,7},{5,8},{6,9},{7,10},{8,11},{9,12},{10... | collective-permute-start | bytes 786440
  328.5 26.2 %collective-permute-start.3 = (f32[16,4096]{1,0:T(8,128)S(1)}, f32[16,4096]{1,0:T(8,128)S(1)}, u32[]{:S(2)}, u32[]{:S(2)}) collective-permute-start(f32[16,4096]{1,0:T(8,128)S(1)} %fusion), channel_id=1, source_target_pairs={{0,4},{1,5},{2,6},{3,7},{4,8},{5,9},{6,10},{7,11},{8,12},{9,13},{1... | collective-permute-start | bytes 786440
  347.5 15.0 %collective-permute-start.4 = (f32[16,4096]{1,0:T(8,128)S(1)}, f32[16,4096]{1,0:T(8,128)S(1)}, u32[]{:S(2)}, u32[]{:S(2)}) collective-permute-start(f32[16,4096]{1,0:T(8,128)S(1)} %fusion), channel_id=1, source_target_pairs={{0,5},{1,6},{2,7},{3,8},{4,9},{5,10},{6,11},{7,12},{8,13},{9,14},{... | collective-permute-start | bytes 786440
  349.5 13.0 %collective-permute-start.5 = (f32[16,4096]{1,0:T(8,128)S(1)}, f32[16,4096]{1,0:T(8,128)S(1)}, u32[]{:S(2)}, u32[]{:S(2)}) collective-permute-start(f32[16,4096]{1,0:T(8,128)S(1)} %fusion), channel_id=1, source_target_pairs={{0,6},{1,7},{2,8},{3,9},{4,10},{5,11},{6,12},{7,13},{8,14},{9,15},... | collective-permute-start | bytes 786440
  351.4 13.7 %collective-permute-start.6 = (f32[16,4096]{1,0:T(8,128)S(1)}, f32[16,4096]{1,0:T(8,128)}, u32[]{:S(2)}, u32[]{:S(2)}) collective-permute-start(f32[16,4096]{1,0:T(8,128)S(1)} %fusion), channel_id=1, source_target_pairs={{0,7},{1,8},{2,9},{3,10},{4,11},{5,12},{6,13},{7,14},{8,15},{9,16}... | collective-permute-start | bytes 786440
  354.6 7.9 %copy-start.3 = (f32[16,4096]{1,0:T(8,128)}, f32[16,4096]{1,0:T(8,128)S(1)}, u32[]{:S(2)}) copy-start(f32[16,4096]{1,0:T(8,128)S(1)} %collective-permute-done.2) | copy-start | bytes 786436
  354.6 7.9 %copy-start.4 = (f32[16,4096]{1,0:T(8,128)}, f32[16,4096]{1,0:T(8,128)S(1)}, u32[]{:S(2)}) copy-start(f32[16,4096]{1,0:T(8,128)S(1)} %collective-permute-done.3) | copy-start | bytes 786436
  362.5 0.7 copy-start.5
  363.2 0.7 copy-start.6
Sparse Core Ops, SparseCore 0:
  24.2 87.5 all-gather.2
where the time goes:
time: 389 us; the launch traced here: 383 us
  blocking collectives  209 us (54%)
  waiting for transfers between devices  60 us (15%)
  local copies, waits for them, and re-layouts  46.8 us (12%)
  starting transfers between devices  36.4 us (9%)
  matrix products  17.1 us (4%)
  between operations  14.4 us (4%)
    all_gather x1, blocking collectives, local(): lax.all_gather(q_fact, 'proj', axis=0, tiled=True)  105 us
    unnamed x1, blocking collectives  104 us
    all_to_all x1, waiting for transfers between devices, local(): lax.all_to_all(q_cot, 'proj', split_axis=1, concat_axis=0, tiled=True)  33 us
    unnamed x9, waiting for transfers between devices  26.9 us
    unnamed x27, local copies, waits for them, and re-layouts  23.3 us
    unnamed x8, starting transfers between devices  16.8 us
    all_to_all x1, starting transfers between devices, local(): lax.all_to_all(q_cot, 'proj', split_axis=1, concat_axis=0, tiled=True)  11.6 us
    dot_general x1, matrix products, local(): jnp.dot(pair_grad, projection, preferred_element_type=jnp.float32)  8.89 us
  transfers between devices with their start and end apart: 11, of which 4 were waited for; matrix products, arithmetic and copies ran while one was open for 6% of the time, Pallas kernels for 0%

commit v1 on v0

v1 whole, which is shorter than its diff:
```python
import jax
import jax.numpy as jnp
from jax import lax
from jax.experimental import pallas as pl
from jax.experimental.pallas import tpu as pltpu
from jax.sharding import Mesh, PartitionSpec as P

KV = 1024
R = 16
QLEN = 32
PLEN = 48
K = 4096
NX, NZ = 4, 8
N = NX * NZ
MINE = 12
PAIRS = N * MINE
ROWS = MINE * 8
VMEM = 60 * 1024 * 1024
BF = jnp.bfloat16
F32 = jnp.float32


def iota(shape, dim):
    return lax.broadcasted_iota(jnp.int32, shape, dim)


def dot(a, b):
    return lax.dot_general(a, b, (((1,), (0,)), ((), ())), preferred_element_type=F32)


def grads_kernel(qf, pf, qc, pc, out):
    layer = pl.program_id(0)
    lane = iota((ROWS, 128), 1)
    for kind, (fact, cot, length) in enumerate(((qf, qc, QLEN), (pf, pc, PLEN))):
        tokens = MINE * length
        row = iota((2 * ROWS, 2 * R), 0)
        rank = jnp.where(row >= ROWS, 8, 0) + (row & 7) + layer * R
        pick = jnp.where(iota((2 * ROWS, 2 * R), 1) == rank, 1.0, 0.0).astype(BF)
        row = iota((2 * ROWS, tokens), 0)
        item = jnp.where(row >= ROWS, row - ROWS, row) >> 3
        token = iota((2 * ROWS, tokens), 1) - item * length
        spread = jnp.where((token >= 0) & (token < length), dot(pick, fact[...]), 0.0)
        grad = dot(spread.astype(BF), cot[...])
        for j in range(8):
            top = grad[:ROWS, 128 * j : 128 * j + 128]
            low = grad[ROWS:, 128 * j : 128 * j + 128]
            even = jnp.where(lane < 64, top, pltpu.roll(low, 64, 1))
            odd = jnp.where(lane < 64, pltpu.roll(top, 64, 1), low)
            out[2 * j, kind * ROWS : kind * ROWS + ROWS, :] = even.astype(BF)
            out[2 * j + 1, kind * ROWS : kind * ROWS + ROWS, :] = odd.astype(BF)


def grads(q_fact, p_fact, q_cot, p_cot):
    return pl.pallas_call(
        grads_kernel,
        grid=(2,),
        in_specs=[
            pl.BlockSpec((2 * R, MINE * QLEN), lambda l: (0, 0)),
            pl.BlockSpec((2 * R, MINE * PLEN), lambda l: (0, 0)),
            pl.BlockSpec((MINE * QLEN, KV), lambda l: (0, l)),
            pl.BlockSpec((MINE * PLEN, KV), lambda l: (0, l)),
        ],
        out_specs=pl.BlockSpec((N // 2, 2 * ROWS, 128), lambda l: (l, 0, 0)),
        out_shape=jax.ShapeDtypeStruct((N, 2 * ROWS, 128), BF),
        compiler_params=pltpu.CompilerParams(vmem_limit_bytes=VMEM),
        cost_estimate=pl.CostEstimate(flops=800_000_000, bytes_accessed=5_500_000, transcendentals=0),
    )(q_fact.T, p_fact.T, q_cot, p_cot)


def product_kernel(recv, passage, order, proj, out, wide_q, wide_p, pair):
    @pl.when(pl.program_id(0) == 0)
    def _():
        r, c = iota((256, 256), 0), iota((256, 256), 1)
        swap = jnp.where(c == (r & 31) * 8 + (r >> 5), 1.0, 0.0).astype(BF)
        for g in range(PAIRS // 32):
            parts = []
            for kind in range(2):
                pieces, at, need = [], g * 256, 256
                while need:
                    src, off = at // ROWS, at % ROWS
                    take = min(ROWS - off, need)
                    pieces.append(recv[src, kind * ROWS + off : kind * ROWS + off + take, :])
                    at, need = at + take, need - take
                parts.append(jnp.concatenate(pieces, axis=0))
            mixed = dot(swap, jnp.concatenate(parts, axis=1)).astype(BF)
            for b in range(8):
                wide_q[32 * g : 32 * g + 32, 128 * b : 128 * b + 128] = mixed[32 * b : 32 * b + 32, :128]
                wide_p[32 * g : 32 * g + 32, 128 * b : 128 * b + 128] = mixed[32 * b : 32 * b + 32, 128:]
        hot = jnp.where(iota((PAIRS, PAIRS), 0) == passage[...], 1.0, 0.0).astype(BF)
        picked = lax.dot_general(hot, wide_p[...], (((0,), (0,)), ((), ())), preferred_element_type=F32)
        summed = (wide_q[...].astype(F32) + picked).astype(BF)
        pair[...] = dot(summed, order[...]).astype(BF)

    out[...] = dot(pair[...], proj[...]).astype(BF)


def product(recv, passage_of, projection):
    u, v = iota((1024, 1024), 0), iota((1024, 1024), 1)
    order = jnp.where(v == (u & 63) * 16 + ((u >> 6) & 1) * 8 + (u >> 7), 1.0, 0.0).astype(BF)
    tile = 512
    return pl.pallas_call(
        product_kernel,
        grid=(K // tile,),
        in_specs=[
            pl.BlockSpec((N, 2 * ROWS, 128), lambda n: (0, 0, 0)),
            pl.BlockSpec((1, PAIRS), lambda n: (0, 0)),
            pl.BlockSpec((1024, 1024), lambda n: (0, 0)),
            pl.BlockSpec((1024, tile), lambda n: (0, n)),
        ],
        out_specs=pl.BlockSpec((PAIRS, tile), lambda n: (0, n)),
        out_shape=jax.ShapeDtypeStruct((PAIRS, K), BF),
        scratch_shapes=[pltpu.VMEM((PAIRS, 1024), BF)] * 3,
        compiler_params=pltpu.CompilerParams(vmem_limit_bytes=VMEM),
        cost_estimate=pl.CostEstimate(flops=5_000_000_000, bytes_accessed=15_000_000, transcendentals=0),
    )(recv, passage_of.reshape(1, PAIRS), order, projection)


def first_sum_kernel(part, out):
    total = part[0].astype(F32)
    for i in range(1, NX):
        total = total + part[i].astype(F32)
    total = total.astype(BF)
    stacked = jnp.concatenate([total[:, KV * q : KV * q + KV] for q in range(4)], axis=0)
    r, c = iota((4 * ROWS, 4 * ROWS), 0), iota((4 * ROWS, 4 * ROWS), 1)
    hot = jnp.zeros((4 * ROWS, 4 * ROWS), F32)
    z = r // 48
    quarter = (r - z * 48) // MINE
    item = r - z * 48 - quarter * MINE
    hot = jnp.where(c == quarter * ROWS + z * MINE + item, 1.0, 0.0).astype(BF)
    out[...] = dot(hot, stacked).astype(BF).reshape(NZ, 48, KV)


def first_sum(part):
    return pl.pallas_call(
        first_sum_kernel,
        out_shape=jax.ShapeDtypeStruct((NZ, 48, KV), BF),
        compiler_params=pltpu.CompilerParams(vmem_limit_bytes=VMEM),
        cost_estimate=pl.CostEstimate(flops=300_000_000, bytes_accessed=4_000_000, transcendentals=0),
    )(part)


def last_sum_kernel(part, out):
    total = part[0].astype(F32)
    for i in range(1, NZ):
        total = total + part[i].astype(F32)
    for q in range(4):
        out[:, KV * q : KV * q + KV] = total[MINE * q : MINE * q + MINE, :]


def last_sum(part):
    return pl.pallas_call(
        last_sum_kernel,
        out_shape=jax.ShapeDtypeStruct((MINE, K), F32),
        compiler_params=pltpu.CompilerParams(vmem_limit_bytes=VMEM),
        cost_estimate=pl.CostEstimate(flops=1_000_000, bytes_accessed=1_000_000, transcendentals=0),
    )(part)


def local(q_fact, p_fact, q_cot, p_cot, passage_of, projection):
    sent = grads(q_fact, p_fact, q_cot, p_cot)
    recv = lax.all_to_all(sent, ("px", "pz"), 0, 0, tiled=True)
    part = product(recv, passage_of, projection).reshape(NX, ROWS, K)
    part = lax.all_to_all(part, "px", 0, 0, tiled=True)
    part = first_sum(part)
    part = lax.all_to_all(part, "pz", 0, 0, tiled=True)
    return last_sum(part)


def solution(mesh):
    cut = Mesh(mesh.devices.reshape(mesh.shape["pairs"], NX, NZ), ("pairs", "px", "pz"))
    rows = P(("pairs", "px", "pz"), None)
    return jax.shard_map(
        local,
        mesh=cut,
        in_specs=(rows, rows, rows, rows, P("pairs"), P(("px", "pz"), None)),
        out_specs=rows,
        check_vma=False,
    )
```

time: 389 us -> 143 us (0.37)
  blocking collectives: 209 us -> 68.2 us
  local copies, waits for them, and re-layouts: 46.8 us -> 1.77 us
  waiting for transfers between devices: 60 us -> 34.7 us
  starting transfers between devices: 36.4 us -> 11.6 us
  Pallas kernels: 0 us -> 22.7 us
  matrix products: 17.1 us -> 0 us
  between operations: 14.4 us -> 0.02 us
    all_gather x1 -> x0, blocking collectives: 105 us -> none  [local(): lax.all_gather(q_fact, 'proj', axis=0, tiled=True)]
    unnamed x1 -> x0, blocking collectives: 104 us -> none
    all_to_all x0 -> x2, blocking collectives: none -> 68.2 us  [the longest x1 40.7 us: local(): part = lax.all_to_all(part, 'px', 0, 0, tiled=True)]
    unnamed x9 -> x0, waiting for transfers between devices: 26.9 us -> none
    pallas_call x0 -> x4, Pallas kernels: none -> 22.7 us  [the longest x1 12.5 us: product(): pl.pallas_call(product_kernel, grid=(K // tile,), in_specs=[pl.BlockSpec(...]
    unnamed x27 -> x4, local copies, waits for them, and re-layouts: 23.3 us -> 1.2 us
    dot_general x3 -> x0, matrix products: 17.1 us -> none  [the longest x1 8.89 us: local(): jnp.dot(pair_grad, projection, preferred_element_type=jnp.float32)]
    unnamed x8 -> x0, starting transfers between devices: 16.8 us -> none
  transfers between devices with their start and end apart: 11 -> 1, of which waited for: 4 -> 1; matrix products, arithmetic and copies ran while one was open for 6% -> 2% of each run, Pallas kernels for 0% -> 0%
where the time goes in v1:
time: 143 us; the launch traced here: 141 us
  blocking collectives  68.2 us (48%)
  waiting for transfers between devices  34.7 us (24%)
  Pallas kernels  22.7 us (16%)
  starting transfers between devices  11.6 us (8%)
  local copies, waits for them, and re-layouts  1.77 us (1%)
  other arithmetic  1.77 us (1%)
    all_to_all x1, blocking collectives, local(): part = lax.all_to_all(part, 'px', 0, 0, tiled=True)  40.7 us
    all_to_all x1, waiting for transfers between devices, local(): recv = lax.all_to_all(sent, ('px', 'pz'), 0, 0, tiled=True)  34.7 us
    all_to_all x1, blocking collectives, local(): part = lax.all_to_all(part, 'pz', 0, 0, tiled=True)  27.5 us
    pallas_call x1, Pallas kernels, product(): pl.pallas_call(product_kernel, grid=(K // tile,), in_specs=[pl.BlockSpec(...  12.5 us
    all_to_all x1, starting transfers between devices, local(): recv = lax.all_to_all(sent, ('px', 'pz'), 0, 0, tiled=True)  11.6 us
    pallas_call x1, Pallas kernels, grads(): pl.pallas_call(grads_kernel, grid=(2,), in_specs=[pl.BlockSpec((2 * R, MI...  4.53 us
    pallas_call x1, Pallas kernels, first_sum(): pl.pallas_call(first_sum_kernel, out_shape=jax.ShapeDtypeStruct((NZ, 48,...  3.75 us
  transfers between devices with their start and end apart: 1, of which 1 were waited for; matrix products, arithmetic and copies ran while one was open for 2% of the time, Pallas kernels for 0%

profile of v1, /device:TPU:14, one launch (start us, length us, event | category | flops | bytes accessed | tf_op | source)
XLA Modules:
  0.0 140.8 jit_solution(3276930351495106960)
XLA Ops:
  0.0 0.0 copy-start.1
  0.0 4.5 %shard_map.64 = bf16[32,192,128]{2,1,0:T(8,128)(2,1)} custom-call(bf16[32,384]{1,0:T(8,128)(2,1)} %bitcast.5, bf16[32,576]{1,0:T(8,128)(2,1)} %bitcast.4, bf16[384,2048]{1,0:T(8,128)(2,1)} %qc.1, bf16[576,2048]{1,0:T(8,128)(2,1)} %pc.1), custom_call_target="tpu_custom_call" | custom-call | flops 800000000 | bytes 5500000 | tf_op jit(solution)/shard_map/pallas_call | solution.py:54
  4.5 11.6 %all-to-all-start = ((bf16[32,192,128]{2,1,0:T(8,128)(2,1)}), bf16[32,192,128]{2,1,0:T(8,128)(2,1)S(1)}, u32[]{:S(2)}, u32[]{:S(2)}) async-start(bf16[32,192,128]{2,1,0:T(8,128)(2,1)} %shard_map.64), calls=%async_computation | async-start | bytes 3145728 | tf_op jit(solution)/shard_map/all_to_all | solution.py:161
  16.1 0.0 copy-done.1
  16.2 0.6 reshape.6.passage
  16.7 1.8 %select_convert_fusion.order = bf16[1024,1024]{1,0:T(8,128)(2,1)} fusion(s32[1024]{0:T(1024)S(1)} %fusion.2), kind=kLoop, calls=%fused_computation | loop fusion | flops 3145728 | bytes 2101248 | tf_op jit(solution)/shard_map/convert_element_type | solution.py:99
  18.5 34.7 %all-to-all-done.recv = bf16[32,192,128]{2,1,0:T(8,128)(2,1)S(1)} async-done(((bf16[32,192,128]{2,1,0:T(8,128)(2,1)}), bf16[32,192,128]{2,1,0:T(8,128)(2,1)S(1)}, u32[]{:S(2)}, u32[]{:S(2)}) %all-to-all-start) | async-done | bytes 1572896 | tf_op jit(solution)/shard_map/all_to_all | solution.py:161
  53.2 0.0 copy-start
  53.2 1.2 copy-done
  54.4 12.5 %shard_map.65 = bf16[384,4096]{1,0:T(8,128)(2,1)} custom-call(bf16[32,192,128]{2,1,0:T(8,128)(2,1)} %copy-done, s32[1,384]{1,0:T(1,128)} %reshape.6.passage, bf16[1024,1024]{1,0:T(8,128)(2,1)} %select_convert_fusion.order, bf16[1024,4096]{1,0:T(8,128)(2,1)} %proj.1), custom_call_target="tpu_custom_call" | custom-call | flops 5000000000 | bytes 15000000 | tf_op jit(solution)/shard_map/pallas_call | solution.py:101
  66.9 40.7 %all_to_all.15.part = bf16[4,96,4096]{2,1,0:T(8,128)(2,1)} all-to-all(bf16[4,96,4096]{2,1,0:T(8,128)(2,1)} %bitcast.3), channel_id=1, replica_groups=mesh['pairs'=8,'px'=4,'pz'=8] {'px'}, dimensions={0} | all-to-all | bytes 6291456 | tf_op jit(solution)/shard_map/all_to_all | solution.py:163
  107.6 3.8 %shard_map.66 = bf16[8,48,1024]{2,1,0:T(8,128)(2,1)} custom-call(bf16[4,96,4096]{2,1,0:T(8,128)(2,1)} %all_to_all.15.part), custom_call_target="tpu_custom_call" | custom-call | flops 300000000 | bytes 4000000 | tf_op jit(solution)/shard_map/pallas_call | solution.py:134
  111.4 27.5 %all_to_all.16.part = bf16[8,48,1024]{2,1,0:T(8,128)(2,1)} all-to-all(bf16[8,48,1024]{2,1,0:T(8,128)(2,1)} %shard_map.66), channel_id=1, replica_groups=mesh['pairs'=8,'px'=4,'pz'=8] {'pz'}, dimensions={0} | all-to-all | bytes 1572864 | tf_op jit(solution)/shard_map/all_to_all | solution.py:165
  138.8 1.9 %shard_map.67 = f32[12,4096]{1,0:T(8,128)} custom-call(bf16[8,48,1024]{2,1,0:T(8,128)(2,1)} %all_to_all.16.part), custom_call_target="tpu_custom_call" | custom-call | flops 1000000 | bytes 1000000 | tf_op jit(solution)/shard_map/pallas_call | solution.py:151
  (1 shorter events, 0.0 us)
Async XLA Ops:
  0.0 16.1 %copy-start.1 = (s32[384]{0:T(512)S(1)}, s32[384]{0:T(512)}, u32[]{:S(2)}) copy-start(s32[384]{0:T(512)} %param.10) | copy-start | bytes 4612
  4.5 48.7 %all-to-all-start = ((bf16[32,192,128]{2,1,0:T(8,128)(2,1)}), bf16[32,192,128]{2,1,0:T(8,128)(2,1)S(1)}, u32[]{:S(2)}, u32[]{:S(2)}) async-start(bf16[32,192,128]{2,1,0:T(8,128)(2,1)} %shard_map.64), calls=%async_computation | async-start | bytes 3145728 | tf_op jit(solution)/shard_map/all_to_all | solution.py:161
  53.2 1.2 copy-start

commit v2 on v0

v2 whole, which is shorter than its diff:
```python
import jax
import jax.numpy as jnp
from jax import lax
from jax.experimental import pallas as pl
from jax.experimental.pallas import tpu as pltpu
from jax.sharding import Mesh, PartitionSpec as P

KV = 1024
R = 16
QLEN = 32
PLEN = 48
K = 4096
NX, NZ = 4, 8
N = NX * NZ
MINE = 12
PAIRS = N * MINE
G = 1024
ROWS = MINE * 8
VMEM = 40 * 1024 * 1024
BF = jnp.bfloat16
F32 = jnp.float32
ANY = pl.BlockSpec(memory_space=pl.ANY)
WHOLE = pl.BlockSpec(memory_space=pltpu.VMEM)


def iota(shape, dim):
    return lax.broadcasted_iota(jnp.int32, shape, dim)


def dot(a, b):
    return lax.dot_general(a, b, (((1,), (0,)), ((), ())), preferred_element_type=F32)


def ones_where(mask):
    return jnp.where(mask, 1.0, 0.0).astype(BF)


def call(kernel, out_shape, flops, moved, **kwargs):
    return pl.pallas_call(
        kernel,
        out_shape=out_shape,
        compiler_params=pltpu.CompilerParams(vmem_limit_bytes=VMEM),
        cost_estimate=pl.CostEstimate(flops=flops, bytes_accessed=moved, transcendentals=0),
        **kwargs,
    )


def array(*shape, dtype=BF):
    return jax.ShapeDtypeStruct(shape, dtype)


def grads(fact, cot, length):
    tokens = MINE * length

    def kernel(fact, cot, out):
        layer = pl.program_id(0)
        row = iota((2 * ROWS, 2 * R), 0)
        rank = jnp.where(row >= ROWS, 8, 0) + (row & 7) + layer * R
        pick = ones_where(iota((2 * ROWS, 2 * R), 1) == rank)
        row = iota((2 * ROWS, tokens), 0)
        item = jnp.where(row >= ROWS, row - ROWS, row) >> 3
        token = iota((2 * ROWS, tokens), 1) - item * length
        spread = jnp.where((token >= 0) & (token < length), dot(pick, fact[...]), 0.0)
        grad = dot(spread.astype(BF), cot[...])
        lane = iota((ROWS, 128), 1)
        for j in range(8):
            top = grad[:ROWS, 128 * j : 128 * j + 128]
            low = grad[ROWS:, 128 * j : 128 * j + 128]
            out[2 * j] = jnp.where(lane < 64, top, pltpu.roll(low, 64, 1)).astype(BF)
            out[2 * j + 1] = jnp.where(lane < 64, pltpu.roll(top, 64, 1), low).astype(BF)

    return call(
        kernel,
        array(N, ROWS, 128),
        400_000_000,
        3_000_000,
        grid=(2,),
        in_specs=[
            pl.BlockSpec((2 * R, tokens), lambda l: (0, 0)),
            pl.BlockSpec((tokens, KV), lambda l: (0, l)),
        ],
        out_specs=pl.BlockSpec((N // 2, ROWS, 128), lambda l: (l, 0, 0)),
    )(fact.T, cot)


def permuted(projection):
    def kernel(proj, out, order):
        @pl.when(pl.program_id(0) == 0)
        def _():
            u, v = iota((G, G), 0), iota((G, G), 1)
            order[...] = ones_where(v == (u & 63) * 16 + ((u >> 6) & 1) * 8 + (u >> 7))

        out[...] = dot(order[...], proj[...]).astype(BF)

    tile = pl.BlockSpec((G, 512), lambda n: (0, n))
    return call(
        kernel,
        array(G, K),
        2 * G * G * K,
        16_000_000,
        grid=(K // 512,),
        in_specs=[tile],
        out_specs=tile,
        scratch_shapes=[pltpu.VMEM((G, G), BF)],
    )(projection)


def widen(recv, out, rotated):
    r, c = iota((256, 256), 0), iota((256, 256), 1)
    swap = ones_where(c == (r & 31) * 8 + (r >> 5))
    x = lax.axis_index("px")
    for g in range(PAIRS // 32):
        mixed = dot(swap, recv[256 * g : 256 * g + 256, :]).astype(BF)
        if rotated:
            at = pl.multiple_of(((g // 3 - x) & 3) * ROWS + (g % 3) * 32, 32)
        else:
            at = 32 * g
        for b in range(8):
            out[pl.ds(at, 32), 128 * b : 128 * b + 128] = mixed[32 * b : 32 * b + 32, :]


def selected(recv, passage_of):
    def kernel(recv, passage, out, wide):
        widen(recv, wide, False)
        hot = ones_where(iota((PAIRS, PAIRS), 0) == passage[...])
        picked = lax.dot_general(hot, wide[...], (((0,), (0,)), ((), ())), preferred_element_type=F32)
        picked = picked.astype(BF)
        x = lax.axis_index("px")
        for i in range(NX):
            at = pl.multiple_of(((i - x) & 3) * ROWS, 32)
            out[pl.ds(at, ROWS), :] = picked[ROWS * i : ROWS * i + ROWS, :]

    return call(
        kernel,
        array(PAIRS, G),
        700_000_000,
        1_600_000,
        scratch_shapes=[pltpu.VMEM((PAIRS, G), BF)],
    )(recv.reshape(N * ROWS, 128), passage_of.reshape(1, PAIRS))


def quarters(pair, proj, outs):
    for half in range(2):
        part = dot(pair[...], proj[:, KV * half : KV * half + KV]).astype(BF)
        for d in range(NX):
            outs[4 * half + d][...] = part[ROWS * d : ROWS * d + ROWS, :]


def product_first(recv, picked, proj):
    def kernel(recv, picked, proj, pair, *rest):
        outs, (wide, held, sem) = rest[:8], rest[8:]
        copy = pltpu.make_async_copy(proj.at[:, : K // 2], held, sem)
        copy.start()
        widen(recv, wide, True)
        pair[...] = (wide[...].astype(F32) + picked[...].astype(F32)).astype(BF)
        copy.wait()
        quarters(pair, held, outs)

    return call(
        kernel,
        [array(PAIRS, G)] + [array(ROWS, KV)] * 8,
        2_500_000_000,
        8_000_000,
        in_specs=[WHOLE, WHOLE, ANY],
        scratch_shapes=[pltpu.VMEM((PAIRS, G), BF), pltpu.VMEM((G, K // 2), BF), pltpu.SemaphoreType.DMA],
    )(recv.reshape(N * ROWS, 128), picked, proj)


def product_second(pair, proj):
    def kernel(pair, proj, *outs):
        quarters(pair, proj, outs)

    return call(
        kernel,
        [array(ROWS, KV)] * 8,
        1_700_000_000,
        7_000_000,
        grid=(1,),
        in_specs=[pl.BlockSpec((PAIRS, G), lambda i: (0, 0)), pl.BlockSpec((G, K // 2), lambda i: (0, 1))],
        out_specs=[pl.BlockSpec((ROWS, KV), lambda i: (0, 0))] * 8,
    )(pair, proj)


def add(a, b):
    return (a.astype(F32) + b.astype(F32)).astype(BF)


def across_x(blocks):
    l0, l1, l2, l3, r0, r1, r2, r3 = blocks
    up = [(i, (i + 1) % NX) for i in range(NX)]
    down = [(i, (i - 1) % NX) for i in range(NX)]
    far_l = lax.ppermute(l2, "px", up)
    far_r = lax.ppermute(r2, "px", down)
    got_r = lax.ppermute(r1, "px", up)
    got_l = lax.ppermute(l3, "px", down)
    sum_l = lax.ppermute(add(l1, far_l), "px", up)
    sum_r = lax.ppermute(add(r3, far_r), "px", down)
    return (l0, got_l, sum_l, r0, got_r, sum_r)


def spread_z(terms):
    def kernel(l0, l1, l2, r0, r1, r2, out):
        left = (l0[...].astype(F32) + l1[...].astype(F32) + l2[...].astype(F32)).astype(BF)
        right = (r0[...].astype(F32) + r1[...].astype(F32) + r2[...].astype(F32)).astype(BF)
        stacked = jnp.concatenate([left[:, :512], left[:, 512:], right[:, :512], right[:, 512:]], axis=0)
        r, c = iota((4 * ROWS, 4 * ROWS), 0), iota((4 * ROWS, 4 * ROWS), 1)
        z = r // 48
        quarter = (r - z * 48) // MINE
        item = r - z * 48 - quarter * MINE
        hot = ones_where(c == quarter * ROWS + z * MINE + item)
        out[...] = dot(hot, stacked).astype(BF).reshape(NZ, 48, 512)

    part = call(kernel, array(NZ, 48, 512), 150_000_000, 2_000_000)(*terms)
    return lax.all_to_all(part, "pz", 0, 0, tiled=True)


def last_sum(first, second):
    def kernel(first, second, out):
        for half, part in enumerate((first, second)):
            total = part[0].astype(F32)
            for i in range(1, NZ):
                total = total + part[i].astype(F32)
            for q in range(4):
                at = 2048 * half + 512 * q
                out[:, at : at + 512] = total[MINE * q : MINE * q + MINE, :]

    return call(kernel, array(MINE, K, dtype=F32), 1_000_000, 1_000_000)(first, second)


def local(q_fact, p_fact, q_cot, p_cot, passage_of, projection):
    axes = ("px", "pz")
    p_recv = lax.all_to_all(grads(p_fact, p_cot, PLEN), axes, 0, 0, tiled=True)
    q_recv = lax.all_to_all(grads(q_fact, q_cot, QLEN), axes, 0, 0, tiled=True)
    proj = permuted(projection)
    picked = selected(p_recv, passage_of)
    pair, *first = product_first(q_recv, picked, proj)
    first = spread_z(across_x(first))
    second = spread_z(across_x(product_second(pair, proj)))
    return last_sum(first, second)


def solution(mesh):
    cut = Mesh(mesh.devices.reshape(mesh.shape["pairs"], NX, NZ), ("pairs", "px", "pz"))
    rows = P(("pairs", "px", "pz"), None)
    return jax.shard_map(
        local,
        mesh=cut,
        in_specs=(rows, rows, rows, rows, P("pairs"), P(("px", "pz"), None)),
        out_specs=rows,
        check_vma=False,
    )
```

time: 389 us -> 132 us (0.34); the launches traced: 383 us -> 131 us
  blocking collectives: 209 us -> 18.1 us
  local copies, waits for them, and re-layouts: 46.8 us -> 11.2 us
  Pallas kernels: 0 us -> 25.8 us
  waiting for transfers between devices: 60 us -> 34.6 us
  matrix products: 17.1 us -> 0 us
  between operations: 14.4 us -> 0.19 us
  starting transfers between devices: 36.4 us -> 40.8 us
    all_gather x1 -> x0, blocking collectives: 105 us -> none  [local(): lax.all_gather(q_fact, 'proj', axis=0, tiled=True)]
    unnamed x1 -> x0, blocking collectives: 104 us -> none
    unnamed x9 -> x0, waiting for transfers between devices: 26.9 us -> none
    pallas_call x0 -> x9, Pallas kernels: none -> 25.8 us  [the longest x1 12.3 us: permuted(): call(kernel, array(G, K), 2 * G * G * K, 16000000, grid=(K // 512,), in_s...]
    ppermute x0 -> x12, starting transfers between devices: none -> 18.7 us  [the longest x2 6.47 us: across_x(): got_r = lax.ppermute(r1, 'px', up)]
    all_to_all x0 -> x1, blocking collectives: none -> 18.1 us  [spread_z(): return lax.all_to_all(part, 'pz', 0, 0, tiled=True)]
    dot_general x3 -> x0, matrix products: 17.1 us -> none  [the longest x1 8.89 us: local(): jnp.dot(pair_grad, projection, preferred_element_type=jnp.float32)]
    unnamed x8 -> x0, starting transfers between devices: 16.8 us -> none
  transfers between devices with their start and end apart: 11 -> 15, of which waited for: 4 -> 7; matrix products, arithmetic and copies ran while one was open for 6% -> 0% of each run, Pallas kernels for 0% -> 15%
where the time goes in v2:
time: 132 us; the launch traced here: 131 us
  starting transfers between devices  40.8 us (31%)
  waiting for transfers between devices  34.6 us (26%)
  Pallas kernels  25.8 us (20%)
  blocking collectives  18.1 us (14%)
  local copies, waits for them, and re-layouts  11.2 us (8%)
    all_to_all x1, blocking collectives, spread_z(): return lax.all_to_all(part, 'pz', 0, 0, tiled=True)  18.1 us
    all_to_all x1, waiting for transfers between devices, local(): p_recv = lax.all_to_all(grads(p_fact, p_cot, PLEN), axes, 0, 0, tiled=True)  16.9 us
    pallas_call x1, Pallas kernels, permuted(): call(kernel, array(G, K), 2 * G * G * K, 16000000, grid=(K // 512,), in_s...  12.3 us
    all_to_all x1, starting transfers between devices, local(): p_recv = lax.all_to_all(grads(p_fact, p_cot, PLEN), axes, 0, 0, tiled=True)  11.6 us
    unnamed x16, local copies, waits for them, and re-layouts  11.2 us
    all_to_all x1, starting transfers between devices, local(): q_recv = lax.all_to_all(grads(q_fact, q_cot, QLEN), axes, 0, 0, tiled=True)  6.96 us
    ppermute x2, starting transfers between devices, across_x(): got_r = lax.ppermute(r1, 'px', up)  6.47 us
    ppermute x2, starting transfers between devices, across_x(): sum_l = lax.ppermute(add(l1, far_l), 'px', up)  6.13 us
  transfers between devices with their start and end apart: 15, of which 7 were waited for; matrix products, arithmetic and copies ran while one was open for 0% of the time, Pallas kernels for 15%

profile of v2, /device:TPU:14, one launch (start us, length us, event | category | flops | bytes accessed | tf_op | source)
XLA Modules:
  0.0 130.9 jit_solution(8962989692738971647)
XLA Ops:
  0.0 0.0 copy-start.3
  0.0 1.7 %copy-done.3 = bf16[576,2048]{1,0:T(8,128)(2,1)S(1)} copy-done((bf16[576,2048]{1,0:T(8,128)(2,1)S(1)}, bf16[576,2048]{1,0:T(8,128)(2,1)}, u32[]{:S(2)}) %copy-start.3) | copy-done | bytes 2359320
  1.7 0.0 copy-start.5
  1.7 0.8 copy-done.5
  2.4 0.0 copy-start.7
  2.4 2.3 %shard_map.65 = bf16[32,96,128]{2,1,0:T(8,128)(2,1)} custom-call(bf16[32,576]{1,0:T(8,128)(2,1)S(1)} %bitcast.6, bf16[576,2048]{1,0:T(8,128)(2,1)S(1)} %copy-done.3), custom_call_target="tpu_custom_call" | custom-call | flops 400000000 | bytes 3000000 | tf_op jit(solution)/shard_map/pallas_call | solution.py:72
  4.7 11.6 %all-to-all-start.1 = ((bf16[32,96,128]{2,1,0:T(8,128)(2,1)}), bf16[32,96,128]{2,1,0:T(8,128)(2,1)S(1)}, u32[]{:S(2)}, u32[]{:S(2)}) async-start(bf16[32,96,128]{2,1,0:T(8,128)(2,1)} %shard_map.65), calls=%async_computation.1 | async-start | bytes 1572864 | tf_op jit(solution)/shard_map/all_to_all | solution.py:232
  16.3 0.0 copy-start.4
  16.3 1.4 %copy-done.4 = bf16[384,2048]{1,0:T(8,128)(2,1)S(1)} copy-done((bf16[384,2048]{1,0:T(8,128)(2,1)S(1)}, bf16[384,2048]{1,0:T(8,128)(2,1)}, u32[]{:S(2)}) %copy-start.4) | copy-done | bytes 1572888
  17.7 0.0 copy-start.6
  17.7 0.7 copy-done.6
  18.5 2.0 %shard_map.64 = bf16[32,96,128]{2,1,0:T(8,128)(2,1)} custom-call(bf16[32,384]{1,0:T(8,128)(2,1)S(1)} %bitcast.7, bf16[384,2048]{1,0:T(8,128)(2,1)S(1)} %copy-done.4), custom_call_target="tpu_custom_call" | custom-call | flops 400000000 | bytes 3000000 | tf_op jit(solution)/shard_map/pallas_call | solution.py:72
  20.5 16.9 %all-to-all-done.1 = bf16[32,96,128]{2,1,0:T(8,128)(2,1)S(1)} async-done(((bf16[32,96,128]{2,1,0:T(8,128)(2,1)}), bf16[32,96,128]{2,1,0:T(8,128)(2,1)S(1)}, u32[]{:S(2)}, u32[]{:S(2)}) %all-to-all-start.1) | async-done | bytes 786464 | tf_op jit(solution)/shard_map/all_to_all | solution.py:232
  37.5 7.0 %all-to-all-start = ((bf16[32,96,128]{2,1,0:T(8,128)(2,1)}), bf16[32,96,128]{2,1,0:T(8,128)(2,1)S(1)}, u32[]{:S(2)}, u32[]{:S(2)}) async-start(bf16[32,96,128]{2,1,0:T(8,128)(2,1)} %shard_map.64), calls=%async_computation | async-start | bytes 1572864 | tf_op jit(solution)/shard_map/all_to_all | solution.py:233
  44.4 0.0 copy-done.7
  44.4 12.3 %shard_map.67.proj = bf16[1024,4096]{1,0:T(8,128)(2,1)S(1)} custom-call(bf16[1024,4096]{1,0:T(8,128)(2,1)} %proj.1), custom_call_target="tpu_custom_call" | custom-call | flops 8589934592 | bytes 16000000 | tf_op jit(solution)/shard_map/pallas_call | solution.py:96
  56.8 0.0 copy-start
  56.8 3.3 %copy-done = bf16[1024,4096]{1,0:T(8,128)(2,1)} copy-done((bf16[1024,4096]{1,0:T(8,128)(2,1)}, bf16[1024,4096]{1,0:T(8,128)(2,1)S(1)}, u32[]{:S(2)}) %copy-start) | copy-done | bytes 8388632
  60.0 1.0 shard_map.66.picked
  61.0 4.0 %all-to-all-done = bf16[32,96,128]{2,1,0:T(8,128)(2,1)S(1)} async-done(((bf16[32,96,128]{2,1,0:T(8,128)(2,1)}), bf16[32,96,128]{2,1,0:T(8,128)(2,1)S(1)}, u32[]{:S(2)}, u32[]{:S(2)}) %all-to-all-start) | async-done | bytes 786464 | tf_op jit(solution)/shard_map/all_to_all | solution.py:233
  65.0 0.0 copy-start.1
  65.0 3.4 %copy-done.1 = bf16[1024,4096]{1,0:T(8,128)(2,1)S(1)} copy-done((bf16[1024,4096]{1,0:T(8,128)(2,1)S(1)}, bf16[1024,4096]{1,0:T(8,128)(2,1)}, u32[]{:S(2)}) %copy-start.1) | copy-done | bytes 8388632
  68.4 0.0 copy-start.2
  68.4 3.6 %shard_map.68 = (bf16[384,1024]{1,0:T(8,128)(2,1)S(1)}, bf16[96,1024]{1,0:T(8,128)(2,1)S(1)}, bf16[96,1024]{1,0:T(8,128)(2,1)S(1)}, bf16[96,1024]{1,0:T(8,128)(2...) custom-call(bf16[3072,128]{1,0:T(8,128)(2,1)S(1)} %bitcast.4, ...), custom_call_target="tpu_custom_call" | custom-call | flops 2500000000 | bytes 8000000 | tf_op jit(solution)/shard_map/pallas_call | solution.py:159
  72.0 2.5 %collective-permute-start.1 = (bf16[96,1024]{1,0:T(8,128)(2,1)S(1)}, bf16[96,1024]{1,0:T(8,128)(2,1)S(1)}, u32[]{:S(2)}, u32[]{:S(2)}) collective-permute-start(bf16[96,1024]{1,0:T(8,128)(2,1)S(1)} %get-tuple-element.25), channel_id=1, source_target_pairs={{0,8},{8,16},{16,24},{24,0},{1,9},{9,17},{17,25},{25,1},{2,10},{10... | collective-permute-start | bytes 589832 | tf_op jit(solution)/shard_map/ppermute | solution.py:192
  74.5 0.0 collective-permute-start
  74.5 3.2 %collective-permute-start.3 = (bf16[96,1024]{1,0:T(8,128)(2,1)S(1)}, bf16[96,1024]{1,0:T(8,128)(2,1)S(1)}, u32[]{:S(2)}, u32[]{:S(2)}) collective-permute-start(bf16[96,1024]{1,0:T(8,128)(2,1)S(1)} %get-tuple-element.27), channel_id=1, source_target_pairs={{0,8},{8,16},{16,24},{24,0},{1,9},{9,17},{17,25},{25,1},{2,10},{10... | collective-permute-start | bytes 589832 | tf_op jit(solution)/shard_map/ppermute | solution.py:194
  77.8 0.0 collective-permute-start.4
  77.8 2.1 %collective-permute-done.1 = bf16[96,1024]{1,0:T(8,128)(2,1)S(1)} collective-permute-done((bf16[96,1024]{1,0:T(8,128)(2,1)S(1)}, bf16[96,1024]{1,0:T(8,128)(2,1)S(1)}, u32[]{:S(2)}, u32[]{:S(2)}) %collective-permute-start.1) | collective-permute-done | bytes 196640 | tf_op jit(solution)/shard_map/ppermute | solution.py:192
  79.9 2.8 %collective-permute-start.2 = (bf16[96,1024]{1,0:T(8,128)(2,1)S(1)}, bf16[96,1024]{1,0:T(8,128)(2,1)S(1)}, u32[]{:S(2)}, u32[]{:S(2)}) collective-permute-start(bf16[96,1024]{1,0:T(8,128)(2,1)S(1)} %add_convert_fusion.3), channel_id=1, source_target_pairs={{0,8},{8,16},{16,24},{24,0},{1,9},{9,17},{17,25},{25,1},{2,10},{10... | collective-permute-start | bytes 589832 | tf_op jit(solution)/shard_map/ppermute | solution.py:196
  82.8 3.9 %collective-permute-done.4 = bf16[96,1024]{1,0:T(8,128)(2,1)S(1)} collective-permute-done((bf16[96,1024]{1,0:T(8,128)(2,1)S(1)}, bf16[96,1024]{1,0:T(8,128)(2,1)S(1)}, u32[]{:S(2)}, u32[]{:S(2)}) %collective-permute-start.4) | collective-permute-done | bytes 196640 | tf_op jit(solution)/shard_map/ppermute | solution.py:193
  86.7 0.1 collective-permute-start.5
  86.8 0.0 copy-done.2
  86.8 1.8 %shard_map.70 = (bf16[96,1024]{1,0:T(8,128)(2,1)S(1)}, bf16[96,1024]{1,0:T(8,128)(2,1)S(1)}, bf16[96,1024]{1,0:T(8,128)(2,1)S(1)}, bf16[96,1024]{1,0:T(8,128)(2,...) custom-call(bf16[384,1024]{1,0:T(8,128)(2,1)S(1)} %get-tuple-element, ...), custom_call_target="tpu_custom_call" | custom-call | flops 1700000000 | bytes 7000000 | tf_op jit(solution)/shard_map/pallas_call | solution.py:173
  88.6 3.5 %collective-permute-start.7 = (bf16[96,1024]{1,0:T(8,128)(2,1)S(1)}, bf16[96,1024]{1,0:T(8,128)(2,1)S(1)}, u32[]{:S(2)}, u32[]{:S(2)}) collective-permute-start(bf16[96,1024]{1,0:T(8,128)(2,1)S(1)} %get-tuple-element.34), channel_id=1, source_target_pairs={{0,8},{8,16},{16,24},{24,0},{1,9},{9,17},{17,25},{25,1},{2,10},{10... | collective-permute-start | bytes 589832 | tf_op jit(solution)/shard_map/ppermute | solution.py:192
  92.1 0.0 collective-permute-done.l1
  92.1 0.0 collective-permute-start.6
  92.1 0.0 collective-permute-done.3.r1
  92.1 3.2 %collective-permute-start.9 = (bf16[96,1024]{1,0:T(8,128)(2,1)S(1)}, bf16[96,1024]{1,0:T(8,128)(2,1)S(1)}, u32[]{:S(2)}, u32[]{:S(2)}) collective-permute-start(bf16[96,1024]{1,0:T(8,128)(2,1)S(1)} %get-tuple-element.36), channel_id=1, source_target_pairs={{0,8},{8,16},{16,24},{24,0},{1,9},{9,17},{17,25},{25,1},{2,10},{10... | collective-permute-start | bytes 589832 | tf_op jit(solution)/shard_map/ppermute | solution.py:194
  95.4 0.0 collective-permute-done.2.l2
  95.4 0.0 collective-permute-start.10
  95.4 0.0 collective-permute-done.5.r2
  95.4 1.4 %shard_map.69 = bf16[8,48,512]{2,1,0:T(8,128)(2,1)} custom-call(bf16[96,1024]{1,0:T(8,128)(2,1)S(1)} %get-tuple-element.22.l0, bf16[96,1024]{1,0:T(8,128)(2,1)S(1)} %collective-permute-done.l1, bf16[96,1024]{1,0:T(8,128)(2,1)S(1)} %collective-permute-done.2.l2, bf16[96,1024]{1,0:T(8,128)(2,1)S(1)} %get-tuple-element.26.r0, ...), custom_call_target="tpu_custom_call" | custom-call | flops 150000000 | bytes 2000000 | tf_op jit(solution)/shard_map/pallas_call | solution.py:213
  96.8 3.5 %all-to-all-start.2 = ((bf16[8,48,512]{2,1,0:T(8,128)(2,1)}), bf16[8,48,512]{2,1,0:T(8,128)(2,1)S(1)}, u32[]{:S(2)}, u32[]{:S(2)}) async-start(bf16[8,48,512]{2,1,0:T(8,128)(2,1)} %shard_map.69), calls=%async_computation.2 | async-start | bytes 786432 | tf_op jit(solution)/shard_map/all_to_all | solution.py:214
  100.2 0.0 collective-permute-done.7
  100.2 0.1 add_convert_fusion.1
  100.3 3.3 %collective-permute-start.8 = (bf16[96,1024]{1,0:T(8,128)(2,1)S(1)}, bf16[96,1024]{1,0:T(8,128)(2,1)S(1)}, u32[]{:S(2)}, u32[]{:S(2)}) collective-permute-start(bf16[96,1024]{1,0:T(8,128)(2,1)S(1)} %add_convert_fusion.1), channel_id=1, source_target_pairs={{0,8},{8,16},{16,24},{24,0},{1,9},{9,17},{17,25},{25,1},{2,10},{10... | collective-permute-start | bytes 589832 | tf_op jit(solution)/shard_map/ppermute | solution.py:196
  103.6 0.0 collective-permute-done.10
  103.6 0.1 collective-permute-start.11
  103.7 0.0 collective-permute-done.6.l1
  103.7 0.0 collective-permute-done.9.r1
  103.8 3.0 %collective-permute-done.8.l2 = bf16[96,1024]{1,0:T(8,128)(2,1)S(1)} collective-permute-done((bf16[96,1024]{1,0:T(8,128)(2,1)S(1)}, bf16[96,1024]{1,0:T(8,128)(2,1)S(1)}, u32[]{:S(2)}, u32[]{:S(2)}) %collective-permute-start.8) | collective-permute-done | bytes 196640 | tf_op jit(solution)/shard_map/ppermute | solution.py:196
  106.8 3.8 %collective-permute-done.11.r2 = bf16[96,1024]{1,0:T(8,128)(2,1)S(1)} collective-permute-done((bf16[96,1024]{1,0:T(8,128)(2,1)S(1)}, bf16[96,1024]{1,0:T(8,128)(2,1)S(1)}, u32[]{:S(2)}, u32[]{:S(2)}) %collective-permute-start.11) | collective-permute-done | bytes 196640 | tf_op jit(solution)/shard_map/ppermute | solution.py:197
  110.6 0.6 shard_map.71
  111.2 0.8 all-to-all-done.2.first
  112.0 18.1 %all_to_all.20.second = bf16[8,48,512]{2,1,0:T(8,128)(2,1)S(1)} all-to-all(bf16[8,48,512]{2,1,0:T(8,128)(2,1)S(1)} %shard_map.71), channel_id=1, replica_groups=mesh['pairs'=8,'px'=4,'pz'=8] {'pz'}, dimensions={0} | all-to-all | bytes 786432 | tf_op jit(solution)/shard_map/all_to_all | solution.py:214
  130.1 0.8 shard_map.72
  (4 shorter events, 0.1 us)
Async XLA Ops:
  0.0 1.7 %copy-start.3 = (bf16[576,2048]{1,0:T(8,128)(2,1)S(1)}, bf16[576,2048]{1,0:T(8,128)(2,1)}, u32[]{:S(2)}) copy-start(bf16[576,2048]{1,0:T(8,128)(2,1)} %cot.3) | copy-start | bytes 7077892
  1.7 0.8 copy-start.5
  2.4 42.0 %copy-start.7 = (s32[384]{0:T(512)S(1)}, s32[384]{0:T(512)}, u32[]{:S(2)}) copy-start(s32[384]{0:T(512)} %param.10) | copy-start | bytes 4612
  4.7 32.7 %all-to-all-start.1 = ((bf16[32,96,128]{2,1,0:T(8,128)(2,1)}), bf16[32,96,128]{2,1,0:T(8,128)(2,1)S(1)}, u32[]{:S(2)}, u32[]{:S(2)}) async-start(bf16[32,96,128]{2,1,0:T(8,128)(2,1)} %shard_map.65), calls=%async_computation.1 | async-start | bytes 1572864 | tf_op jit(solution)/shard_map/all_to_all | solution.py:232
  16.3 1.4 %copy-start.4 = (bf16[384,2048]{1,0:T(8,128)(2,1)S(1)}, bf16[384,2048]{1,0:T(8,128)(2,1)}, u32[]{:S(2)}) copy-start(bf16[384,2048]{1,0:T(8,128)(2,1)} %cot.2) | copy-start | bytes 4718596
  17.7 0.7 copy-start.6
  37.5 27.6 %all-to-all-start = ((bf16[32,96,128]{2,1,0:T(8,128)(2,1)}), bf16[32,96,128]{2,1,0:T(8,128)(2,1)S(1)}, u32[]{:S(2)}, u32[]{:S(2)}) async-start(bf16[32,96,128]{2,1,0:T(8,128)(2,1)} %shard_map.64), calls=%async_computation | async-start | bytes 1572864 | tf_op jit(solution)/shard_map/all_to_all | solution.py:233
  56.8 3.3 %copy-start = (bf16[1024,4096]{1,0:T(8,128)(2,1)}, bf16[1024,4096]{1,0:T(8,128)(2,1)S(1)}, u32[]{:S(2)}) copy-start(bf16[1024,4096]{1,0:T(8,128)(2,1)S(1)} %shard_map.67.proj) | copy-start | bytes 25165828
  65.0 3.4 %copy-start.1 = (bf16[1024,4096]{1,0:T(8,128)(2,1)S(1)}, bf16[1024,4096]{1,0:T(8,128)(2,1)}, u32[]{:S(2)}) copy-start(bf16[1024,4096]{1,0:T(8,128)(2,1)} %copy-done) | copy-start | bytes 25165828
  68.4 18.4 %copy-start.2 = (bf16[1024,4096]{1,0:T(8,128)(2,1)S(1)}, bf16[1024,4096]{1,0:T(8,128)(2,1)}, u32[]{:S(2)}) copy-start(bf16[1024,4096]{1,0:T(8,128)(2,1)} %copy-done) | copy-start | bytes 25165828
  72.0 7.8 %collective-permute-start.1 = (bf16[96,1024]{1,0:T(8,128)(2,1)S(1)}, bf16[96,1024]{1,0:T(8,128)(2,1)S(1)}, u32[]{:S(2)}, u32[]{:S(2)}) collective-permute-start(bf16[96,1024]{1,0:T(8,128)(2,1)S(1)} %get-tuple-element.25), channel_id=1, source_target_pairs={{0,8},{8,16},{16,24},{24,0},{1,9},{9,17},{17,25},{25,1},{2,10},{10... | collective-permute-start | bytes 589832 | tf_op jit(solution)/shard_map/ppermute | solution.py:192
  74.5 17.6 %collective-permute-start = (bf16[96,1024]{1,0:T(8,128)(2,1)S(1)}, bf16[96,1024]{1,0:T(8,128)(2,1)S(1)}, u32[]{:S(2)}, u32[]{:S(2)}) collective-permute-start(bf16[96,1024]{1,0:T(8,128)(2,1)S(1)} %get-tuple-element.23), channel_id=1, source_target_pairs={{0,24},{8,0},{16,8},{24,16},{1,25},{9,1},{17,9},{25,17},{2,26},{10... | collective-permute-start | bytes 589832 | tf_op jit(solution)/shard_map/ppermute | solution.py:195
  74.5 17.6 %collective-permute-start.3 = (bf16[96,1024]{1,0:T(8,128)(2,1)S(1)}, bf16[96,1024]{1,0:T(8,128)(2,1)S(1)}, u32[]{:S(2)}, u32[]{:S(2)}) collective-permute-start(bf16[96,1024]{1,0:T(8,128)(2,1)S(1)} %get-tuple-element.27), channel_id=1, source_target_pairs={{0,8},{8,16},{16,24},{24,0},{1,9},{9,17},{17,25},{25,1},{2,10},{10... | collective-permute-start | bytes 589832 | tf_op jit(solution)/shard_map/ppermute | solution.py:194
  77.8 8.9 %collective-permute-start.4 = (bf16[96,1024]{1,0:T(8,128)(2,1)S(1)}, bf16[96,1024]{1,0:T(8,128)(2,1)S(1)}, u32[]{:S(2)}, u32[]{:S(2)}) collective-permute-start(bf16[96,1024]{1,0:T(8,128)(2,1)S(1)} %get-tuple-element.29), channel_id=1, source_target_pairs={{0,24},{8,0},{16,8},{24,16},{1,25},{9,1},{17,9},{25,17},{2,26},{10... | collective-permute-start | bytes 589832 | tf_op jit(solution)/shard_map/ppermute | solution.py:193
  79.9 15.4 %collective-permute-start.2 = (bf16[96,1024]{1,0:T(8,128)(2,1)S(1)}, bf16[96,1024]{1,0:T(8,128)(2,1)S(1)}, u32[]{:S(2)}, u32[]{:S(2)}) collective-permute-start(bf16[96,1024]{1,0:T(8,128)(2,1)S(1)} %add_convert_fusion.3), channel_id=1, source_target_pairs={{0,8},{8,16},{16,24},{24,0},{1,9},{9,17},{17,25},{25,1},{2,10},{10... | collective-permute-start | bytes 589832 | tf_op jit(solution)/shard_map/ppermute | solution.py:196
  86.7 8.6 %collective-permute-start.5 = (bf16[96,1024]{1,0:T(8,128)(2,1)S(1)}, bf16[96,1024]{1,0:T(8,128)(2,1)S(1)}, u32[]{:S(2)}, u32[]{:S(2)}) collective-permute-start(bf16[96,1024]{1,0:T(8,128)(2,1)S(1)} %add_convert_fusion.2), channel_id=1, source_target_pairs={{0,24},{8,0},{16,8},{24,16},{1,25},{9,1},{17,9},{25,17},{2,26},{10... | collective-permute-start | bytes 589832 | tf_op jit(solution)/shard_map/ppermute | solution.py:197
  88.6 11.6 %collective-permute-start.7 = (bf16[96,1024]{1,0:T(8,128)(2,1)S(1)}, bf16[96,1024]{1,0:T(8,128)(2,1)S(1)}, u32[]{:S(2)}, u32[]{:S(2)}) collective-permute-start(bf16[96,1024]{1,0:T(8,128)(2,1)S(1)} %get-tuple-element.34), channel_id=1, source_target_pairs={{0,8},{8,16},{16,24},{24,0},{1,9},{9,17},{17,25},{25,1},{2,10},{10... | collective-permute-start | bytes 589832 | tf_op jit(solution)/shard_map/ppermute | solution.py:192
  92.1 11.6 %collective-permute-start.6 = (bf16[96,1024]{1,0:T(8,128)(2,1)S(1)}, bf16[96,1024]{1,0:T(8,128)(2,1)S(1)}, u32[]{:S(2)}, u32[]{:S(2)}) collective-permute-start(bf16[96,1024]{1,0:T(8,128)(2,1)S(1)} %get-tuple-element.32), channel_id=1, source_target_pairs={{0,24},{8,0},{16,8},{24,16},{1,25},{9,1},{17,9},{25,17},{2,26},{10... | collective-permute-start | bytes 589832 | tf_op jit(solution)/shard_map/ppermute | solution.py:195
  92.1 11.6 %collective-permute-start.9 = (bf16[96,1024]{1,0:T(8,128)(2,1)S(1)}, bf16[96,1024]{1,0:T(8,128)(2,1)S(1)}, u32[]{:S(2)}, u32[]{:S(2)}) collective-permute-start(bf16[96,1024]{1,0:T(8,128)(2,1)S(1)} %get-tuple-element.36), channel_id=1, source_target_pairs={{0,8},{8,16},{16,24},{24,0},{1,9},{9,17},{17,25},{25,1},{2,10},{10... | collective-permute-start | bytes 589832 | tf_op jit(solution)/shard_map/ppermute | solution.py:194
  95.4 8.2 %collective-permute-start.10 = (bf16[96,1024]{1,0:T(8,128)(2,1)S(1)}, bf16[96,1024]{1,0:T(8,128)(2,1)S(1)}, u32[]{:S(2)}, u32[]{:S(2)}) collective-permute-start(bf16[96,1024]{1,0:T(8,128)(2,1)S(1)} %get-tuple-element.38), channel_id=1, source_target_pairs={{0,24},{8,0},{16,8},{24,16},{1,25},{9,1},{17,9},{25,17},{2,26},{10... | collective-permute-start | bytes 589832 | tf_op jit(solution)/shard_map/ppermute | solution.py:193
  96.8 15.3 %all-to-all-start.2 = ((bf16[8,48,512]{2,1,0:T(8,128)(2,1)}), bf16[8,48,512]{2,1,0:T(8,128)(2,1)S(1)}, u32[]{:S(2)}, u32[]{:S(2)}) async-start(bf16[8,48,512]{2,1,0:T(8,128)(2,1)} %shard_map.69), calls=%async_computation.2 | async-start | bytes 786432 | tf_op jit(solution)/shard_map/all_to_all | solution.py:214
  100.3 6.5 %collective-permute-start.8 = (bf16[96,1024]{1,0:T(8,128)(2,1)S(1)}, bf16[96,1024]{1,0:T(8,128)(2,1)S(1)}, u32[]{:S(2)}, u32[]{:S(2)}) collective-permute-start(bf16[96,1024]{1,0:T(8,128)(2,1)S(1)} %add_convert_fusion.1), channel_id=1, source_target_pairs={{0,8},{8,16},{16,24},{24,0},{1,9},{9,17},{17,25},{25,1},{2,10},{10... | collective-permute-start | bytes 589832 | tf_op jit(solution)/shard_map/ppermute | solution.py:196
  103.6 7.0 %collective-permute-start.11 = (bf16[96,1024]{1,0:T(8,128)(2,1)S(1)}, bf16[96,1024]{1,0:T(8,128)(2,1)S(1)}, u32[]{:S(2)}, u32[]{:S(2)}) collective-permute-start(bf16[96,1024]{1,0:T(8,128)(2,1)S(1)} %add_convert_fusion), channel_id=1, source_target_pairs={{0,24},{8,0},{16,8},{24,16},{1,25},{9,1},{17,9},{25,17},{2,26},{10... | collective-permute-start | bytes 589832 | tf_op jit(solution)/shard_map/ppermute | solution.py:197

commit v3 on v0

v3 whole, which is shorter than its diff:
```python
import jax
import jax.numpy as jnp
from jax import lax
from jax.experimental import pallas as pl
from jax.experimental.pallas import tpu as pltpu
from jax.sharding import Mesh, PartitionSpec as P

KV = 1024
R = 16
QLEN = 32
PLEN = 48
K = 4096
NX, NZ = 4, 8
N = NX * NZ
MINE = 12
PAIRS = N * MINE
G = 1024
ROWS = MINE * 8
MIB = 1024 * 1024
BF = jnp.bfloat16
F32 = jnp.float32
HBM = pl.BlockSpec(memory_space=pltpu.HBM)
WHOLE = pl.BlockSpec(memory_space=pltpu.VMEM)


def iota(shape, dim):
    return lax.broadcasted_iota(jnp.int32, shape, dim)


def dot(a, b):
    return lax.dot_general(a, b, (((1,), (0,)), ((), ())), preferred_element_type=F32)


def ones_where(mask):
    return jnp.where(mask, 1.0, 0.0).astype(BF)


def call(kernel, out_shape, flops, moved, vmem=24, **kwargs):
    return pl.pallas_call(
        kernel,
        out_shape=out_shape,
        compiler_params=pltpu.CompilerParams(vmem_limit_bytes=vmem * MIB),
        cost_estimate=pl.CostEstimate(flops=flops, bytes_accessed=moved, transcendentals=0),
        **kwargs,
    )


def array(*shape, dtype=BF):
    return jax.ShapeDtypeStruct(shape, dtype)


def grads(q_fact, p_fact, q_cot, p_cot):
    steps = 4
    cols = 2 * KV // steps

    def kernel(q_fact, p_fact, q_cot, p_cot, out, q_spread, p_spread):
        step = pl.program_id(0)
        lane = iota((ROWS, 128), 1)
        for kind, (fact, cot, length, spread) in enumerate(
            ((q_fact, q_cot, QLEN, q_spread), (p_fact, p_cot, PLEN, p_spread))
        ):
            tokens = MINE * length

            @pl.when(step % (steps // 2) == 0)
            def _():
                row = iota((2 * ROWS, 2 * R), 0)
                rank = jnp.where(row >= ROWS, 8, 0) + (row & 7) + (step // (steps // 2)) * R
                pick = ones_where(iota((2 * ROWS, 2 * R), 1) == rank)
                row = iota((2 * ROWS, tokens), 0)
                item = jnp.where(row >= ROWS, row - ROWS, row) >> 3
                token = iota((2 * ROWS, tokens), 1) - item * length
                held = (token >= 0) & (token < length)
                spread[...] = jnp.where(held, dot(pick, fact[...]), 0.0).astype(BF)

            grad = dot(spread[...], cot[...])
            for j in range(cols // 128):
                top = grad[:ROWS, 128 * j : 128 * j + 128]
                low = grad[ROWS:, 128 * j : 128 * j + 128]
                at = pl.ds(kind * ROWS, ROWS)
                out[2 * j, at, :] = jnp.where(lane < 64, top, pltpu.roll(low, 64, 1)).astype(BF)
                out[2 * j + 1, at, :] = jnp.where(lane < 64, pltpu.roll(top, 64, 1), low).astype(BF)

    return call(
        kernel,
        array(N, 2 * ROWS, 128),
        800_000_000,
        5_500_000,
        vmem=60,
        grid=(steps,),
        in_specs=[
            pl.BlockSpec((2 * R, MINE * QLEN), lambda n: (0, 0)),
            pl.BlockSpec((2 * R, MINE * PLEN), lambda n: (0, 0)),
            pl.BlockSpec((MINE * QLEN, cols), lambda n: (0, n)),
            pl.BlockSpec((MINE * PLEN, cols), lambda n: (0, n)),
        ],
        out_specs=pl.BlockSpec((N // steps, 2 * ROWS, 128), lambda n: (n, 0, 0)),
        scratch_shapes=[pltpu.VMEM((2 * ROWS, MINE * QLEN), BF), pltpu.VMEM((2 * ROWS, MINE * PLEN), BF)],
    )(q_fact.T, p_fact.T, q_cot, p_cot)


def permuted(projection):
    def kernel(proj, out, order):
        @pl.when(pl.program_id(0) == 0)
        def _():
            u, v = iota((G, G), 0), iota((G, G), 1)
            order[...] = ones_where(v == (u & 63) * 16 + ((u >> 6) & 1) * 8 + (u >> 7))

        out[...] = dot(order[...], proj[...]).astype(BF)

    tile = pl.BlockSpec((G, 512), lambda n: (0, n))
    return call(
        kernel,
        array(G, K),
        2 * G * G * K,
        16_000_000,
        vmem=60,
        grid=(K // 512,),
        in_specs=[tile],
        out_specs=tile,
        scratch_shapes=[pltpu.VMEM((G, G), BF)],
    )(projection)


def rows_of(recv, kind, at, count):
    pieces = []
    while count:
        src, off = at // ROWS, at % ROWS
        take = min(ROWS - off, count)
        pieces.append(recv[src, kind * ROWS + off : kind * ROWS + off + take, :])
        at, count = at + take, count - take
    return jnp.concatenate(pieces, axis=0)


def halves(pair, proj, outs):
    part = dot(pair[...], proj[...]).astype(BF)
    for d in range(NX):
        outs[d][...] = part[ROWS * d : ROWS * d + ROWS, :]


def product_left(recv, passage_of, proj):
    def kernel(recv, passage, proj, pair, o0, o1, o2, o3, wide_q, wide_p, held, sem):
        copy = pltpu.make_async_copy(proj.at[:, : K // 2], held, sem)
        copy.start()
        x = lax.axis_index("px")
        r, c = iota((256, 256), 0), iota((256, 256), 1)
        swap = ones_where(c == (r & 31) * 8 + (r >> 5))
        for g in range(PAIRS // 32):
            both = jnp.concatenate([rows_of(recv, kind, 256 * g, 256) for kind in range(2)], axis=1)
            mixed = dot(swap, both).astype(BF)
            for b in range(8):
                wide_q[32 * g : 32 * g + 32, 128 * b : 128 * b + 128] = mixed[32 * b : 32 * b + 32, :128]
                wide_p[32 * g : 32 * g + 32, 128 * b : 128 * b + 128] = mixed[32 * b : 32 * b + 32, 128:]
        hot = ones_where(iota((PAIRS, PAIRS), 0) == passage[...])
        picked = lax.dot_general(hot, wide_p[...], (((0,), (0,)), ((), ())), preferred_element_type=F32)
        summed = (wide_q[...].astype(F32) + picked).astype(BF)
        for i in range(NX):
            at = pl.multiple_of(((i - x) & 3) * ROWS, 32)
            pair[pl.ds(at, ROWS), :] = summed[ROWS * i : ROWS * i + ROWS, :]
        copy.wait()
        halves(pair, held, (o0, o1, o2, o3))

    return call(
        kernel,
        [array(PAIRS, G)] + [array(ROWS, K // 2)] * 4,
        2_500_000_000,
        8_000_000,
        in_specs=[WHOLE, WHOLE, HBM],
        scratch_shapes=[
            pltpu.VMEM((PAIRS, G), BF),
            pltpu.VMEM((PAIRS, G), BF),
            pltpu.VMEM((G, K // 2), BF),
            pltpu.SemaphoreType.DMA,
        ],
    )(recv, passage_of.reshape(1, PAIRS), proj)


def product_right(pair, proj):
    def kernel(pair, proj, o0, o1, o2, o3, held, sems):
        copies = []
        for i in range(2):
            at = pl.ds(K // 2 + KV * i, KV)
            copies.append(pltpu.make_async_copy(proj.at[:, at], held.at[i], sems.at[i]))
            copies[i].start()
        for i in range(2):
            copies[i].wait()
            part = dot(pair[...], held[i]).astype(BF)
            for d, out in enumerate((o0, o1, o2, o3)):
                out[:, KV * i : KV * i + KV] = part[ROWS * d : ROWS * d + ROWS, :]

    return call(
        kernel,
        [array(ROWS, K // 2)] * 4,
        1_700_000_000,
        7_000_000,
        in_specs=[WHOLE, HBM],
        scratch_shapes=[pltpu.VMEM((2, G, KV), BF), pltpu.SemaphoreType.DMA((2,))],
    )(pair, proj)


def add(a, b):
    return (a.astype(F32) + b.astype(F32)).astype(BF)


def shift(x, axis, size, by):
    return lax.ppermute(x, axis, [(i, (i + by) % size) for i in range(size)])


def across_x(left, right):
    l0, l1, l2, l3 = left
    r0, r1, r2, r3 = right
    far_l = shift(l2, "px", NX, 1)
    got_l = shift(l3, "px", NX, -1)
    far_r = shift(r2, "px", NX, -1)
    got_r = shift(r1, "px", NX, 1)
    sum_l = shift(add(l1, far_l), "px", NX, 1)
    sum_r = shift(add(r3, far_r), "px", NX, -1)
    return l0, got_l, sum_l, r0, got_r, sum_r


def across_z(terms):
    def kernel(l0, l1, l2, r0, r1, r2, *outs):
        left = (l0[...].astype(F32) + l1[...].astype(F32) + l2[...].astype(F32)).astype(BF)
        right = (r0[...].astype(F32) + r1[...].astype(F32) + r2[...].astype(F32)).astype(BF)
        stacked = jnp.concatenate([left[:, :KV], left[:, KV:], right[:, :KV], right[:, KV:]], axis=0)
        r, c = iota((4 * ROWS, 4 * ROWS), 0), iota((4 * ROWS, 4 * ROWS), 1)
        block = r // 48
        quarter = (r - block * 48) // MINE
        item = r - block * 48 - quarter * MINE
        z = (block + lax.axis_index("pz")) & (NZ - 1)
        hot = ones_where(c == quarter * ROWS + z * MINE + item)
        rows = dot(hot, stacked).astype(BF)
        for k in range(NZ):
            outs[k][...] = rows[48 * k : 48 * k + 48, :]

    blocks = call(kernel, [array(48, KV)] * NZ, 300_000_000, 4_000_000)(*terms)
    return [blocks[0]] + [shift(blocks[k], "pz", NZ, k) for k in (4, 3, 5, 2, 6, 1, 7)]


def last_sum(parts):
    def kernel(*refs):
        out = refs[NZ]
        total = refs[0][...].astype(F32)
        for i in range(1, NZ):
            total = total + refs[i][...].astype(F32)
        for q in range(4):
            out[:, KV * q : KV * q + KV] = total[MINE * q : MINE * q + MINE, :]

    return call(kernel, array(MINE, K, dtype=F32), 1_000_000, 1_000_000)(*parts)


def local(q_fact, p_fact, q_cot, p_cot, passage_of, projection):
    recv = lax.all_to_all(grads(q_fact, p_fact, q_cot, p_cot), ("px", "pz"), 0, 0, tiled=True)
    proj = permuted(projection)
    pair, *left = product_left(recv, passage_of, proj)
    return last_sum(across_z(across_x(left, product_right(pair, proj))))


def solution(mesh):
    cut = Mesh(mesh.devices.reshape(mesh.shape["pairs"], NX, NZ), ("pairs", "px", "pz"))
    rows = P(("pairs", "px", "pz"), None)
    return jax.shard_map(
        local,
        mesh=cut,
        in_specs=(rows, rows, rows, rows, P("pairs"), P(("px", "pz"), None)),
        out_specs=rows,
        check_vma=False,
    )
```

time: 389 us -> 117 us (0.30); the launches traced: 383 us -> 116 us
  blocking collectives: 209 us -> 0 us
  local copies, waits for them, and re-layouts: 46.8 us -> 3.39 us
  Pallas kernels: 0 us -> 28.9 us
  matrix products: 17.1 us -> 0 us
  between operations: 14.4 us -> 0.1 us
  waiting for transfers between devices: 60 us -> 47.3 us
    all_gather x1 -> x0, blocking collectives: 105 us -> none  [local(): lax.all_gather(q_fact, 'proj', axis=0, tiled=True)]
    unnamed x1 -> x0, blocking collectives: 104 us -> none
    pallas_call x0 -> x6, Pallas kernels: none -> 28.9 us  [the longest x1 14.1 us: permuted(): call(kernel, array(G, K), 2 * G * G * K, 16000000, vmem=60, grid=(K // 51...]
    unnamed x9 -> x0, waiting for transfers between devices: 26.9 us -> none
    ppermute x0 -> x13, starting transfers between devices: none -> 24.7 us  [shift(): return lax.ppermute(x, axis, [(i, (i + by) % size) for i in range(size)])]
    ppermute x0 -> x13, waiting for transfers between devices: none -> 24.4 us  [shift(): return lax.ppermute(x, axis, [(i, (i + by) % size) for i in range(size)])]
    unnamed x27 -> x4, local copies, waits for them, and re-layouts: 23.3 us -> 3.39 us
    dot_general x3 -> x0, matrix products: 17.1 us -> none  [the longest x1 8.89 us: local(): jnp.dot(pair_grad, projection, preferred_element_type=jnp.float32)]
  transfers between devices with their start and end apart: 11 -> 14, of which waited for: 4 -> 11; matrix products, arithmetic and copies ran while one was open for 6% -> 0% of each run, Pallas kernels for 0% -> 14%
where the time goes in v3:
time: 117 us; the launch traced here: 116 us
  waiting for transfers between devices  47.3 us (40%)
  starting transfers between devices  36.5 us (31%)
  Pallas kernels  28.9 us (25%)
  local copies, waits for them, and re-layouts  3.39 us (3%)
    ppermute x13, starting transfers between devices, shift(): return lax.ppermute(x, axis, [(i, (i + by) % size) for i in range(size)])  24.7 us
    ppermute x13, waiting for transfers between devices, shift(): return lax.ppermute(x, axis, [(i, (i + by) % size) for i in range(size)])  24.4 us
    all_to_all x1, waiting for transfers between devices, local(): lax.all_to_all(grads(q_fact, p_fact, q_cot, p_cot), ('px', 'pz'), 0, 0, t...  23 us
    pallas_call x1, Pallas kernels, permuted(): call(kernel, array(G, K), 2 * G * G * K, 16000000, vmem=60, grid=(K // 51...  14.1 us
    all_to_all x1, starting transfers between devices, local(): lax.all_to_all(grads(q_fact, p_fact, q_cot, p_cot), ('px', 'pz'), 0, 0, t...  11.7 us
    pallas_call x1, Pallas kernels, grads(): call(kernel, array(N, 2 * ROWS, 128), 800000000, 5500000, vmem=60, grid=(...  6.37 us
    pallas_call x1, Pallas kernels, product_left(): call(kernel, [array(PAIRS, G)] + [array(ROWS, K // 2)] * 4, 2500000000, 8...  3.94 us
    unnamed x4, local copies, waits for them, and re-layouts  3.39 us
  transfers between devices with their start and end apart: 14, of which 11 were waited for; matrix products, arithmetic and copies ran while one was open for 0% of the time, Pallas kernels for 14%

profile of v3, /device:TPU:14, one launch (start us, length us, event | category | flops | bytes accessed | tf_op | source)
XLA Modules:
  0.0 116.4 jit_solution(17860314218053303876)
XLA Ops:
  0.0 6.4 %shard_map.64 = bf16[32,192,128]{2,1,0:T(8,128)(2,1)} custom-call(bf16[32,384]{1,0:T(8,128)(2,1)} %bitcast.3, bf16[32,576]{1,0:T(8,128)(2,1)} %bitcast.2, bf16[384,2048]{1,0:T(8,128)(2,1)} %q_cot.1, bf16[576,2048]{1,0:T(8,128)(2,1)} %p_cot.1), custom_call_target="tpu_custom_call" | custom-call | flops 800000000 | bytes 5500000 | tf_op jit(solution)/shard_map/pallas_call | solution.py:83
  6.4 0.0 copy-start.1
  6.4 11.7 %all-to-all-start = ((bf16[32,192,128]{2,1,0:T(8,128)(2,1)}), bf16[32,192,128]{2,1,0:T(8,128)(2,1)S(1)}, u32[]{:S(2)}, u32[]{:S(2)}) async-start(bf16[32,192,128]{2,1,0:T(8,128)(2,1)} %shard_map.64), calls=%async_computation | async-start | bytes 3145728 | tf_op jit(solution)/shard_map/all_to_all | solution.py:252
  18.1 0.0 copy-done.1
  18.1 14.1 %shard_map.65.proj = bf16[1024,4096]{1,0:T(8,128)(2,1)} custom-call(bf16[1024,4096]{1,0:T(8,128)(2,1)} %proj.1), custom_call_target="tpu_custom_call" | custom-call | flops 8589934592 | bytes 16000000 | tf_op jit(solution)/shard_map/pallas_call | solution.py:111
  32.2 23.0 %all-to-all-done.recv = bf16[32,192,128]{2,1,0:T(8,128)(2,1)S(1)} async-done(((bf16[32,192,128]{2,1,0:T(8,128)(2,1)}), bf16[32,192,128]{2,1,0:T(8,128)(2,1)S(1)}, u32[]{:S(2)}, u32[]{:S(2)}) %all-to-all-start) | async-done | bytes 1572896 | tf_op jit(solution)/shard_map/all_to_all | solution.py:252
  55.2 0.0 copy-start
  55.2 3.4 %copy-done = bf16[1024,4096]{1,0:T(8,128)(2,1)S(1)} copy-done((bf16[1024,4096]{1,0:T(8,128)(2,1)S(1)}, bf16[1024,4096]{1,0:T(8,128)(2,1)}, u32[]{:S(2)}) %copy-start) | copy-done | bytes 8388632
  58.6 3.9 %shard_map.66 = (bf16[384,1024]{1,0:T(8,128)(2,1)S(1)}, bf16[96,2048]{1,0:T(8,128)(2,1)S(1)}, bf16[96,2048]{1,0:T(8,128)(2,1)S(1)}, bf16[96,2048]{1,0:T(8,128)(2,1)S(1)}, bf16[96,2048]{1,0:T(8,128)(2,1)S(1)}) custom-call(bf16[32,192,128]{2,1,0:T(8,128)(2,1)S(1)} %all-to-all-done.recv, s32[1,384]{1,0:T(1,128)S(1)} %reshape.3.passage, ...), custom_call_target="tpu_custom_call" | custom-call | flops 2500000000 | bytes 8000000 | tf_op jit(solution)/shard_map/pallas_call | solution.py:162
  62.5 2.5 %collective-permute-start.1 = (bf16[96,2048]{1,0:T(8,128)(2,1)S(1)}, bf16[96,2048]{1,0:T(8,128)(2,1)S(1)}, u32[]{:S(2)}, u32[]{:S(2)}) collective-permute-start(bf16[96,2048]{1,0:T(8,128)(2,1)S(1)} %get-tuple-element.25), channel_id=1, source_target_pairs={{0,8},{8,16},{16,24},{24,0},{1,9},{9,17},{17,25},{25,1},{2,10},{10... | collective-permute-start | bytes 1179656 | tf_op jit(solution)/shard_map/ppermute | solution.py:205
  65.0 0.0 collective-permute-start
  65.0 2.8 %shard_map.67 = (bf16[96,2048]{1,0:T(8,128)(2,1)S(1)}, bf16[96,2048]{1,0:T(8,128)(2,1)S(1)}, bf16[96,2048]{1,0:T(8,128)(2,1)S(1)}, bf16[96,2048]{1,0:T(8,128)(2,1)S(1)}) custom-call(bf16[384,1024]{1,0:T(8,128)(2,1)S(1)} %get-tuple-element.26.pair, bf16[1024,4096]{1,0:T(8,128)(2,1)S(1)} %copy-done), custom_call_target="tpu_custom_call" | custom-call | flops 1700000000 | bytes 7000000 | tf_op jit(solution)/shard_map/pallas_call | solution.py:190
  67.8 3.3 %collective-permute-start.3 = (bf16[96,2048]{1,0:T(8,128)(2,1)S(1)}, bf16[96,2048]{1,0:T(8,128)(2,1)S(1)}, u32[]{:S(2)}, u32[]{:S(2)}) collective-permute-start(bf16[96,2048]{1,0:T(8,128)(2,1)S(1)} %get-tuple-element.28), channel_id=1, source_target_pairs={{0,8},{8,16},{16,24},{24,0},{1,9},{9,17},{17,25},{25,1},{2,10},{10... | collective-permute-start | bytes 1179656 | tf_op jit(solution)/shard_map/ppermute | solution.py:205
  71.2 0.0 collective-permute-start.4
  71.2 3.5 %collective-permute-done.1 = bf16[96,2048]{1,0:T(8,128)(2,1)S(1)} collective-permute-done((bf16[96,2048]{1,0:T(8,128)(2,1)S(1)}, bf16[96,2048]{1,0:T(8,128)(2,1)S(1)}, u32[]{:S(2)}, u32[]{:S(2)}) %collective-permute-start.1) | collective-permute-done | bytes 393248 | tf_op jit(solution)/shard_map/ppermute | solution.py:205
  74.7 0.1 add_convert_fusion.1
  74.8 2.5 %collective-permute-start.2 = (bf16[96,2048]{1,0:T(8,128)(2,1)S(1)}, bf16[96,2048]{1,0:T(8,128)(2,1)S(1)}, u32[]{:S(2)}, u32[]{:S(2)}) collective-permute-start(bf16[96,2048]{1,0:T(8,128)(2,1)S(1)} %add_convert_fusion.1), channel_id=1, source_target_pairs={{0,8},{8,16},{16,24},{24,0},{1,9},{9,17},{17,25},{25,1},{2,10},{10... | collective-permute-start | bytes 1179656 | tf_op jit(solution)/shard_map/ppermute | solution.py:205
  77.3 5.2 %collective-permute-done.4 = bf16[96,2048]{1,0:T(8,128)(2,1)S(1)} collective-permute-done((bf16[96,2048]{1,0:T(8,128)(2,1)S(1)}, bf16[96,2048]{1,0:T(8,128)(2,1)S(1)}, u32[]{:S(2)}, u32[]{:S(2)}) %collective-permute-start.4) | collective-permute-done | bytes 393248 | tf_op jit(solution)/shard_map/ppermute | solution.py:205
  82.5 0.1 add_convert_fusion
  82.6 0.1 collective-permute-start.5
  82.7 0.0 collective-permute-done.l1
  82.7 0.4 collective-permute-done.3.r1
  83.1 4.7 %collective-permute-done.2.l2 = bf16[96,2048]{1,0:T(8,128)(2,1)S(1)} collective-permute-done((bf16[96,2048]{1,0:T(8,128)(2,1)S(1)}, bf16[96,2048]{1,0:T(8,128)(2,1)S(1)}, u32[]{:S(2)}, u32[]{:S(2)}) %collective-permute-start.2) | collective-permute-done | bytes 393248 | tf_op jit(solution)/shard_map/ppermute | solution.py:205
  87.8 4.3 %collective-permute-done.5.r2 = bf16[96,2048]{1,0:T(8,128)(2,1)S(1)} collective-permute-done((bf16[96,2048]{1,0:T(8,128)(2,1)S(1)}, bf16[96,2048]{1,0:T(8,128)(2,1)S(1)}, u32[]{:S(2)}, u32[]{:S(2)}) %collective-permute-start.5) | collective-permute-done | bytes 393248 | tf_op jit(solution)/shard_map/ppermute | solution.py:205
  92.1 0.9 shard_map.68
  93.0 5.2 %collective-permute-start.6 = (bf16[48,1024]{1,0:T(8,128)(2,1)S(1)}, bf16[48,1024]{1,0:T(8,128)(2,1)S(1)}, u32[]{:S(2)}, u32[]{:S(2)}) collective-permute-start(bf16[48,1024]{1,0:T(8,128)(2,1)S(1)} %get-tuple-element.32), channel_id=1, source_target_pairs={{0,4},{1,5},{2,6},{3,7},{4,0},{5,1},{6,2},{7,3},{8,12},{9,13},{10,... | collective-permute-start | bytes 294920 | tf_op jit(solution)/shard_map/ppermute | solution.py:205
  98.3 2.3 %collective-permute-start.7 = (bf16[48,1024]{1,0:T(8,128)(2,1)S(1)}, bf16[48,1024]{1,0:T(8,128)(2,1)S(1)}, u32[]{:S(2)}, u32[]{:S(2)}) collective-permute-start(bf16[48,1024]{1,0:T(8,128)(2,1)S(1)} %get-tuple-element.33), channel_id=1, source_target_pairs={{0,3},{1,4},{2,5},{3,6},{4,7},{5,0},{6,1},{7,2},{8,11},{9,12},{10,... | collective-permute-start | bytes 294920 | tf_op jit(solution)/shard_map/ppermute | solution.py:205
  100.5 2.8 %collective-permute-start.8 = (bf16[48,1024]{1,0:T(8,128)(2,1)S(1)}, bf16[48,1024]{1,0:T(8,128)(2,1)S(1)}, u32[]{:S(2)}, u32[]{:S(2)}) collective-permute-start(bf16[48,1024]{1,0:T(8,128)(2,1)S(1)} %get-tuple-element.34), channel_id=1, source_target_pairs={{0,5},{1,6},{2,7},{3,0},{4,1},{5,2},{6,3},{7,4},{8,13},{9,14},{10,... | collective-permute-start | bytes 294920 | tf_op jit(solution)/shard_map/ppermute | solution.py:205
  103.3 0.0 collective-permute-start.9
  103.3 4.1 %collective-permute-start.10 = (bf16[48,1024]{1,0:T(8,128)(2,1)S(1)}, bf16[48,1024]{1,0:T(8,128)(2,1)S(1)}, u32[]{:S(2)}, u32[]{:S(2)}) collective-permute-start(bf16[48,1024]{1,0:T(8,128)(2,1)S(1)} %get-tuple-element.36), channel_id=1, source_target_pairs={{0,6},{1,7},{2,0},{3,1},{4,2},{5,3},{6,4},{7,5},{8,14},{9,15},{10,... | collective-permute-start | bytes 294920 | tf_op jit(solution)/shard_map/ppermute | solution.py:205
  107.5 0.0 collective-permute-done.6.refs_1_
  107.5 1.6 %collective-permute-start.11 = (bf16[48,1024]{1,0:T(8,128)(2,1)S(1)}, bf16[48,1024]{1,0:T(8,128)(2,1)S(1)}, u32[]{:S(2)}, u32[]{:S(2)}) collective-permute-start(bf16[48,1024]{1,0:T(8,128)(2,1)S(1)} %get-tuple-element.37), channel_id=1, source_target_pairs={{0,1},{1,2},{2,3},{3,4},{4,5},{5,6},{6,7},{7,0},{8,9},{9,10},{10,1... | collective-permute-start | bytes 294920 | tf_op jit(solution)/shard_map/ppermute | solution.py:205
  109.1 1.4 %collective-permute-done.7.refs_2_ = bf16[48,1024]{1,0:T(8,128)(2,1)S(1)} collective-permute-done((bf16[48,1024]{1,0:T(8,128)(2,1)S(1)}, bf16[48,1024]{1,0:T(8,128)(2,1)S(1)}, u32[]{:S(2)}, u32[]{:S(2)}) %collective-permute-start.7) | collective-permute-done | bytes 98336 | tf_op jit(solution)/shard_map/ppermute | solution.py:205
  110.4 0.3 collective-permute-start.12
  110.7 0.0 collective-permute-done.8.refs_3_
  110.7 3.1 %collective-permute-done.9.refs_4_ = bf16[48,1024]{1,0:T(8,128)(2,1)S(1)} collective-permute-done((bf16[48,1024]{1,0:T(8,128)(2,1)S(1)}, bf16[48,1024]{1,0:T(8,128)(2,1)S(1)}, u32[]{:S(2)}, u32[]{:S(2)}) %collective-permute-start.9) | collective-permute-done | bytes 98336 | tf_op jit(solution)/shard_map/ppermute | solution.py:205
  113.8 0.4 collective-permute-done.10.refs_5_
  114.3 0.2 collective-permute-done.11.refs_6_
  114.5 1.1 collective-permute-done.12.refs_7_
  115.5 0.8 shard_map.69
  (1 shorter events, 0.0 us)
Async XLA Ops:
  6.4 11.7 %copy-start.1 = (s32[384]{0:T(512)S(1)}, s32[384]{0:T(512)}, u32[]{:S(2)}) copy-start(s32[384]{0:T(512)} %param.10) | copy-start | bytes 4612
  6.4 48.8 %all-to-all-start = ((bf16[32,192,128]{2,1,0:T(8,128)(2,1)}), bf16[32,192,128]{2,1,0:T(8,128)(2,1)S(1)}, u32[]{:S(2)}, u32[]{:S(2)}) async-start(bf16[32,192,128]{2,1,0:T(8,128)(2,1)} %shard_map.64), calls=%async_computation | async-start | bytes 3145728 | tf_op jit(solution)/shard_map/all_to_all | solution.py:252
  55.2 3.4 %copy-start = (bf16[1024,4096]{1,0:T(8,128)(2,1)S(1)}, bf16[1024,4096]{1,0:T(8,128)(2,1)}, u32[]{:S(2)}) copy-start(bf16[1024,4096]{1,0:T(8,128)(2,1)} %shard_map.65.proj) | copy-start | bytes 25165828
  62.5 12.1 %collective-permute-start.1 = (bf16[96,2048]{1,0:T(8,128)(2,1)S(1)}, bf16[96,2048]{1,0:T(8,128)(2,1)S(1)}, u32[]{:S(2)}, u32[]{:S(2)}) collective-permute-start(bf16[96,2048]{1,0:T(8,128)(2,1)S(1)} %get-tuple-element.25), channel_id=1, source_target_pairs={{0,8},{8,16},{16,24},{24,0},{1,9},{9,17},{17,25},{25,1},{2,10},{10... | collective-permute-start | bytes 1179656 | tf_op jit(solution)/shard_map/ppermute | solution.py:205
  65.0 17.6 %collective-permute-start = (bf16[96,2048]{1,0:T(8,128)(2,1)S(1)}, bf16[96,2048]{1,0:T(8,128)(2,1)S(1)}, u32[]{:S(2)}, u32[]{:S(2)}) collective-permute-start(bf16[96,2048]{1,0:T(8,128)(2,1)S(1)} %get-tuple-element.23), channel_id=1, source_target_pairs={{0,24},{8,0},{16,8},{24,16},{1,25},{9,1},{17,9},{25,17},{2,26},{10... | collective-permute-start | bytes 1179656 | tf_op jit(solution)/shard_map/ppermute | solution.py:205
  67.8 15.3 %collective-permute-start.3 = (bf16[96,2048]{1,0:T(8,128)(2,1)S(1)}, bf16[96,2048]{1,0:T(8,128)(2,1)S(1)}, u32[]{:S(2)}, u32[]{:S(2)}) collective-permute-start(bf16[96,2048]{1,0:T(8,128)(2,1)S(1)} %get-tuple-element.28), channel_id=1, source_target_pairs={{0,8},{8,16},{16,24},{24,0},{1,9},{9,17},{17,25},{25,1},{2,10},{10... | collective-permute-start | bytes 1179656 | tf_op jit(solution)/shard_map/ppermute | solution.py:205
  71.2 11.3 %collective-permute-start.4 = (bf16[96,2048]{1,0:T(8,128)(2,1)S(1)}, bf16[96,2048]{1,0:T(8,128)(2,1)S(1)}, u32[]{:S(2)}, u32[]{:S(2)}) collective-permute-start(bf16[96,2048]{1,0:T(8,128)(2,1)S(1)} %get-tuple-element.30), channel_id=1, source_target_pairs={{0,24},{8,0},{16,8},{24,16},{1,25},{9,1},{17,9},{25,17},{2,26},{10... | collective-permute-start | bytes 1179656 | tf_op jit(solution)/shard_map/ppermute | solution.py:205
  74.8 13.0 %collective-permute-start.2 = (bf16[96,2048]{1,0:T(8,128)(2,1)S(1)}, bf16[96,2048]{1,0:T(8,128)(2,1)S(1)}, u32[]{:S(2)}, u32[]{:S(2)}) collective-permute-start(bf16[96,2048]{1,0:T(8,128)(2,1)S(1)} %add_convert_fusion.1), channel_id=1, source_target_pairs={{0,8},{8,16},{16,24},{24,0},{1,9},{9,17},{17,25},{25,1},{2,10},{10... | collective-permute-start | bytes 1179656 | tf_op jit(solution)/shard_map/ppermute | solution.py:205
  82.6 9.6 %collective-permute-start.5 = (bf16[96,2048]{1,0:T(8,128)(2,1)S(1)}, bf16[96,2048]{1,0:T(8,128)(2,1)S(1)}, u32[]{:S(2)}, u32[]{:S(2)}) collective-permute-start(bf16[96,2048]{1,0:T(8,128)(2,1)S(1)} %add_convert_fusion), channel_id=1, source_target_pairs={{0,24},{8,0},{16,8},{24,16},{1,25},{9,1},{17,9},{25,17},{2,26},{10... | collective-permute-start | bytes 1179656 | tf_op jit(solution)/shard_map/ppermute | solution.py:205
  93.0 14.4 %collective-permute-start.6 = (bf16[48,1024]{1,0:T(8,128)(2,1)S(1)}, bf16[48,1024]{1,0:T(8,128)(2,1)S(1)}, u32[]{:S(2)}, u32[]{:S(2)}) collective-permute-start(bf16[48,1024]{1,0:T(8,128)(2,1)S(1)} %get-tuple-element.32), channel_id=1, source_target_pairs={{0,4},{1,5},{2,6},{3,7},{4,0},{5,1},{6,2},{7,3},{8,12},{9,13},{10,... | collective-permute-start | bytes 294920 | tf_op jit(solution)/shard_map/ppermute | solution.py:205
  98.3 12.2 %collective-permute-start.7 = (bf16[48,1024]{1,0:T(8,128)(2,1)S(1)}, bf16[48,1024]{1,0:T(8,128)(2,1)S(1)}, u32[]{:S(2)}, u32[]{:S(2)}) collective-permute-start(bf16[48,1024]{1,0:T(8,128)(2,1)S(1)} %get-tuple-element.33), channel_id=1, source_target_pairs={{0,3},{1,4},{2,5},{3,6},{4,7},{5,0},{6,1},{7,2},{8,11},{9,12},{10,... | collective-permute-start | bytes 294920 | tf_op jit(solution)/shard_map/ppermute | solution.py:205
  100.5 10.2 %collective-permute-start.8 = (bf16[48,1024]{1,0:T(8,128)(2,1)S(1)}, bf16[48,1024]{1,0:T(8,128)(2,1)S(1)}, u32[]{:S(2)}, u32[]{:S(2)}) collective-permute-start(bf16[48,1024]{1,0:T(8,128)(2,1)S(1)} %get-tuple-element.34), channel_id=1, source_target_pairs={{0,5},{1,6},{2,7},{3,0},{4,1},{5,2},{6,3},{7,4},{8,13},{9,14},{10,... | collective-permute-start | bytes 294920 | tf_op jit(solution)/shard_map/ppermute | solution.py:205
  103.3 10.5 %collective-permute-start.9 = (bf16[48,1024]{1,0:T(8,128)(2,1)S(1)}, bf16[48,1024]{1,0:T(8,128)(2,1)S(1)}, u32[]{:S(2)}, u32[]{:S(2)}) collective-permute-start(bf16[48,1024]{1,0:T(8,128)(2,1)S(1)} %get-tuple-element.35), channel_id=1, source_target_pairs={{0,2},{1,3},{2,4},{3,5},{4,6},{5,7},{6,0},{7,1},{8,10},{9,11},{10,... | collective-permute-start | bytes 294920 | tf_op jit(solution)/shard_map/ppermute | solution.py:205
  103.3 10.9 %collective-permute-start.10 = (bf16[48,1024]{1,0:T(8,128)(2,1)S(1)}, bf16[48,1024]{1,0:T(8,128)(2,1)S(1)}, u32[]{:S(2)}, u32[]{:S(2)}) collective-permute-start(bf16[48,1024]{1,0:T(8,128)(2,1)S(1)} %get-tuple-element.36), channel_id=1, source_target_pairs={{0,6},{1,7},{2,0},{3,1},{4,2},{5,3},{6,4},{7,5},{8,14},{9,15},{10,... | collective-permute-start | bytes 294920 | tf_op jit(solution)/shard_map/ppermute | solution.py:205
  107.5 7.0 %collective-permute-start.11 = (bf16[48,1024]{1,0:T(8,128)(2,1)S(1)}, bf16[48,1024]{1,0:T(8,128)(2,1)S(1)}, u32[]{:S(2)}, u32[]{:S(2)}) collective-permute-start(bf16[48,1024]{1,0:T(8,128)(2,1)S(1)} %get-tuple-element.37), channel_id=1, source_target_pairs={{0,1},{1,2},{2,3},{3,4},{4,5},{5,6},{6,7},{7,0},{8,9},{9,10},{10,1... | collective-permute-start | bytes 294920 | tf_op jit(solution)/shard_map/ppermute | solution.py:205
  110.4 5.1 %collective-permute-start.12 = (bf16[48,1024]{1,0:T(8,128)(2,1)S(1)}, bf16[48,1024]{1,0:T(8,128)(2,1)S(1)}, u32[]{:S(2)}, u32[]{:S(2)}) collective-permute-start(bf16[48,1024]{1,0:T(8,128)(2,1)S(1)} %get-tuple-element.38), channel_id=1, source_target_pairs={{0,7},{1,0},{2,1},{3,2},{4,3},{5,4},{6,5},{7,6},{8,15},{9,8},{10,9... | collective-permute-start | bytes 294920 | tf_op jit(solution)/shard_map/ppermute | solution.py:205

commit v4 on v3

v4 whole, which is shorter than its diff:
```python
import jax
import jax.numpy as jnp
from jax import lax
from jax.experimental import pallas as pl
from jax.experimental.pallas import tpu as pltpu
from jax.sharding import Mesh, PartitionSpec as P

KV = 1024
R = 16
QLEN = 32
PLEN = 48
K = 4096
NX, NZ = 4, 8
N = NX * NZ
MINE = 12
PAIRS = N * MINE
G = 1024
ROWS = MINE * 8
MIB = 1024 * 1024
BF = jnp.bfloat16
F32 = jnp.float32
HBM = pl.BlockSpec(memory_space=pltpu.HBM)
WHOLE = pl.BlockSpec(memory_space=pltpu.VMEM)


def iota(shape, dim):
    return lax.broadcasted_iota(jnp.int32, shape, dim)


def dot(a, b):
    return lax.dot_general(a, b, (((1,), (0,)), ((), ())), preferred_element_type=F32)


def ones_where(mask):
    return jnp.where(mask, 1.0, 0.0).astype(BF)


def call(kernel, out_shape, flops, moved, vmem=24, **kwargs):
    return pl.pallas_call(
        kernel,
        out_shape=out_shape,
        compiler_params=pltpu.CompilerParams(vmem_limit_bytes=vmem * MIB),
        cost_estimate=pl.CostEstimate(flops=flops, bytes_accessed=moved, transcendentals=0),
        **kwargs,
    )


def array(*shape, dtype=BF):
    return jax.ShapeDtypeStruct(shape, dtype)


def grads(q_fact, p_fact, q_cot, p_cot):
    steps = 4
    cols = 2 * KV // steps
    dests = N // steps

    def kernel(q_fact, p_fact, q_cot, p_cot, out, q_held, p_held, made, in_sems, out_sems):
        def load(kind, n):
            cot, held = ((q_cot, q_held), (p_cot, p_held))[kind]
            return pltpu.make_async_copy(cot.at[:, pl.ds(cols * n, cols)], held.at[n], in_sems.at[kind, n])

        def store(n):
            at = pl.ds(dests * n, dests)
            return pltpu.make_async_copy(made.at[at], out.at[at], out_sems.at[n])

        for n in range(steps):
            for kind in range(2):
                load(kind, n).start()
        lane = iota((ROWS, 128), 1)
        spreads = []
        for layer in range(2):
            for fact, length in ((q_fact, QLEN), (p_fact, PLEN)):
                tokens = MINE * length
                row = iota((2 * ROWS, R), 0)
                rank = jnp.where(row >= ROWS, 8, 0) + (row & 7)
                pick = ones_where(iota((2 * ROWS, R), 1) == rank)
                row = iota((2 * ROWS, tokens), 0)
                item = jnp.where(row >= ROWS, row - ROWS, row) >> 3
                token = iota((2 * ROWS, tokens), 1) - item * length
                held = (token >= 0) & (token < length)
                rows = dot(pick, fact[R * layer : R * layer + R, :])
                spreads.append(jnp.where(held, rows, 0.0).astype(BF))
        for n in range(steps):
            for kind, held in enumerate((q_held, p_held)):
                load(kind, n).wait()
                grad = dot(spreads[2 * (2 * n // steps) + kind], held[n])
                for j in range(cols // 128):
                    top = grad[:ROWS, 128 * j : 128 * j + 128]
                    low = grad[ROWS:, 128 * j : 128 * j + 128]
                    at = pl.ds(kind * ROWS, ROWS)
                    dest = dests * n + 2 * j
                    made[dest, at, :] = jnp.where(lane < 64, top, pltpu.roll(low, 64, 1)).astype(BF)
                    made[dest + 1, at, :] = jnp.where(lane < 64, pltpu.roll(top, 64, 1), low).astype(BF)
            store(n).start()
        for n in range(steps):
            store(n).wait()

    return call(
        kernel,
        array(N, 2 * ROWS, 128),
        800_000_000,
        5_500_000,
        vmem=60,
        in_specs=[WHOLE, WHOLE, HBM, HBM],
        out_specs=HBM,
        scratch_shapes=[
            pltpu.VMEM((steps, MINE * QLEN, cols), BF),
            pltpu.VMEM((steps, MINE * PLEN, cols), BF),
            pltpu.VMEM((N, 2 * ROWS, 128), BF),
            pltpu.SemaphoreType.DMA((2, steps)),
            pltpu.SemaphoreType.DMA((steps,)),
        ],
    )(q_fact.T, p_fact.T, q_cot, p_cot)


def prepared(projection, passage_of):
    steps = 8
    cols = K // steps

    def kernel(passage, proj, out, hot, held, made, order, in_sems, out_sems):
        def load(n):
            return pltpu.make_async_copy(proj.at[:, pl.ds(cols * n, cols)], held.at[n], in_sems.at[n])

        def store(n):
            return pltpu.make_async_copy(made.at[n], out.at[:, pl.ds(cols * n, cols)], out_sems.at[n])

        for n in range(steps):
            load(n).start()
        hot[...] = ones_where(iota((PAIRS, PAIRS), 1) == passage[...])
        u, v = iota((G, G), 0), iota((G, G), 1)
        order[...] = ones_where(v == (u & 63) * 16 + ((u >> 6) & 1) * 8 + (u >> 7))
        for n in range(steps):
            load(n).wait()
            made[n] = dot(order[...], held[n]).astype(BF)
            store(n).start()
        for n in range(steps):
            store(n).wait()

    return call(
        kernel,
        [array(G, K), array(PAIRS, PAIRS)],
        2 * G * G * K,
        16_000_000,
        vmem=32,
        in_specs=[WHOLE, HBM],
        out_specs=[HBM, WHOLE],
        scratch_shapes=[
            pltpu.VMEM((steps, G, cols), BF),
            pltpu.VMEM((steps, G, cols), BF),
            pltpu.VMEM((G, G), BF),
            pltpu.SemaphoreType.DMA((steps,)),
            pltpu.SemaphoreType.DMA((steps,)),
        ],
    )(passage_of.reshape(PAIRS, 1), projection)


def rows_of(recv, kind, at, count):
    pieces = []
    while count:
        src, off = at // ROWS, at % ROWS
        take = min(ROWS - off, count)
        pieces.append(recv[src, kind * ROWS + off : kind * ROWS + off + take, :])
        at, count = at + take, count - take
    return jnp.concatenate(pieces, axis=0)


def parts(pair, proj, held, sems, takes):
    for i in range(4):
        pltpu.make_async_copy(proj.at[:, pl.ds(KV * i, KV)], held.at[i], sems.at[i]).wait()
        first, outs = takes[i // 2]
        part = dot(pair[ROWS * first : ROWS * (first + len(outs)), :], held[i]).astype(BF)
        for j, out in enumerate(outs):
            out[:, KV * (i % 2) : KV * (i % 2) + KV] = part[ROWS * j : ROWS * j + ROWS, :]


def fetch(proj, held, sems):
    for i in range(4):
        pltpu.make_async_copy(proj.at[:, pl.ds(KV * i, KV)], held.at[i], sems.at[i]).start()


QUARTERS = [pltpu.VMEM((4, G, KV), BF), pltpu.SemaphoreType.DMA((4,))]


def product_far(recv, hot, proj):
    def kernel(recv, hot, proj, pair, l1, l2, r2, r3, wide_q, wide_p, held, sems):
        fetch(proj, held, sems)
        x = lax.axis_index("px")
        r, c = iota((256, 256), 0), iota((256, 256), 1)
        swap = ones_where(c == (r & 31) * 8 + (r >> 5))
        for g in range(PAIRS // 32):
            both = jnp.concatenate([rows_of(recv, kind, 256 * g, 256) for kind in range(2)], axis=1)
            mixed = dot(swap, both).astype(BF)
            for b in range(8):
                wide_q[32 * g : 32 * g + 32, 128 * b : 128 * b + 128] = mixed[32 * b : 32 * b + 32, :128]
                wide_p[32 * g : 32 * g + 32, 128 * b : 128 * b + 128] = mixed[32 * b : 32 * b + 32, 128:]
        summed = (wide_q[...].astype(F32) + dot(hot[...], wide_p[...])).astype(BF)
        for i in range(NX):
            at = pl.multiple_of(((i - x) & 3) * ROWS, 32)
            pair[pl.ds(at, ROWS), :] = summed[ROWS * i : ROWS * i + ROWS, :]
        parts(pair, proj, held, sems, ((1, (l1, l2)), (2, (r2, r3))))

    return call(
        kernel,
        [array(PAIRS, G)] + [array(ROWS, K // 2)] * 4,
        2_500_000_000,
        12_000_000,
        in_specs=[WHOLE, WHOLE, HBM],
        scratch_shapes=[pltpu.VMEM((PAIRS, G), BF), pltpu.VMEM((PAIRS, G), BF)] + QUARTERS,
    )(recv, hot, proj)


def product_near(pair, proj):
    def kernel(pair, proj, l0, l3, r0, r1, turned, held, sems):
        fetch(proj, held, sems)
        turned[:ROWS, :] = pair[3 * ROWS :, :]
        turned[ROWS:, :] = pair[: 3 * ROWS, :]
        parts(turned, proj, held, sems, ((0, (l3, l0)), (1, (r0, r1))))

    return call(
        kernel,
        [array(ROWS, K // 2)] * 4,
        1_700_000_000,
        10_000_000,
        in_specs=[WHOLE, HBM],
        scratch_shapes=[pltpu.VMEM((PAIRS, G), BF)] + QUARTERS,
    )(pair, proj)


def add(a, b):
    return (a.astype(F32) + b.astype(F32)).astype(BF)


def shift(x, axis, size, by):
    return lax.ppermute(x, axis, [(i, (i + by) % size) for i in range(size)])


def across_x(recv, hot, proj):
    pair, l1, l2, r2, r3 = product_far(recv, hot, proj)
    far_l = shift(l2, "px", NX, 1)
    far_r = shift(r2, "px", NX, -1)
    l0, l3, r0, r1 = product_near(pair, proj)
    got_l = shift(l3, "px", NX, -1)
    got_r = shift(r1, "px", NX, 1)
    sum_l = shift(add(l1, far_l), "px", NX, 1)
    sum_r = shift(add(r3, far_r), "px", NX, -1)
    return l0, got_l, sum_l, r0, got_r, sum_r


def across_z(terms):
    def kernel(l0, l1, l2, r0, r1, r2, *outs):
        left = (l0[...].astype(F32) + l1[...].astype(F32) + l2[...].astype(F32)).astype(BF)
        right = (r0[...].astype(F32) + r1[...].astype(F32) + r2[...].astype(F32)).astype(BF)
        stacked = jnp.concatenate([left[:, :KV], left[:, KV:], right[:, :KV], right[:, KV:]], axis=0)
        r, c = iota((4 * ROWS, 4 * ROWS), 0), iota((4 * ROWS, 4 * ROWS), 1)
        block = r // 48
        quarter = (r - block * 48) // MINE
        item = r - block * 48 - quarter * MINE
        z = (block + lax.axis_index("pz")) & (NZ - 1)
        hot = ones_where(c == quarter * ROWS + z * MINE + item)
        rows = dot(hot, stacked).astype(BF)
        for k in range(NZ):
            outs[k][...] = rows[48 * k : 48 * k + 48, :]

    blocks = call(kernel, [array(48, KV)] * NZ, 300_000_000, 4_000_000)(*terms)
    return [blocks[0]] + [shift(blocks[k], "pz", NZ, k) for k in (4, 3, 5, 2, 6, 1, 7)]


def last_sum(parts):
    def kernel(*refs):
        out = refs[NZ]
        total = refs[0][...].astype(F32)
        for i in range(1, NZ):
            total = total + refs[i][...].astype(F32)
        for q in range(4):
            out[:, KV * q : KV * q + KV] = total[MINE * q : MINE * q + MINE, :]

    return call(kernel, array(MINE, K, dtype=F32), 1_000_000, 1_000_000)(*parts)


def local(q_fact, p_fact, q_cot, p_cot, passage_of, projection):
    recv = lax.all_to_all(grads(q_fact, p_fact, q_cot, p_cot), ("px", "pz"), 0, 0, tiled=True)
    proj, hot = prepared(projection, passage_of)
    return last_sum(across_z(across_x(recv, hot, proj)))


def solution(mesh):
    cut = Mesh(mesh.devices.reshape(mesh.shape["pairs"], NX, NZ), ("pairs", "px", "pz"))
    rows = P(("pairs", "px", "pz"), None)
    return jax.shard_map(
        local,
        mesh=cut,
        in_specs=(rows, rows, rows, rows, P("pairs"), P(("px", "pz"), None)),
        out_specs=rows,
        check_vma=False,
    )
```

time: 117 us -> 121 us (1.034)
  local copies, waits for them, and re-layouts: 3.39 us -> 10.1 us
  waiting for transfers between devices: 47.3 us -> 43.1 us
  Pallas kernels: 28.9 us -> 30.4 us
    unnamed x4 -> x8, local copies, waits for them, and re-layouts: 3.39 us -> 10 us
    all_to_all x1, waiting for transfers between devices: 23 us -> 16.4 us  [local(): lax.all_to_all(grads(q_fact, p_fact, q_cot, p_cot), ('px', 'pz'), 0, 0, t...]
    ppermute x13, waiting for transfers between devices: 24.4 us -> 26.7 us  [shift(): return lax.ppermute(x, axis, [(i, (i + by) % size) for i in range(size)])]
    pallas_call x4, Pallas kernels: 27.2 us -> 28.7 us  [the longest x1 13.9 us: prepared(): call(kernel, [array(G, K), array(PAIRS, PAIRS)], 2 * G * G * K, 16000000,...]
  transfers between devices with their start and end apart: 14 -> 14, of which waited for: 11 -> 9; matrix products, arithmetic and copies ran while one was open for 0% -> 0% of each run, Pallas kernels for 14% -> 15%
where the time goes in v4:
time: 121 us
  waiting for transfers between devices  43.1 us (36%)
  starting transfers between devices  37.2 us (31%)
  Pallas kernels  30.4 us (25%)
  local copies, waits for them, and re-layouts  10.1 us (8%)
    ppermute x13, waiting for transfers between devices, shift(): return lax.ppermute(x, axis, [(i, (i + by) % size) for i in range(size)])  26.7 us
    ppermute x13, starting transfers between devices, shift(): return lax.ppermute(x, axis, [(i, (i + by) % size) for i in range(size)])  25.5 us
    all_to_all x1, waiting for transfers between devices, local(): lax.all_to_all(grads(q_fact, p_fact, q_cot, p_cot), ('px', 'pz'), 0, 0, t...  16.4 us
    pallas_call x1, Pallas kernels, prepared(): call(kernel, [array(G, K), array(PAIRS, PAIRS)], 2 * G * G * K, 16000000,...  13.9 us
    all_to_all x1, starting transfers between devices, local(): lax.all_to_all(grads(q_fact, p_fact, q_cot, p_cot), ('px', 'pz'), 0, 0, t...  11.6 us
    unnamed x8, local copies, waits for them, and re-layouts  10 us
    pallas_call x1, Pallas kernels, grads(): call(kernel, array(N, 2 * ROWS, 128), 800000000, 5500000, vmem=60, in_spe...  5.65 us
    pallas_call x1, Pallas kernels, product_far(): call(kernel, [array(PAIRS, G)] + [array(ROWS, K // 2)] * 4, 2500000000, 1...  5.09 us
  transfers between devices with their start and end apart: 14, of which 9 were waited for; matrix products, arithmetic and copies ran while one was open for 0% of the time, Pallas kernels for 15%

profile of v4, /device:TPU:14, one launch (start us, length us, event | category | flops | bytes accessed | tf_op | source)
XLA Modules:
  0.0 121.1 jit_solution(2643857585066675855)
XLA Ops:
  0.0 5.6 %shard_map.64 = bf16[32,192,128]{2,1,0:T(8,128)(2,1)} custom-call(bf16[32,384]{1,0:T(8,128)(2,1)} %bitcast.3, bf16[32,576]{1,0:T(8,128)(2,1)} %bitcast.2, bf16[384,2048]{1,0:T(8,128)(2,1)} %q_cot.1, bf16[576,2048]{1,0:T(8,128)(2,1)} %p_cot.1), custom_call_target="tpu_custom_call" | custom-call | flops 800000000 | bytes 5500000 | tf_op jit(solution)/shard_map/pallas_call | solution.py:98
  5.7 0.0 copy-start.3
  5.7 11.6 %all-to-all-start = ((bf16[32,192,128]{2,1,0:T(8,128)(2,1)}), bf16[32,192,128]{2,1,0:T(8,128)(2,1)S(1)}, u32[]{:S(2)}, u32[]{:S(2)}) async-start(bf16[32,192,128]{2,1,0:T(8,128)(2,1)} %shard_map.64), calls=%async_computation | async-start | bytes 3145728 | tf_op jit(solution)/shard_map/all_to_all | solution.py:281
  17.3 0.0 copy-done.3
  17.3 0.1 reshape.4.passage
  17.4 0.0 copy-start.2
  17.4 3.4 %copy-done.2 = bf16[1024,4096]{1,0:T(8,128)(2,1)S(1)} copy-done((bf16[1024,4096]{1,0:T(8,128)(2,1)S(1)}, bf16[1024,4096]{1,0:T(8,128)(2,1)}, u32[]{:S(2)}) %copy-start.2) | copy-done | bytes 8388632
  20.8 13.9 %shard_map.65 = (bf16[1024,4096]{1,0:T(8,128)(2,1)S(1)}, bf16[384,384]{1,0:T(8,128)(2,1)S(1)}) custom-call(s32[384,1]{1,0:T(8,128)S(1)} %reshape.4.passage, bf16[1024,4096]{1,0:T(8,128)(2,1)S(1)} %copy-done.2), custom_call_target="tpu_custom_call" | custom-call | flops 8589934592 | bytes 16000000 | tf_op jit(solution)/shard_map/pallas_call | solution.py:139
  34.7 0.0 copy-start
  34.8 3.2 %copy-done = bf16[1024,4096]{1,0:T(8,128)(2,1)} copy-done((bf16[1024,4096]{1,0:T(8,128)(2,1)}, bf16[1024,4096]{1,0:T(8,128)(2,1)S(1)}, u32[]{:S(2)}) %copy-start) | copy-done | bytes 8388632
  38.0 16.4 %all-to-all-done.recv = bf16[32,192,128]{2,1,0:T(8,128)(2,1)S(1)} async-done(((bf16[32,192,128]{2,1,0:T(8,128)(2,1)}), bf16[32,192,128]{2,1,0:T(8,128)(2,1)S(1)}, u32[]{:S(2)}, u32[]{:S(2)}) %all-to-all-start) | async-done | bytes 1572896 | tf_op jit(solution)/shard_map/all_to_all | solution.py:281
  54.4 0.0 copy-start.1
  54.4 3.4 %copy-done.1 = bf16[1024,4096]{1,0:T(8,128)(2,1)S(1)} copy-done((bf16[1024,4096]{1,0:T(8,128)(2,1)S(1)}, bf16[1024,4096]{1,0:T(8,128)(2,1)}, u32[]{:S(2)}) %copy-start.1) | copy-done | bytes 8388632
  57.8 5.1 %shard_map.66 = (bf16[384,1024]{1,0:T(8,128)(2,1)S(1)}, bf16[96,2048]{1,0:T(8,128)(2,1)S(1)}, bf16[96,2048]{1,0:T(8,128)(2,1)S(1)}, bf16[96,2048]{1,0:T(8,128)(2,1)S(1)}, bf16[96,2048]{1,0:T(8,128)(2,1)S(1)}) custom-call(bf16[32,192,128]{2,1,0:T(8,128)(2,1)S(1)} %all-to-all-done.recv, bf16[384,384]{1,0:T(8,128)(2,1)S(1)} %get-tuple-element.24.hot, ...), custom_call_target="tpu_custom_call" | custom-call | flops 2500000000 | bytes 12000000 | tf_op jit(solution)/shard_map/pallas_call | solution.py:202
  62.9 2.8 %collective-permute-start.1 = (bf16[96,2048]{1,0:T(8,128)(2,1)S(1)}, bf16[96,2048]{1,0:T(8,128)(2,1)S(1)}, u32[]{:S(2)}, u32[]{:S(2)}) collective-permute-start(bf16[96,2048]{1,0:T(8,128)(2,1)S(1)} %get-tuple-element.30), channel_id=1, source_target_pairs={{0,8},{8,16},{16,24},{24,0},{1,9},{9,17},{17,25},{25,1},{2,10},{10... | collective-permute-start | bytes 1179656 | tf_op jit(solution)/shard_map/ppermute | solution.py:234
  65.6 4.0 %shard_map.67 = (bf16[96,2048]{1,0:T(8,128)(2,1)S(1)}, bf16[96,2048]{1,0:T(8,128)(2,1)S(1)}, bf16[96,2048]{1,0:T(8,128)(2,1)S(1)}, bf16[96,2048]{1,0:T(8,128)(2,1)S(1)}) custom-call(bf16[384,1024]{1,0:T(8,128)(2,1)S(1)} %get-tuple-element.26.pair, bf16[1024,4096]{1,0:T(8,128)(2,1)S(1)} %copy-done.1), custom_call_target="tpu_custom_call" | custom-call | flops 1700000000 | bytes 10000000 | tf_op jit(solution)/shard_map/pallas_call | solution.py:219
  69.6 0.1 collective-permute-start
  69.7 3.2 %collective-permute-start.3 = (bf16[96,2048]{1,0:T(8,128)(2,1)S(1)}, bf16[96,2048]{1,0:T(8,128)(2,1)S(1)}, u32[]{:S(2)}, u32[]{:S(2)}) collective-permute-start(bf16[96,2048]{1,0:T(8,128)(2,1)S(1)} %get-tuple-element.32), channel_id=1, source_target_pairs={{0,8},{8,16},{16,24},{24,0},{1,9},{9,17},{17,25},{25,1},{2,10},{10... | collective-permute-start | bytes 1179656 | tf_op jit(solution)/shard_map/ppermute | solution.py:234
  72.9 0.0 collective-permute-start.4
  72.9 1.0 collective-permute-done.1
  73.9 0.1 add_convert_fusion.1
  74.0 2.7 %collective-permute-start.2 = (bf16[96,2048]{1,0:T(8,128)(2,1)S(1)}, bf16[96,2048]{1,0:T(8,128)(2,1)S(1)}, u32[]{:S(2)}, u32[]{:S(2)}) collective-permute-start(bf16[96,2048]{1,0:T(8,128)(2,1)S(1)} %add_convert_fusion.1), channel_id=1, source_target_pairs={{0,8},{8,16},{16,24},{24,0},{1,9},{9,17},{17,25},{25,1},{2,10},{10... | collective-permute-start | bytes 1179656 | tf_op jit(solution)/shard_map/ppermute | solution.py:234
  76.7 10.6 %collective-permute-done.4 = bf16[96,2048]{1,0:T(8,128)(2,1)S(1)} collective-permute-done((bf16[96,2048]{1,0:T(8,128)(2,1)S(1)}, bf16[96,2048]{1,0:T(8,128)(2,1)S(1)}, u32[]{:S(2)}, u32[]{:S(2)}) %collective-permute-start.4) | collective-permute-done | bytes 393248 | tf_op jit(solution)/shard_map/ppermute | solution.py:234
  87.2 0.1 add_convert_fusion
  87.3 0.1 collective-permute-start.5
  87.4 0.0 collective-permute-done.l1
  87.4 0.0 collective-permute-done.3.r1
  87.4 1.0 collective-permute-done.2.l2
  88.4 8.0 %collective-permute-done.5.r2 = bf16[96,2048]{1,0:T(8,128)(2,1)S(1)} collective-permute-done((bf16[96,2048]{1,0:T(8,128)(2,1)S(1)}, bf16[96,2048]{1,0:T(8,128)(2,1)S(1)}, u32[]{:S(2)}, u32[]{:S(2)}) %collective-permute-start.5) | collective-permute-done | bytes 393248 | tf_op jit(solution)/shard_map/ppermute | solution.py:234
  96.4 0.9 shard_map.68
  97.3 5.6 %collective-permute-start.6 = (bf16[48,1024]{1,0:T(8,128)(2,1)S(1)}, bf16[48,1024]{1,0:T(8,128)(2,1)S(1)}, u32[]{:S(2)}, u32[]{:S(2)}) collective-permute-start(bf16[48,1024]{1,0:T(8,128)(2,1)S(1)} %get-tuple-element.36), channel_id=1, source_target_pairs={{0,4},{1,5},{2,6},{3,7},{4,0},{5,1},{6,2},{7,3},{8,12},{9,13},{10,... | collective-permute-start | bytes 294920 | tf_op jit(solution)/shard_map/ppermute | solution.py:234
  102.9 2.3 %collective-permute-start.7 = (bf16[48,1024]{1,0:T(8,128)(2,1)S(1)}, bf16[48,1024]{1,0:T(8,128)(2,1)S(1)}, u32[]{:S(2)}, u32[]{:S(2)}) collective-permute-start(bf16[48,1024]{1,0:T(8,128)(2,1)S(1)} %get-tuple-element.37), channel_id=1, source_target_pairs={{0,3},{1,4},{2,5},{3,6},{4,7},{5,0},{6,1},{7,2},{8,11},{9,12},{10,... | collective-permute-start | bytes 294920 | tf_op jit(solution)/shard_map/ppermute | solution.py:234
  105.2 2.7 %collective-permute-start.8 = (bf16[48,1024]{1,0:T(8,128)(2,1)S(1)}, bf16[48,1024]{1,0:T(8,128)(2,1)S(1)}, u32[]{:S(2)}, u32[]{:S(2)}) collective-permute-start(bf16[48,1024]{1,0:T(8,128)(2,1)S(1)} %get-tuple-element.38), channel_id=1, source_target_pairs={{0,5},{1,6},{2,7},{3,0},{4,1},{5,2},{6,3},{7,4},{8,13},{9,14},{10,... | collective-permute-start | bytes 294920 | tf_op jit(solution)/shard_map/ppermute | solution.py:234
  108.0 0.0 collective-permute-start.9
  108.0 4.1 %collective-permute-start.10 = (bf16[48,1024]{1,0:T(8,128)(2,1)S(1)}, bf16[48,1024]{1,0:T(8,128)(2,1)S(1)}, u32[]{:S(2)}, u32[]{:S(2)}) collective-permute-start(bf16[48,1024]{1,0:T(8,128)(2,1)S(1)} %get-tuple-element.40), channel_id=1, source_target_pairs={{0,6},{1,7},{2,0},{3,1},{4,2},{5,3},{6,4},{7,5},{8,14},{9,15},{10,... | collective-permute-start | bytes 294920 | tf_op jit(solution)/shard_map/ppermute | solution.py:234
  112.1 0.0 collective-permute-done.6.refs_1_
  112.1 1.8 %collective-permute-start.11 = (bf16[48,1024]{1,0:T(8,128)(2,1)S(1)}, bf16[48,1024]{1,0:T(8,128)(2,1)S(1)}, u32[]{:S(2)}, u32[]{:S(2)}) collective-permute-start(bf16[48,1024]{1,0:T(8,128)(2,1)S(1)} %get-tuple-element.41), channel_id=1, source_target_pairs={{0,1},{1,2},{2,3},{3,4},{4,5},{5,6},{6,7},{7,0},{8,9},{9,10},{10,1... | collective-permute-start | bytes 294920 | tf_op jit(solution)/shard_map/ppermute | solution.py:234
  113.9 1.3 %collective-permute-done.7.refs_2_ = bf16[48,1024]{1,0:T(8,128)(2,1)S(1)} collective-permute-done((bf16[48,1024]{1,0:T(8,128)(2,1)S(1)}, bf16[48,1024]{1,0:T(8,128)(2,1)S(1)}, u32[]{:S(2)}, u32[]{:S(2)}) %collective-permute-start.7) | collective-permute-done | bytes 98336 | tf_op jit(solution)/shard_map/ppermute | solution.py:234
  115.2 0.2 collective-permute-start.12
  115.3 0.0 collective-permute-done.8.refs_3_
  115.4 2.4 %collective-permute-done.9.refs_4_ = bf16[48,1024]{1,0:T(8,128)(2,1)S(1)} collective-permute-done((bf16[48,1024]{1,0:T(8,128)(2,1)S(1)}, bf16[48,1024]{1,0:T(8,128)(2,1)S(1)}, u32[]{:S(2)}, u32[]{:S(2)}) %collective-permute-start.9) | collective-permute-done | bytes 98336 | tf_op jit(solution)/shard_map/ppermute | solution.py:234
  117.7 1.2 collective-permute-done.10.refs_5_
  118.9 0.0 collective-permute-done.11.refs_6_
  118.9 1.4 %collective-permute-done.12.refs_7_ = bf16[48,1024]{1,0:T(8,128)(2,1)S(1)} collective-permute-done((bf16[48,1024]{1,0:T(8,128)(2,1)S(1)}, bf16[48,1024]{1,0:T(8,128)(2,1)S(1)}, u32[]{:S(2)}, u32[]{:S(2)}) %collective-permute-start.12) | collective-permute-done | bytes 98336 | tf_op jit(solution)/shard_map/ppermute | solution.py:234
  120.3 0.8 shard_map.69
Async XLA Ops:
  5.7 11.6 %copy-start.3 = (s32[384]{0:T(512)S(1)}, s32[384]{0:T(512)}, u32[]{:S(2)}) copy-start(s32[384]{0:T(512)} %param.10) | copy-start | bytes 4612
  5.7 48.7 %all-to-all-start = ((bf16[32,192,128]{2,1,0:T(8,128)(2,1)}), bf16[32,192,128]{2,1,0:T(8,128)(2,1)S(1)}, u32[]{:S(2)}, u32[]{:S(2)}) async-start(bf16[32,192,128]{2,1,0:T(8,128)(2,1)} %shard_map.64), calls=%async_computation | async-start | bytes 3145728 | tf_op jit(solution)/shard_map/all_to_all | solution.py:281
  17.4 3.4 %copy-start.2 = (bf16[1024,4096]{1,0:T(8,128)(2,1)S(1)}, bf16[1024,4096]{1,0:T(8,128)(2,1)}, u32[]{:S(2)}) copy-start(bf16[1024,4096]{1,0:T(8,128)(2,1)} %proj.1) | copy-start | bytes 25165828
  34.7 3.3 %copy-start = (bf16[1024,4096]{1,0:T(8,128)(2,1)}, bf16[1024,4096]{1,0:T(8,128)(2,1)S(1)}, u32[]{:S(2)}) copy-start(bf16[1024,4096]{1,0:T(8,128)(2,1)S(1)} %get-tuple-element.25.proj) | copy-start | bytes 25165828
  54.4 3.4 %copy-start.1 = (bf16[1024,4096]{1,0:T(8,128)(2,1)S(1)}, bf16[1024,4096]{1,0:T(8,128)(2,1)}, u32[]{:S(2)}) copy-start(bf16[1024,4096]{1,0:T(8,128)(2,1)} %copy-done) | copy-start | bytes 25165828
  62.9 11.0 %collective-permute-start.1 = (bf16[96,2048]{1,0:T(8,128)(2,1)S(1)}, bf16[96,2048]{1,0:T(8,128)(2,1)S(1)}, u32[]{:S(2)}, u32[]{:S(2)}) collective-permute-start(bf16[96,2048]{1,0:T(8,128)(2,1)S(1)} %get-tuple-element.30), channel_id=1, source_target_pairs={{0,8},{8,16},{16,24},{24,0},{1,9},{9,17},{17,25},{25,1},{2,10},{10... | collective-permute-start | bytes 1179656 | tf_op jit(solution)/shard_map/ppermute | solution.py:234
  69.6 17.8 %collective-permute-start = (bf16[96,2048]{1,0:T(8,128)(2,1)S(1)}, bf16[96,2048]{1,0:T(8,128)(2,1)S(1)}, u32[]{:S(2)}, u32[]{:S(2)}) collective-permute-start(bf16[96,2048]{1,0:T(8,128)(2,1)S(1)} %get-tuple-element.28), channel_id=1, source_target_pairs={{0,24},{8,0},{16,8},{24,16},{1,25},{9,1},{17,9},{25,17},{2,26},{10... | collective-permute-start | bytes 1179656 | tf_op jit(solution)/shard_map/ppermute | solution.py:234
  69.7 17.7 %collective-permute-start.3 = (bf16[96,2048]{1,0:T(8,128)(2,1)S(1)}, bf16[96,2048]{1,0:T(8,128)(2,1)S(1)}, u32[]{:S(2)}, u32[]{:S(2)}) collective-permute-start(bf16[96,2048]{1,0:T(8,128)(2,1)S(1)} %get-tuple-element.32), channel_id=1, source_target_pairs={{0,8},{8,16},{16,24},{24,0},{1,9},{9,17},{17,25},{25,1},{2,10},{10... | collective-permute-start | bytes 1179656 | tf_op jit(solution)/shard_map/ppermute | solution.py:234
  72.9 14.3 %collective-permute-start.4 = (bf16[96,2048]{1,0:T(8,128)(2,1)S(1)}, bf16[96,2048]{1,0:T(8,128)(2,1)S(1)}, u32[]{:S(2)}, u32[]{:S(2)}) collective-permute-start(bf16[96,2048]{1,0:T(8,128)(2,1)S(1)} %get-tuple-element.34), channel_id=1, source_target_pairs={{0,24},{8,0},{16,8},{24,16},{1,25},{9,1},{17,9},{25,17},{2,26},{10... | collective-permute-start | bytes 1179656 | tf_op jit(solution)/shard_map/ppermute | solution.py:234
  74.0 14.4 %collective-permute-start.2 = (bf16[96,2048]{1,0:T(8,128)(2,1)S(1)}, bf16[96,2048]{1,0:T(8,128)(2,1)S(1)}, u32[]{:S(2)}, u32[]{:S(2)}) collective-permute-start(bf16[96,2048]{1,0:T(8,128)(2,1)S(1)} %add_convert_fusion.1), channel_id=1, source_target_pairs={{0,8},{8,16},{16,24},{24,0},{1,9},{9,17},{17,25},{25,1},{2,10},{10... | collective-permute-start | bytes 1179656 | tf_op jit(solution)/shard_map/ppermute | solution.py:234
  87.3 9.1 %collective-permute-start.5 = (bf16[96,2048]{1,0:T(8,128)(2,1)S(1)}, bf16[96,2048]{1,0:T(8,128)(2,1)S(1)}, u32[]{:S(2)}, u32[]{:S(2)}) collective-permute-start(bf16[96,2048]{1,0:T(8,128)(2,1)S(1)} %add_convert_fusion), channel_id=1, source_target_pairs={{0,24},{8,0},{16,8},{24,16},{1,25},{9,1},{17,9},{25,17},{2,26},{10... | collective-permute-start | bytes 1179656 | tf_op jit(solution)/shard_map/ppermute | solution.py:234
  97.3 14.8 %collective-permute-start.6 = (bf16[48,1024]{1,0:T(8,128)(2,1)S(1)}, bf16[48,1024]{1,0:T(8,128)(2,1)S(1)}, u32[]{:S(2)}, u32[]{:S(2)}) collective-permute-start(bf16[48,1024]{1,0:T(8,128)(2,1)S(1)} %get-tuple-element.36), channel_id=1, source_target_pairs={{0,4},{1,5},{2,6},{3,7},{4,0},{5,1},{6,2},{7,3},{8,12},{9,13},{10,... | collective-permute-start | bytes 294920 | tf_op jit(solution)/shard_map/ppermute | solution.py:234
  102.9 12.2 %collective-permute-start.7 = (bf16[48,1024]{1,0:T(8,128)(2,1)S(1)}, bf16[48,1024]{1,0:T(8,128)(2,1)S(1)}, u32[]{:S(2)}, u32[]{:S(2)}) collective-permute-start(bf16[48,1024]{1,0:T(8,128)(2,1)S(1)} %get-tuple-element.37), channel_id=1, source_target_pairs={{0,3},{1,4},{2,5},{3,6},{4,7},{5,0},{6,1},{7,2},{8,11},{9,12},{10,... | collective-permute-start | bytes 294920 | tf_op jit(solution)/shard_map/ppermute | solution.py:234
  105.2 10.1 %collective-permute-start.8 = (bf16[48,1024]{1,0:T(8,128)(2,1)S(1)}, bf16[48,1024]{1,0:T(8,128)(2,1)S(1)}, u32[]{:S(2)}, u32[]{:S(2)}) collective-permute-start(bf16[48,1024]{1,0:T(8,128)(2,1)S(1)} %get-tuple-element.38), channel_id=1, source_target_pairs={{0,5},{1,6},{2,7},{3,0},{4,1},{5,2},{6,3},{7,4},{8,13},{9,14},{10,... | collective-permute-start | bytes 294920 | tf_op jit(solution)/shard_map/ppermute | solution.py:234
  108.0 9.8 %collective-permute-start.9 = (bf16[48,1024]{1,0:T(8,128)(2,1)S(1)}, bf16[48,1024]{1,0:T(8,128)(2,1)S(1)}, u32[]{:S(2)}, u32[]{:S(2)}) collective-permute-start(bf16[48,1024]{1,0:T(8,128)(2,1)S(1)} %get-tuple-element.39), channel_id=1, source_target_pairs={{0,2},{1,3},{2,4},{3,5},{4,6},{5,7},{6,0},{7,1},{8,10},{9,11},{10,... | collective-permute-start | bytes 294920 | tf_op jit(solution)/shard_map/ppermute | solution.py:234
  108.0 11.0 %collective-permute-start.10 = (bf16[48,1024]{1,0:T(8,128)(2,1)S(1)}, bf16[48,1024]{1,0:T(8,128)(2,1)S(1)}, u32[]{:S(2)}, u32[]{:S(2)}) collective-permute-start(bf16[48,1024]{1,0:T(8,128)(2,1)S(1)} %get-tuple-element.40), channel_id=1, source_target_pairs={{0,6},{1,7},{2,0},{3,1},{4,2},{5,3},{6,4},{7,5},{8,14},{9,15},{10,... | collective-permute-start | bytes 294920 | tf_op jit(solution)/shard_map/ppermute | solution.py:234
  112.1 6.8 %collective-permute-start.11 = (bf16[48,1024]{1,0:T(8,128)(2,1)S(1)}, bf16[48,1024]{1,0:T(8,128)(2,1)S(1)}, u32[]{:S(2)}, u32[]{:S(2)}) collective-permute-start(bf16[48,1024]{1,0:T(8,128)(2,1)S(1)} %get-tuple-element.41), channel_id=1, source_target_pairs={{0,1},{1,2},{2,3},{3,4},{4,5},{5,6},{6,7},{7,0},{8,9},{9,10},{10,1... | collective-permute-start | bytes 294920 | tf_op jit(solution)/shard_map/ppermute | solution.py:234
  115.2 5.1 %collective-permute-start.12 = (bf16[48,1024]{1,0:T(8,128)(2,1)S(1)}, bf16[48,1024]{1,0:T(8,128)(2,1)S(1)}, u32[]{:S(2)}, u32[]{:S(2)}) collective-permute-start(bf16[48,1024]{1,0:T(8,128)(2,1)S(1)} %get-tuple-element.42), channel_id=1, source_target_pairs={{0,7},{1,0},{2,1},{3,2},{4,3},{5,4},{6,5},{7,6},{8,15},{9,8},{10,9... | collective-permute-start | bytes 294920 | tf_op jit(solution)/shard_map/ppermute | solution.py:234

commit v5 on v3

--- a/solution.py
+++ b/solution.py
@@ -50,7 +50,7 @@
 
 
 def grads(q_fact, p_fact, q_cot, p_cot):
-    steps = 4
+    steps = 2
     cols = 2 * KV // steps
 
     def kernel(q_fact, p_fact, q_cot, p_cot, out, q_spread, p_spread):
@@ -98,27 +98,45 @@
     )(q_fact.T, p_fact.T, q_cot, p_cot)
 
 
-def permuted(projection):
-    def kernel(proj, out, order):
-        @pl.when(pl.program_id(0) == 0)
-        def _():
-            u, v = iota((G, G), 0), iota((G, G), 1)
-            order[...] = ones_where(v == (u & 63) * 16 + ((u >> 6) & 1) * 8 + (u >> 7))
-
-        out[...] = dot(order[...], proj[...]).astype(BF)
-
-    tile = pl.BlockSpec((G, 512), lambda n: (0, n))
+def prepared(projection, passage_of):
+    steps = 8
+    cols = K // steps
+
+    def kernel(passage, proj, out, hot, held, made, order, in_sems, out_sems):
+        def load(n):
+            return pltpu.make_async_copy(proj.at[:, pl.ds(cols * n, cols)], held.at[n], in_sems.at[n])
+
+        def store(n):
+            return pltpu.make_async_copy(made.at[n], out.at[:, pl.ds(cols * n, cols)], out_sems.at[n])
+
+        for n in range(steps):
+            load(n).start()
+        hot[...] = ones_where(iota((PAIRS, PAIRS), 1) == passage[...])
+        u, v = iota((G, G), 0), iota((G, G), 1)
+        order[...] = ones_where(v == (u & 63) * 16 + ((u >> 6) & 1) * 8 + (u >> 7))
+        for n in range(steps):
+            load(n).wait()
+            made[n] = dot(order[...], held[n]).astype(BF)
+            store(n).start()
+        for n in range(steps):
+            store(n).wait()
+
     return call(
         kernel,
-        array(G, K),
+        [array(G, K), array(PAIRS, PAIRS)],
         2 * G * G * K,
         16_000_000,
-        vmem=60,
-        grid=(K // 512,),
-        in_specs=[tile],
-        out_specs=tile,
-        scratch_shapes=[pltpu.VMEM((G, G), BF)],
-    )(projection)
+        vmem=57,
+        in_specs=[WHOLE, HBM],
+        out_specs=[HBM, WHOLE],
+        scratch_shapes=[
+            pltpu.VMEM((steps, G, cols), BF),
+            pltpu.VMEM((steps, G, cols), BF),
+            pltpu.VMEM((G, G), BF),
+            pltpu.SemaphoreType.DMA((steps,)),
+            pltpu.SemaphoreType.DMA((steps,)),
+        ],
+    )(passage_of.reshape(PAIRS, 1), projection)
 
 
 def rows_of(recv, kind, at, count):
@@ -131,16 +149,13 @@
     return jnp.concatenate(pieces, axis=0)
 
 
-def halves(pair, proj, outs):
-    part = dot(pair[...], proj[...]).astype(BF)
-    for d in range(NX):
-        outs[d][...] = part[ROWS * d : ROWS * d + ROWS, :]
-
-
-def product_left(recv, passage_of, proj):
-    def kernel(recv, passage, proj, pair, o0, o1, o2, o3, wide_q, wide_p, held, sem):
-        copy = pltpu.make_async_copy(proj.at[:, : K // 2], held, sem)
-        copy.start()
+def product(recv, hot, proj):
+    def kernel(recv, hot, proj, l0, l1, l2, l3, r0, r1, r2, r3, wide_q, wide_p, pair, held, sems):
+        def load(n):
+            return pltpu.make_async_copy(proj.at[:, pl.ds(KV * n, KV)], held.at[n], sems.at[n])
+
+        for n in range(4):
+            load(n).start()
         x = lax.axis_index("px")
         r, c = iota((256, 256), 0), iota((256, 256), 1)
         swap = ones_where(c == (r & 31) * 8 + (r >> 5))
@@ -150,51 +165,27 @@
             for b in range(8):
                 wide_q[32 * g : 32 * g + 32, 128 * b : 128 * b + 128] = mixed[32 * b : 32 * b + 32, :128]
                 wide_p[32 * g : 32 * g + 32, 128 * b : 128 * b + 128] = mixed[32 * b : 32 * b + 32, 128:]
-        hot = ones_where(iota((PAIRS, PAIRS), 0) == passage[...])
-        picked = lax.dot_general(hot, wide_p[...], (((0,), (0,)), ((), ())), preferred_element_type=F32)
-        summed = (wide_q[...].astype(F32) + picked).astype(BF)
+        summed = (wide_q[...].astype(F32) + dot(hot[...], wide_p[...])).astype(BF)
         for i in range(NX):
             at = pl.multiple_of(((i - x) & 3) * ROWS, 32)
             pair[pl.ds(at, ROWS), :] = summed[ROWS * i : ROWS * i + ROWS, :]
-        copy.wait()
-        halves(pair, held, (o0, o1, o2, o3))
+        for n in range(4):
+            load(n).wait()
+            part = dot(pair[...], held[n]).astype(BF)
+            at = KV * (n % 2)
+            for d, out in enumerate(((l0, l1, l2, l3), (r0, r1, r2, r3))[n // 2]):
+                out[:, at : at + KV] = part[ROWS * d : ROWS * d + ROWS, :]
 
     return call(
         kernel,
-        [array(PAIRS, G)] + [array(ROWS, K // 2)] * 4,
-        2_500_000_000,
-        8_000_000,
+        [array(ROWS, K // 2)] * 8,
+        4_000_000_000,
+        14_000_000,
+        vmem=57,
         in_specs=[WHOLE, WHOLE, HBM],
-        scratch_shapes=[
-            pltpu.VMEM((PAIRS, G), BF),
-            pltpu.VMEM((PAIRS, G), BF),
-            pltpu.VMEM((G, K // 2), BF),
-            pltpu.SemaphoreType.DMA,
-        ],
-    )(recv, passage_of.reshape(1, PAIRS), proj)
-
-
-def product_right(pair, proj):
-    def kernel(pair, proj, o0, o1, o2, o3, held, sems):
-        copies = []
-        for i in range(2):
-            at = pl.ds(K // 2 + KV * i, KV)
-            copies.append(pltpu.make_async_copy(proj.at[:, at], held.at[i], sems.at[i]))
-            copies[i].start()
-        for i in range(2):
-            copies[i].wait()
-            part = dot(pair[...], held[i]).astype(BF)
-            for d, out in enumerate((o0, o1, o2, o3)):
-                out[:, KV * i : KV * i + KV] = part[ROWS * d : ROWS * d + ROWS, :]
-
-    return call(
-        kernel,
-        [array(ROWS, K // 2)] * 4,
-        1_700_000_000,
-        7_000_000,
-        in_specs=[WHOLE, HBM],
-        scratch_shapes=[pltpu.VMEM((2, G, KV), BF), pltpu.SemaphoreType.DMA((2,))],
-    )(pair, proj)
+        scratch_shapes=[pltpu.VMEM((PAIRS, G), BF)] * 3
+        + [pltpu.VMEM((4, G, KV), BF), pltpu.SemaphoreType.DMA((4,))],
+    )(recv, hot, proj)
 
 
 def add(a, b):
@@ -205,12 +196,11 @@
     return lax.ppermute(x, axis, [(i, (i + by) % size) for i in range(size)])
 
 
-def across_x(left, right):
-    l0, l1, l2, l3 = left
-    r0, r1, r2, r3 = right
+def across_x(blocks):
+    l0, l1, l2, l3, r0, r1, r2, r3 = blocks
     far_l = shift(l2, "px", NX, 1)
+    far_r = shift(r2, "px", NX, -1)
     got_l = shift(l3, "px", NX, -1)
-    far_r = shift(r2, "px", NX, -1)
     got_r = shift(r1, "px", NX, 1)
     sum_l = shift(add(l1, far_l), "px", NX, 1)
     sum_r = shift(add(r3, far_r), "px", NX, -1)
@@ -250,9 +240,8 @@
 
 def local(q_fact, p_fact, q_cot, p_cot, passage_of, projection):
     recv = lax.all_to_all(grads(q_fact, p_fact, q_cot, p_cot), ("px", "pz"), 0, 0, tiled=True)
-    proj = permuted(projection)
-    pair, *left = product_left(recv, passage_of, proj)
-    return last_sum(across_z(across_x(left, product_right(pair, proj))))
+    proj, hot = prepared(projection, passage_of)
+    return last_sum(across_z(across_x(product(recv, hot, proj))))
 
 
 def solution(mesh):

time: 117 us -> 119 us (1.017)
  other arithmetic: 0.19 us -> 2.19 us
  starting transfers between devices: 36.5 us -> 38.2 us
  local copies, waits for them, and re-layouts: 3.39 us -> 2.02 us
    pallas_call x3 -> x2, Pallas kernels: 20.8 us -> 23.3 us  [the longest x1 14.1 us: prepared(): call(kernel, [array(G, K), array(PAIRS, PAIRS)], 2 * G * G * K, 16000000,...]
    unnamed x4 -> x8, local copies, waits for them, and re-layouts: 3.39 us -> 1.23 us
    convert_element_type x2, other arithmetic: 0.19 us -> 2.19 us  [add(): return (a.astype(F32) + b.astype(F32)).astype(BF)]
    pallas_call x1, Pallas kernels: 6.37 us -> 4.59 us  [grads(): call(kernel, array(N, 2 * ROWS, 128), 800000000, 5500000, vmem=60, grid=(...]
    ppermute x13, starting transfers between devices: 24.7 us -> 26.5 us  [shift(): return lax.ppermute(x, axis, [(i, (i + by) % size) for i in range(size)])]
  transfers between devices with their start and end apart: 14 -> 14, of which waited for: 11 -> 9; matrix products, arithmetic and copies ran while one was open for 0% -> 3% of each run, Pallas kernels for 14% -> 12%
where the time goes in v5:
time: 119 us
  waiting for transfers between devices  47.1 us (40%)
  starting transfers between devices  38.2 us (32%)
  Pallas kernels  29.6 us (25%)
  other arithmetic  2.19 us (2%)
  local copies, waits for them, and re-layouts  2.02 us (2%)
    ppermute x13, starting transfers between devices, shift(): return lax.ppermute(x, axis, [(i, (i + by) % size) for i in range(size)])  26.5 us
    ppermute x13, waiting for transfers between devices, shift(): return lax.ppermute(x, axis, [(i, (i + by) % size) for i in range(size)])  24.9 us
    all_to_all x1, waiting for transfers between devices, local(): lax.all_to_all(grads(q_fact, p_fact, q_cot, p_cot), ('px', 'pz'), 0, 0, t...  22.2 us
    pallas_call x1, Pallas kernels, prepared(): call(kernel, [array(G, K), array(PAIRS, PAIRS)], 2 * G * G * K, 16000000,...  14.1 us
    all_to_all x1, starting transfers between devices, local(): lax.all_to_all(grads(q_fact, p_fact, q_cot, p_cot), ('px', 'pz'), 0, 0, t...  11.7 us
    pallas_call x1, Pallas kernels, product(): call(kernel, [array(ROWS, K // 2)] * 8, 4000000000, 14000000, vmem=57, in...  9.2 us
    pallas_call x1, Pallas kernels, grads(): call(kernel, array(N, 2 * ROWS, 128), 800000000, 5500000, vmem=60, grid=(...  4.59 us
  transfers between devices with their start and end apart: 14, of which 9 were waited for; matrix products, arithmetic and copies ran while one was open for 3% of the time, Pallas kernels for 12%

profile of v5, /device:TPU:14, one launch (start us, length us, event | category | flops | bytes accessed | tf_op | source)
XLA Modules:
  0.0 119.2 jit_solution(3056784321386482326)
XLA Ops:
  0.0 4.6 %shard_map.64 = bf16[32,192,128]{2,1,0:T(8,128)(2,1)} custom-call(bf16[32,384]{1,0:T(8,128)(2,1)} %bitcast.3, bf16[32,576]{1,0:T(8,128)(2,1)} %bitcast.2, bf16[384,2048]{1,0:T(8,128)(2,1)} %q_cot.1, bf16[576,2048]{1,0:T(8,128)(2,1)} %p_cot.1), custom_call_target="tpu_custom_call" | custom-call | flops 800000000 | bytes 5500000 | tf_op jit(solution)/shard_map/pallas_call | solution.py:83
  4.6 0.0 copy-start.3
  4.6 11.7 %all-to-all-start = ((bf16[32,192,128]{2,1,0:T(8,128)(2,1)}), bf16[32,192,128]{2,1,0:T(8,128)(2,1)S(1)}, u32[]{:S(2)}, u32[]{:S(2)}) async-start(bf16[32,192,128]{2,1,0:T(8,128)(2,1)} %shard_map.64), calls=%async_computation | async-start | bytes 3145728 | tf_op jit(solution)/shard_map/all_to_all | solution.py:242
  16.3 0.0 copy-done.3
  16.3 0.8 reshape.4.passage
  17.1 14.1 %shard_map.65 = (bf16[1024,4096]{1,0:T(8,128)(2,1)}, bf16[384,384]{1,0:T(8,128)(2,1)}) custom-call(s32[384,1]{1,0:T(8,128)} %reshape.4.passage, bf16[1024,4096]{1,0:T(8,128)(2,1)} %proj.1), custom_call_target="tpu_custom_call" | custom-call | flops 8589934592 | bytes 16000000 | tf_op jit(solution)/shard_map/pallas_call | solution.py:124
  31.2 22.2 %all-to-all-done.recv = bf16[32,192,128]{2,1,0:T(8,128)(2,1)S(1)} async-done(((bf16[32,192,128]{2,1,0:T(8,128)(2,1)}), bf16[32,192,128]{2,1,0:T(8,128)(2,1)S(1)}, u32[]{:S(2)}, u32[]{:S(2)}) %all-to-all-start) | async-done | bytes 1572896 | tf_op jit(solution)/shard_map/all_to_all | solution.py:242
  53.4 0.0 copy-start.2
  53.4 1.2 %copy-done.2 = bf16[32,192,128]{2,1,0:T(8,128)(2,1)} copy-done((bf16[32,192,128]{2,1,0:T(8,128)(2,1)}, bf16[32,192,128]{2,1,0:T(8,128)(2,1)S(1)}, u32[]{:S(2)}) %copy-start.2) | copy-done | bytes 1572888
  54.6 9.2 %shard_map.66 = (bf16[96,2048]{1,0:T(8,128)(2,1)}, bf16[96,2048]{1,0:T(8,128)(2,1)}, bf16[96,2048]{1,0:T(8,128)(2,1)}, bf16[96,2048]{1,0:T(8,128)(2,1)}, bf16[96...) custom-call(bf16[32,192,128]{2,1,0:T(8,128)(2,1)} %copy-done.2, ...), custom_call_target="tpu_custom_call" | custom-call | flops 4000000000 | bytes 14000000 | tf_op jit(solution)/shard_map/pallas_call | solution.py:179
  63.8 0.0 copy-start
  63.9 0.0 copy-start.1
  63.9 2.5 %collective-permute-start.1 = (bf16[96,2048]{1,0:T(8,128)(2,1)}, bf16[96,2048]{1,0:T(8,128)(2,1)S(1)}, u32[]{:S(2)}, u32[]{:S(2)}) collective-permute-start(bf16[96,2048]{1,0:T(8,128)(2,1)} %get-tuple-element.28), channel_id=1, source_target_pairs={{0,8},{8,16},{16,24},{24,0},{1,9},{9,17},{17,25},{25,1},{2,10},{10... | collective-permute-start | bytes 1179656 | tf_op jit(solution)/shard_map/ppermute | solution.py:196
  66.4 0.0 collective-permute-start
  66.4 3.2 %collective-permute-start.3 = (bf16[96,2048]{1,0:T(8,128)(2,1)}, bf16[96,2048]{1,0:T(8,128)(2,1)S(1)}, u32[]{:S(2)}, u32[]{:S(2)}) collective-permute-start(bf16[96,2048]{1,0:T(8,128)(2,1)} %get-tuple-element.30), channel_id=1, source_target_pairs={{0,8},{8,16},{16,24},{24,0},{1,9},{9,17},{17,25},{25,1},{2,10},{10... | collective-permute-start | bytes 1179656 | tf_op jit(solution)/shard_map/ppermute | solution.py:196
  69.6 0.0 collective-permute-start.4
  69.6 6.6 %collective-permute-done.1 = bf16[96,2048]{1,0:T(8,128)(2,1)S(1)} collective-permute-done((bf16[96,2048]{1,0:T(8,128)(2,1)}, bf16[96,2048]{1,0:T(8,128)(2,1)S(1)}, u32[]{:S(2)}, u32[]{:S(2)}) %collective-permute-start.1) | collective-permute-done | bytes 393248 | tf_op jit(solution)/shard_map/ppermute | solution.py:196
  76.3 1.1 add_convert_fusion.1
  77.4 3.7 %collective-permute-start.2 = (bf16[96,2048]{1,0:T(8,128)(2,1)S(1)}, bf16[96,2048]{1,0:T(8,128)(2,1)S(1)}, u32[]{:S(2)}, u32[]{:S(2)}) collective-permute-start(bf16[96,2048]{1,0:T(8,128)(2,1)S(1)} %add_convert_fusion.1), channel_id=1, source_target_pairs={{0,8},{8,16},{16,24},{24,0},{1,9},{9,17},{17,25},{25,1},{2,10},{10... | collective-permute-start | bytes 1179656 | tf_op jit(solution)/shard_map/ppermute | solution.py:196
  81.0 3.0 %collective-permute-done.4 = bf16[96,2048]{1,0:T(8,128)(2,1)S(1)} collective-permute-done((bf16[96,2048]{1,0:T(8,128)(2,1)}, bf16[96,2048]{1,0:T(8,128)(2,1)S(1)}, u32[]{:S(2)}, u32[]{:S(2)}) %collective-permute-start.4) | collective-permute-done | bytes 393248 | tf_op jit(solution)/shard_map/ppermute | solution.py:196
  84.0 1.1 add_convert_fusion
  85.1 0.1 collective-permute-start.5
  85.2 0.0 collective-permute-done.l1
  85.2 0.0 collective-permute-done.3.r1
  85.2 4.1 %collective-permute-done.2.l2 = bf16[96,2048]{1,0:T(8,128)(2,1)S(1)} collective-permute-done((bf16[96,2048]{1,0:T(8,128)(2,1)S(1)}, bf16[96,2048]{1,0:T(8,128)(2,1)S(1)}, u32[]{:S(2)}, u32[]{:S(2)}) %collective-permute-start.2) | collective-permute-done | bytes 393248 | tf_op jit(solution)/shard_map/ppermute | solution.py:196
  89.4 4.8 %collective-permute-done.5.r2 = bf16[96,2048]{1,0:T(8,128)(2,1)S(1)} collective-permute-done((bf16[96,2048]{1,0:T(8,128)(2,1)S(1)}, bf16[96,2048]{1,0:T(8,128)(2,1)S(1)}, u32[]{:S(2)}, u32[]{:S(2)}) %collective-permute-start.5) | collective-permute-done | bytes 393248 | tf_op jit(solution)/shard_map/ppermute | solution.py:196
  94.2 0.0 copy-done
  94.2 0.0 copy-done.1
  94.2 0.9 shard_map.67
  95.1 5.8 %collective-permute-start.6 = (bf16[48,1024]{1,0:T(8,128)(2,1)S(1)}, bf16[48,1024]{1,0:T(8,128)(2,1)S(1)}, u32[]{:S(2)}, u32[]{:S(2)}) collective-permute-start(bf16[48,1024]{1,0:T(8,128)(2,1)S(1)} %get-tuple-element.34), channel_id=1, source_target_pairs={{0,4},{1,5},{2,6},{3,7},{4,0},{5,1},{6,2},{7,3},{8,12},{9,13},{10,... | collective-permute-start | bytes 294920 | tf_op jit(solution)/shard_map/ppermute | solution.py:196
  100.8 2.6 %collective-permute-start.7 = (bf16[48,1024]{1,0:T(8,128)(2,1)S(1)}, bf16[48,1024]{1,0:T(8,128)(2,1)S(1)}, u32[]{:S(2)}, u32[]{:S(2)}) collective-permute-start(bf16[48,1024]{1,0:T(8,128)(2,1)S(1)} %get-tuple-element.35), channel_id=1, source_target_pairs={{0,3},{1,4},{2,5},{3,6},{4,7},{5,0},{6,1},{7,2},{8,11},{9,12},{10,... | collective-permute-start | bytes 294920 | tf_op jit(solution)/shard_map/ppermute | solution.py:196
  103.4 2.4 %collective-permute-start.8 = (bf16[48,1024]{1,0:T(8,128)(2,1)S(1)}, bf16[48,1024]{1,0:T(8,128)(2,1)S(1)}, u32[]{:S(2)}, u32[]{:S(2)}) collective-permute-start(bf16[48,1024]{1,0:T(8,128)(2,1)S(1)} %get-tuple-element.36), channel_id=1, source_target_pairs={{0,5},{1,6},{2,7},{3,0},{4,1},{5,2},{6,3},{7,4},{8,13},{9,14},{10,... | collective-permute-start | bytes 294920 | tf_op jit(solution)/shard_map/ppermute | solution.py:196
  105.9 0.0 collective-permute-start.9
  105.9 4.1 %collective-permute-start.10 = (bf16[48,1024]{1,0:T(8,128)(2,1)S(1)}, bf16[48,1024]{1,0:T(8,128)(2,1)S(1)}, u32[]{:S(2)}, u32[]{:S(2)}) collective-permute-start(bf16[48,1024]{1,0:T(8,128)(2,1)S(1)} %get-tuple-element.38), channel_id=1, source_target_pairs={{0,6},{1,7},{2,0},{3,1},{4,2},{5,3},{6,4},{7,5},{8,14},{9,15},{10,... | collective-permute-start | bytes 294920 | tf_op jit(solution)/shard_map/ppermute | solution.py:196
  110.0 0.0 collective-permute-done.6.refs_1_
  110.0 2.0 %collective-permute-start.11 = (bf16[48,1024]{1,0:T(8,128)(2,1)S(1)}, bf16[48,1024]{1,0:T(8,128)(2,1)S(1)}, u32[]{:S(2)}, u32[]{:S(2)}) collective-permute-start(bf16[48,1024]{1,0:T(8,128)(2,1)S(1)} %get-tuple-element.39), channel_id=1, source_target_pairs={{0,1},{1,2},{2,3},{3,4},{4,5},{5,6},{6,7},{7,0},{8,9},{9,10},{10,1... | collective-permute-start | bytes 294920 | tf_op jit(solution)/shard_map/ppermute | solution.py:196
  112.0 1.3 %collective-permute-done.7.refs_2_ = bf16[48,1024]{1,0:T(8,128)(2,1)S(1)} collective-permute-done((bf16[48,1024]{1,0:T(8,128)(2,1)S(1)}, bf16[48,1024]{1,0:T(8,128)(2,1)S(1)}, u32[]{:S(2)}, u32[]{:S(2)}) %collective-permute-start.7) | collective-permute-done | bytes 98336 | tf_op jit(solution)/shard_map/ppermute | solution.py:196
  113.3 0.1 collective-permute-start.12
  113.3 0.0 collective-permute-done.8.refs_3_
  113.4 2.1 %collective-permute-done.9.refs_4_ = bf16[48,1024]{1,0:T(8,128)(2,1)S(1)} collective-permute-done((bf16[48,1024]{1,0:T(8,128)(2,1)S(1)}, bf16[48,1024]{1,0:T(8,128)(2,1)S(1)}, u32[]{:S(2)}, u32[]{:S(2)}) %collective-permute-start.9) | collective-permute-done | bytes 98336 | tf_op jit(solution)/shard_map/ppermute | solution.py:196
  115.5 1.5 %collective-permute-done.10.refs_5_ = bf16[48,1024]{1,0:T(8,128)(2,1)S(1)} collective-permute-done((bf16[48,1024]{1,0:T(8,128)(2,1)S(1)}, bf16[48,1024]{1,0:T(8,128)(2,1)S(1)}, u32[]{:S(2)}, u32[]{:S(2)}) %collective-permute-start.10) | collective-permute-done | bytes 98336 | tf_op jit(solution)/shard_map/ppermute | solution.py:196
  117.0 0.0 collective-permute-done.11.refs_6_
  117.1 1.3 %collective-permute-done.12.refs_7_ = bf16[48,1024]{1,0:T(8,128)(2,1)S(1)} collective-permute-done((bf16[48,1024]{1,0:T(8,128)(2,1)S(1)}, bf16[48,1024]{1,0:T(8,128)(2,1)S(1)}, u32[]{:S(2)}, u32[]{:S(2)}) %collective-permute-start.12) | collective-permute-done | bytes 98336 | tf_op jit(solution)/shard_map/ppermute | solution.py:196
  118.4 0.8 shard_map.68
Async XLA Ops:
  4.6 11.7 %copy-start.3 = (s32[384]{0:T(512)S(1)}, s32[384]{0:T(512)}, u32[]{:S(2)}) copy-start(s32[384]{0:T(512)} %param.10) | copy-start | bytes 4612
  4.6 48.8 %all-to-all-start = ((bf16[32,192,128]{2,1,0:T(8,128)(2,1)}), bf16[32,192,128]{2,1,0:T(8,128)(2,1)S(1)}, u32[]{:S(2)}, u32[]{:S(2)}) async-start(bf16[32,192,128]{2,1,0:T(8,128)(2,1)} %shard_map.64), calls=%async_computation | async-start | bytes 3145728 | tf_op jit(solution)/shard_map/all_to_all | solution.py:242
  53.4 1.2 %copy-start.2 = (bf16[32,192,128]{2,1,0:T(8,128)(2,1)}, bf16[32,192,128]{2,1,0:T(8,128)(2,1)S(1)}, u32[]{:S(2)}) copy-start(bf16[32,192,128]{2,1,0:T(8,128)(2,1)S(1)} %all-to-all-done.recv) | copy-start | bytes 4718596
  63.8 30.3 %copy-start = (bf16[96,2048]{1,0:T(8,128)(2,1)S(1)}, bf16[96,2048]{1,0:T(8,128)(2,1)}, u32[]{:S(2)}) copy-start(bf16[96,2048]{1,0:T(8,128)(2,1)} %get-tuple-element.25.l0) | copy-start | bytes 1179652
  63.9 30.3 %copy-start.1 = (bf16[96,2048]{1,0:T(8,128)(2,1)S(1)}, bf16[96,2048]{1,0:T(8,128)(2,1)}, u32[]{:S(2)}) copy-start(bf16[96,2048]{1,0:T(8,128)(2,1)} %get-tuple-element.29.r0) | copy-start | bytes 1179652
  63.9 12.4 %collective-permute-start.1 = (bf16[96,2048]{1,0:T(8,128)(2,1)}, bf16[96,2048]{1,0:T(8,128)(2,1)S(1)}, u32[]{:S(2)}, u32[]{:S(2)}) collective-permute-start(bf16[96,2048]{1,0:T(8,128)(2,1)} %get-tuple-element.28), channel_id=1, source_target_pairs={{0,8},{8,16},{16,24},{24,0},{1,9},{9,17},{17,25},{25,1},{2,10},{10... | collective-permute-start | bytes 1179656 | tf_op jit(solution)/shard_map/ppermute | solution.py:196
  66.4 18.8 %collective-permute-start = (bf16[96,2048]{1,0:T(8,128)(2,1)}, bf16[96,2048]{1,0:T(8,128)(2,1)S(1)}, u32[]{:S(2)}, u32[]{:S(2)}) collective-permute-start(bf16[96,2048]{1,0:T(8,128)(2,1)} %get-tuple-element.26), channel_id=1, source_target_pairs={{0,24},{8,0},{16,8},{24,16},{1,25},{9,1},{17,9},{25,17},{2,26},{10... | collective-permute-start | bytes 1179656 | tf_op jit(solution)/shard_map/ppermute | solution.py:196
  66.4 18.8 %collective-permute-start.3 = (bf16[96,2048]{1,0:T(8,128)(2,1)}, bf16[96,2048]{1,0:T(8,128)(2,1)S(1)}, u32[]{:S(2)}, u32[]{:S(2)}) collective-permute-start(bf16[96,2048]{1,0:T(8,128)(2,1)} %get-tuple-element.30), channel_id=1, source_target_pairs={{0,8},{8,16},{16,24},{24,0},{1,9},{9,17},{17,25},{25,1},{2,10},{10... | collective-permute-start | bytes 1179656 | tf_op jit(solution)/shard_map/ppermute | solution.py:196
  69.6 14.4 %collective-permute-start.4 = (bf16[96,2048]{1,0:T(8,128)(2,1)}, bf16[96,2048]{1,0:T(8,128)(2,1)S(1)}, u32[]{:S(2)}, u32[]{:S(2)}) collective-permute-start(bf16[96,2048]{1,0:T(8,128)(2,1)} %get-tuple-element.32), channel_id=1, source_target_pairs={{0,24},{8,0},{16,8},{24,16},{1,25},{9,1},{17,9},{25,17},{2,26},{10... | collective-permute-start | bytes 1179656 | tf_op jit(solution)/shard_map/ppermute | solution.py:196
  77.4 12.0 %collective-permute-start.2 = (bf16[96,2048]{1,0:T(8,128)(2,1)S(1)}, bf16[96,2048]{1,0:T(8,128)(2,1)S(1)}, u32[]{:S(2)}, u32[]{:S(2)}) collective-permute-start(bf16[96,2048]{1,0:T(8,128)(2,1)S(1)} %add_convert_fusion.1), channel_id=1, source_target_pairs={{0,8},{8,16},{16,24},{24,0},{1,9},{9,17},{17,25},{25,1},{2,10},{10... | collective-permute-start | bytes 1179656 | tf_op jit(solution)/shard_map/ppermute | solution.py:196
  85.1 9.1 %collective-permute-start.5 = (bf16[96,2048]{1,0:T(8,128)(2,1)S(1)}, bf16[96,2048]{1,0:T(8,128)(2,1)S(1)}, u32[]{:S(2)}, u32[]{:S(2)}) collective-permute-start(bf16[96,2048]{1,0:T(8,128)(2,1)S(1)} %add_convert_fusion), channel_id=1, source_target_pairs={{0,24},{8,0},{16,8},{24,16},{1,25},{9,1},{17,9},{25,17},{2,26},{10... | collective-permute-start | bytes 1179656 | tf_op jit(solution)/shard_map/ppermute | solution.py:196
  95.1 14.9 %collective-permute-start.6 = (bf16[48,1024]{1,0:T(8,128)(2,1)S(1)}, bf16[48,1024]{1,0:T(8,128)(2,1)S(1)}, u32[]{:S(2)}, u32[]{:S(2)}) collective-permute-start(bf16[48,1024]{1,0:T(8,128)(2,1)S(1)} %get-tuple-element.34), channel_id=1, source_target_pairs={{0,4},{1,5},{2,6},{3,7},{4,0},{5,1},{6,2},{7,3},{8,12},{9,13},{10,... | collective-permute-start | bytes 294920 | tf_op jit(solution)/shard_map/ppermute | solution.py:196
  100.8 12.4 %collective-permute-start.7 = (bf16[48,1024]{1,0:T(8,128)(2,1)S(1)}, bf16[48,1024]{1,0:T(8,128)(2,1)S(1)}, u32[]{:S(2)}, u32[]{:S(2)}) collective-permute-start(bf16[48,1024]{1,0:T(8,128)(2,1)S(1)} %get-tuple-element.35), channel_id=1, source_target_pairs={{0,3},{1,4},{2,5},{3,6},{4,7},{5,0},{6,1},{7,2},{8,11},{9,12},{10,... | collective-permute-start | bytes 294920 | tf_op jit(solution)/shard_map/ppermute | solution.py:196
  103.4 9.9 %collective-permute-start.8 = (bf16[48,1024]{1,0:T(8,128)(2,1)S(1)}, bf16[48,1024]{1,0:T(8,128)(2,1)S(1)}, u32[]{:S(2)}, u32[]{:S(2)}) collective-permute-start(bf16[48,1024]{1,0:T(8,128)(2,1)S(1)} %get-tuple-element.36), channel_id=1, source_target_pairs={{0,5},{1,6},{2,7},{3,0},{4,1},{5,2},{6,3},{7,4},{8,13},{9,14},{10,... | collective-permute-start | bytes 294920 | tf_op jit(solution)/shard_map/ppermute | solution.py:196
  105.9 9.6 %collective-permute-start.9 = (bf16[48,1024]{1,0:T(8,128)(2,1)S(1)}, bf16[48,1024]{1,0:T(8,128)(2,1)S(1)}, u32[]{:S(2)}, u32[]{:S(2)}) collective-permute-start(bf16[48,1024]{1,0:T(8,128)(2,1)S(1)} %get-tuple-element.37), channel_id=1, source_target_pairs={{0,2},{1,3},{2,4},{3,5},{4,6},{5,7},{6,0},{7,1},{8,10},{9,11},{10,... | collective-permute-start | bytes 294920 | tf_op jit(solution)/shard_map/ppermute | solution.py:196
  105.9 11.2 %collective-permute-start.10 = (bf16[48,1024]{1,0:T(8,128)(2,1)S(1)}, bf16[48,1024]{1,0:T(8,128)(2,1)S(1)}, u32[]{:S(2)}, u32[]{:S(2)}) collective-permute-start(bf16[48,1024]{1,0:T(8,128)(2,1)S(1)} %get-tuple-element.38), channel_id=1, source_target_pairs={{0,6},{1,7},{2,0},{3,1},{4,2},{5,3},{6,4},{7,5},{8,14},{9,15},{10,... | collective-permute-start | bytes 294920 | tf_op jit(solution)/shard_map/ppermute | solution.py:196
  110.0 7.0 %collective-permute-start.11 = (bf16[48,1024]{1,0:T(8,128)(2,1)S(1)}, bf16[48,1024]{1,0:T(8,128)(2,1)S(1)}, u32[]{:S(2)}, u32[]{:S(2)}) collective-permute-start(bf16[48,1024]{1,0:T(8,128)(2,1)S(1)} %get-tuple-element.39), channel_id=1, source_target_pairs={{0,1},{1,2},{2,3},{3,4},{4,5},{5,6},{6,7},{7,0},{8,9},{9,10},{10,1... | collective-permute-start | bytes 294920 | tf_op jit(solution)/shard_map/ppermute | solution.py:196
  113.3 5.1 %collective-permute-start.12 = (bf16[48,1024]{1,0:T(8,128)(2,1)S(1)}, bf16[48,1024]{1,0:T(8,128)(2,1)S(1)}, u32[]{:S(2)}, u32[]{:S(2)}) collective-permute-start(bf16[48,1024]{1,0:T(8,128)(2,1)S(1)} %get-tuple-element.40), channel_id=1, source_target_pairs={{0,7},{1,0},{2,1},{3,2},{4,3},{5,4},{6,5},{7,6},{8,15},{9,8},{10,9... | collective-permute-start | bytes 294920 | tf_op jit(solution)/shard_map/ppermute | solution.py:196

commit v6 on v5

--- a/solution.py
+++ b/solution.py
@@ -107,7 +107,7 @@
             return pltpu.make_async_copy(proj.at[:, pl.ds(cols * n, cols)], held.at[n], in_sems.at[n])
 
         def store(n):
-            return pltpu.make_async_copy(made.at[n], out.at[:, pl.ds(cols * n, cols)], out_sems.at[n])
+            return pltpu.make_async_copy(made.at[n], out.at[:G, pl.ds(cols * n, cols)], out_sems.at[n])
 
         for n in range(steps):
             load(n).start()
@@ -123,7 +123,7 @@
 
     return call(
         kernel,
-        [array(G, K), array(PAIRS, PAIRS)],
+        [array(3 * G, K), array(PAIRS, PAIRS)],
         2 * G * G * K,
         16_000_000,
         vmem=57,
@@ -149,13 +149,29 @@
     return jnp.concatenate(pieces, axis=0)
 
 
-def product(recv, hot, proj):
-    def kernel(recv, hot, proj, l0, l1, l2, l3, r0, r1, r2, r3, wide_q, wide_p, pair, held, sems):
-        def load(n):
-            return pltpu.make_async_copy(proj.at[:, pl.ds(KV * n, KV)], held.at[n], sems.at[n])
-
-        for n in range(4):
-            load(n).start()
+def fetch(proj, held, sems, first):
+    copies = []
+    for n in range(2):
+        at = pl.ds(KV * (first + n), KV)
+        copies.append(pltpu.make_async_copy(proj.at[:G, at], held.at[n], sems.at[n]))
+        copies[n].start()
+    return copies
+
+
+def products(pair, copies, held, outs):
+    for n in range(2):
+        copies[n].wait()
+        part = dot(pair[...], held[n]).astype(BF)
+        for d, out in enumerate(outs):
+            out[:, KV * n : KV * n + KV] = part[ROWS * d : ROWS * d + ROWS, :]
+
+
+HELD = [pltpu.VMEM((2, G, KV), BF), pltpu.SemaphoreType.DMA((2,))]
+
+
+def product_left(recv, hot, proj):
+    def kernel(recv, hot, proj, pair, o0, o1, o2, o3, wide_q, wide_p, held, sems):
+        copies = fetch(proj, held, sems, 0)
         x = lax.axis_index("px")
         r, c = iota((256, 256), 0), iota((256, 256), 1)
         swap = ones_where(c == (r & 31) * 8 + (r >> 5))
@@ -169,23 +185,32 @@
         for i in range(NX):
             at = pl.multiple_of(((i - x) & 3) * ROWS, 32)
             pair[pl.ds(at, ROWS), :] = summed[ROWS * i : ROWS * i + ROWS, :]
-        for n in range(4):
-            load(n).wait()
-            part = dot(pair[...], held[n]).astype(BF)
-            at = KV * (n % 2)
-            for d, out in enumerate(((l0, l1, l2, l3), (r0, r1, r2, r3))[n // 2]):
-                out[:, at : at + KV] = part[ROWS * d : ROWS * d + ROWS, :]
+        products(pair, copies, held, (o0, o1, o2, o3))
 
     return call(
         kernel,
-        [array(ROWS, K // 2)] * 8,
-        4_000_000_000,
-        14_000_000,
-        vmem=57,
+        [array(PAIRS, G)] + [array(ROWS, K // 2)] * 4,
+        2_500_000_000,
+        8_000_000,
+        vmem=44,
         in_specs=[WHOLE, WHOLE, HBM],
-        scratch_shapes=[pltpu.VMEM((PAIRS, G), BF)] * 3
-        + [pltpu.VMEM((4, G, KV), BF), pltpu.SemaphoreType.DMA((4,))],
+        scratch_shapes=[pltpu.VMEM((PAIRS, G), BF)] * 2 + HELD,
     )(recv, hot, proj)
+
+
+def product_right(pair, proj):
+    def kernel(pair, proj, o0, o1, o2, o3, held, sems):
+        products(pair, fetch(proj, held, sems, 2), held, (o0, o1, o2, o3))
+
+    return call(
+        kernel,
+        [array(ROWS, K // 2)] * 4,
+        1_700_000_000,
+        7_000_000,
+        vmem=44,
+        in_specs=[WHOLE, HBM],
+        scratch_shapes=HELD,
+    )(pair, proj)
 
 
 def add(a, b):
@@ -196,11 +221,12 @@
     return lax.ppermute(x, axis, [(i, (i + by) % size) for i in range(size)])
 
 
-def across_x(blocks):
-    l0, l1, l2, l3, r0, r1, r2, r3 = blocks
+def across_x(left, right):
+    l0, l1, l2, l3 = left
+    r0, r1, r2, r3 = right
     far_l = shift(l2, "px", NX, 1)
+    got_l = shift(l3, "px", NX, -1)
     far_r = shift(r2, "px", NX, -1)
-    got_l = shift(l3, "px", NX, -1)
     got_r = shift(r1, "px", NX, 1)
     sum_l = shift(add(l1, far_l), "px", NX, 1)
     sum_r = shift(add(r3, far_r), "px", NX, -1)
@@ -208,7 +234,7 @@
 
 
 def across_z(terms):
-    def kernel(l0, l1, l2, r0, r1, r2, *outs):
+    def kernel(l0, l1, l2, r0, r1, r2, far_up, far_down, own, up1, up2, down1, down2):
         left = (l0[...].astype(F32) + l1[...].astype(F32) + l2[...].astype(F32)).astype(BF)
         right = (r0[...].astype(F32) + r1[...].astype(F32) + r2[...].astype(F32)).astype(BF)
         stacked = jnp.concatenate([left[:, :KV], left[:, KV:], right[:, :KV], right[:, KV:]], axis=0)
@@ -219,19 +245,48 @@
         z = (block + lax.axis_index("pz")) & (NZ - 1)
         hot = ones_where(c == quarter * ROWS + z * MINE + item)
         rows = dot(hot, stacked).astype(BF)
-        for k in range(NZ):
-            outs[k][...] = rows[48 * k : 48 * k + 48, :]
-
-    blocks = call(kernel, [array(48, KV)] * NZ, 300_000_000, 4_000_000)(*terms)
-    return [blocks[0]] + [shift(blocks[k], "pz", NZ, k) for k in (4, 3, 5, 2, 6, 1, 7)]
+        for k, out in ((0, own), (1, up1), (2, up2), (6, down2), (7, down1)):
+            out[...] = rows[48 * k : 48 * k + 48, :]
+        half = KV // 2
+        far_up[0] = rows[48 * 3 : 48 * 4, :half]
+        far_up[1] = rows[48 * 3 : 48 * 4, half:]
+        far_up[2] = rows[48 * 4 : 48 * 5, :half]
+        far_down[0] = rows[48 * 5 : 48 * 6, :half]
+        far_down[1] = rows[48 * 5 : 48 * 6, half:]
+        far_down[2] = rows[48 * 4 : 48 * 5, half:]
+
+    outs = [array(3, 48, KV // 2)] * 2 + [array(48, KV)] * 5
+    far_up, far_down, *near = call(kernel, outs, 300_000_000, 4_000_000)(*terms)
+    far_up = shift(far_up, "pz", NZ, 2)
+    far_down = shift(far_down, "pz", NZ, -2)
+
+    def add_kernel(far_up, far_down, up1, up2, down1, down2, *outs):
+        half = KV // 2
+        for far, near1, near2, out1, out2, side in (
+            (far_up, up1, up2, outs[0], outs[1], 0),
+            (far_down, down1, down2, outs[2], outs[3], 1),
+        ):
+            out1[:, :half] = add(near1[:, :half], far[0])
+            out1[:, half:] = add(near1[:, half:], far[1])
+            for i in range(2):
+                at = slice(half * i, half * i + half)
+                out2[:, at] = add(near2[:, at], far[2]) if i == side else near2[:, at]
+
+    own, *near = near
+    up1, up2, down1, down2 = call(add_kernel, [array(48, KV)] * 4, 1_000_000, 1_000_000)(far_up, far_down, *near)
+    up2 = shift(up2, "pz", NZ, 2)
+    down2 = shift(down2, "pz", NZ, -2)
+    up1 = shift(up1, "pz", NZ, 1)
+    down1 = shift(down1, "pz", NZ, -1)
+    return own, up1, up2, down1, down2
 
 
 def last_sum(parts):
     def kernel(*refs):
-        out = refs[NZ]
-        total = refs[0][...].astype(F32)
-        for i in range(1, NZ):
-            total = total + refs[i][...].astype(F32)
+        *terms, out = refs
+        total = terms[0][...].astype(F32)
+        for term in terms[1:]:
+            total = total + term[...].astype(F32)
         for q in range(4):
             out[:, KV * q : KV * q + KV] = total[MINE * q : MINE * q + MINE, :]
 
@@ -241,7 +296,8 @@
 def local(q_fact, p_fact, q_cot, p_cot, passage_of, projection):
     recv = lax.all_to_all(grads(q_fact, p_fact, q_cot, p_cot), ("px", "pz"), 0, 0, tiled=True)
     proj, hot = prepared(projection, passage_of)
-    return last_sum(across_z(across_x(product(recv, hot, proj))))
+    pair, *left = product_left(recv, hot, proj)
+    return last_sum(across_z(across_x(left, product_right(pair, proj))))
 
 
 def solution(mesh):

time: 119 us -> 115 us (0.966)
  starting transfers between devices: 38.2 us -> 34.5 us
  waiting for transfers between devices: 47.1 us -> 49.8 us
  other arithmetic: 2.19 us -> 0.19 us
    ppermute x13 -> x12, starting transfers between devices: 26.5 us -> 22.8 us  [shift(): return lax.ppermute(x, axis, [(i, (i + by) % size) for i in range(size)])]
    ppermute x13 -> x12, waiting for transfers between devices: 24.9 us -> 27.6 us  [shift(): return lax.ppermute(x, axis, [(i, (i + by) % size) for i in range(size)])]
    convert_element_type x2, other arithmetic: 2.19 us -> 0.19 us  [add(): return (a.astype(F32) + b.astype(F32)).astype(BF)]
    pallas_call x3 -> x5, Pallas kernels: 24.2 us -> 23.2 us  [the longest x1 14 us: prepared(): call(kernel, [array(3 * G, K), array(PAIRS, PAIRS)], 2 * G * G * K, 16000...]
  transfers between devices with their start and end apart: 14 -> 13, of which waited for: 9 -> 10; matrix products, arithmetic and copies ran while one was open for 3% -> 1% of each run, Pallas kernels for 12% -> 15%
where the time goes in v6:
time: 115 us
  waiting for transfers between devices  49.8 us (43%)
  starting transfers between devices  34.5 us (30%)
  Pallas kernels  28.6 us (25%)
  local copies, waits for them, and re-layouts  1.76 us (2%)
    ppermute x12, waiting for transfers between devices, shift(): return lax.ppermute(x, axis, [(i, (i + by) % size) for i in range(size)])  27.6 us
    ppermute x12, starting transfers between devices, shift(): return lax.ppermute(x, axis, [(i, (i + by) % size) for i in range(size)])  22.8 us
    all_to_all x1, waiting for transfers between devices, local(): lax.all_to_all(grads(q_fact, p_fact, q_cot, p_cot), ('px', 'pz'), 0, 0, t...  22.2 us
    pallas_call x1, Pallas kernels, prepared(): call(kernel, [array(3 * G, K), array(PAIRS, PAIRS)], 2 * G * G * K, 16000...  14 us
    all_to_all x1, starting transfers between devices, local(): lax.all_to_all(grads(q_fact, p_fact, q_cot, p_cot), ('px', 'pz'), 0, 0, t...  11.7 us
    pallas_call x1, Pallas kernels, product_left(): call(kernel, [array(PAIRS, G)] + [array(ROWS, K // 2)] * 4, 2500000000, 8...  4.6 us
    pallas_call x1, Pallas kernels, grads(): call(kernel, array(N, 2 * ROWS, 128), 800000000, 5500000, vmem=60, grid=(...  4.59 us
    pallas_call x1, Pallas kernels, product_right(): call(kernel, [array(ROWS, K // 2)] * 4, 1700000000, 7000000, vmem=44, in_...  3.57 us
  transfers between devices with their start and end apart: 13, of which 10 were waited for; matrix products, arithmetic and copies ran while one was open for 1% of the time, Pallas kernels for 15%

profile of v6, /device:TPU:14, one launch (start us, length us, event | category | flops | bytes accessed | tf_op | source)
XLA Modules:
  0.0 114.9 jit_solution(4088641139245964613)
XLA Ops:
  0.0 4.6 %shard_map.64 = bf16[32,192,128]{2,1,0:T(8,128)(2,1)} custom-call(bf16[32,384]{1,0:T(8,128)(2,1)} %bitcast.3, bf16[32,576]{1,0:T(8,128)(2,1)} %bitcast.2, bf16[384,2048]{1,0:T(8,128)(2,1)} %q_cot.1, bf16[576,2048]{1,0:T(8,128)(2,1)} %p_cot.1), custom_call_target="tpu_custom_call" | custom-call | flops 800000000 | bytes 5500000 | tf_op jit(solution)/shard_map/pallas_call | solution.py:83
  4.6 0.0 copy-start.1
  4.6 11.7 %all-to-all-start = ((bf16[32,192,128]{2,1,0:T(8,128)(2,1)}), bf16[32,192,128]{2,1,0:T(8,128)(2,1)S(1)}, u32[]{:S(2)}, u32[]{:S(2)}) async-start(bf16[32,192,128]{2,1,0:T(8,128)(2,1)} %shard_map.64), calls=%async_computation | async-start | bytes 3145728 | tf_op jit(solution)/shard_map/all_to_all | solution.py:297
  16.3 0.0 copy-done.1
  16.3 0.8 reshape.4.passage
  17.1 14.0 %shard_map.65 = (bf16[3072,4096]{1,0:T(8,128)(2,1)}, bf16[384,384]{1,0:T(8,128)(2,1)}) custom-call(s32[384,1]{1,0:T(8,128)} %reshape.4.passage, bf16[1024,4096]{1,0:T(8,128)(2,1)} %proj.1), custom_call_target="tpu_custom_call" | custom-call | flops 8589934592 | bytes 16000000 | tf_op jit(solution)/shard_map/pallas_call | solution.py:124
  31.2 22.2 %all-to-all-done.recv = bf16[32,192,128]{2,1,0:T(8,128)(2,1)S(1)} async-done(((bf16[32,192,128]{2,1,0:T(8,128)(2,1)}), bf16[32,192,128]{2,1,0:T(8,128)(2,1)S(1)}, u32[]{:S(2)}, u32[]{:S(2)}) %all-to-all-start) | async-done | bytes 1572896 | tf_op jit(solution)/shard_map/all_to_all | solution.py:297
  53.4 0.0 copy-start
  53.4 1.0 copy-done
  54.4 4.6 %shard_map.66 = (bf16[384,1024]{1,0:T(8,128)(2,1)S(1)}, bf16[96,2048]{1,0:T(8,128)(2,1)S(1)}, bf16[96,2048]{1,0:T(8,128)(2,1)S(1)}, bf16[96,2048]{1,0:T(8,128)(2,1)S(1)}, bf16[96,2048]{1,0:T(8,128)(2,1)S(1)}) custom-call(bf16[32,192,128]{2,1,0:T(8,128)(2,1)S(1)} %all-to-all-done.recv, bf16[384,384]{1,0:T(8,128)(2,1)S(1)} %copy-done, ...), custom_call_target="tpu_custom_call" | custom-call | flops 2500000000 | bytes 8000000 | tf_op jit(solution)/shard_map/pallas_call | solution.py:190
  59.0 2.5 %collective-permute-start.1 = (bf16[96,2048]{1,0:T(8,128)(2,1)S(1)}, bf16[96,2048]{1,0:T(8,128)(2,1)S(1)}, u32[]{:S(2)}, u32[]{:S(2)}) collective-permute-start(bf16[96,2048]{1,0:T(8,128)(2,1)S(1)} %get-tuple-element.32), channel_id=1, source_target_pairs={{0,8},{8,16},{16,24},{24,0},{1,9},{9,17},{17,25},{25,1},{2,10},{10... | collective-permute-start | bytes 1179656 | tf_op jit(solution)/shard_map/ppermute | solution.py:221
  61.5 0.0 collective-permute-start
  61.5 3.6 %shard_map.67 = (bf16[96,2048]{1,0:T(8,128)(2,1)S(1)}, bf16[96,2048]{1,0:T(8,128)(2,1)S(1)}, bf16[96,2048]{1,0:T(8,128)(2,1)S(1)}, bf16[96,2048]{1,0:T(8,128)(2,1)S(1)}) custom-call(bf16[384,1024]{1,0:T(8,128)(2,1)S(1)} %get-tuple-element.33.pair, bf16[3072,4096]{1,0:T(8,128)(2,1)} %get-tuple-element.28.proj), custom_call_target="tpu_custom_call" | custom-call | flops 1700000000 | bytes 7000000 | tf_op jit(solution)/shard_map/pallas_call | solution.py:205
  65.1 3.3 %collective-permute-start.3 = (bf16[96,2048]{1,0:T(8,128)(2,1)S(1)}, bf16[96,2048]{1,0:T(8,128)(2,1)S(1)}, u32[]{:S(2)}, u32[]{:S(2)}) collective-permute-start(bf16[96,2048]{1,0:T(8,128)(2,1)S(1)} %get-tuple-element.35), channel_id=1, source_target_pairs={{0,8},{8,16},{16,24},{24,0},{1,9},{9,17},{17,25},{25,1},{2,10},{10... | collective-permute-start | bytes 1179656 | tf_op jit(solution)/shard_map/ppermute | solution.py:221
  68.4 0.0 collective-permute-start.4
  68.4 1.9 %collective-permute-done.1 = bf16[96,2048]{1,0:T(8,128)(2,1)S(1)} collective-permute-done((bf16[96,2048]{1,0:T(8,128)(2,1)S(1)}, bf16[96,2048]{1,0:T(8,128)(2,1)S(1)}, u32[]{:S(2)}, u32[]{:S(2)}) %collective-permute-start.1) | collective-permute-done | bytes 393248 | tf_op jit(solution)/shard_map/ppermute | solution.py:221
  70.3 0.1 add_convert_fusion.1
  70.4 2.6 %collective-permute-start.2 = (bf16[96,2048]{1,0:T(8,128)(2,1)S(1)}, bf16[96,2048]{1,0:T(8,128)(2,1)S(1)}, u32[]{:S(2)}, u32[]{:S(2)}) collective-permute-start(bf16[96,2048]{1,0:T(8,128)(2,1)S(1)} %add_convert_fusion.1), channel_id=1, source_target_pairs={{0,8},{8,16},{16,24},{24,0},{1,9},{9,17},{17,25},{25,1},{2,10},{10... | collective-permute-start | bytes 1179656 | tf_op jit(solution)/shard_map/ppermute | solution.py:221
  73.0 6.0 %collective-permute-done.4 = bf16[96,2048]{1,0:T(8,128)(2,1)S(1)} collective-permute-done((bf16[96,2048]{1,0:T(8,128)(2,1)S(1)}, bf16[96,2048]{1,0:T(8,128)(2,1)S(1)}, u32[]{:S(2)}, u32[]{:S(2)}) %collective-permute-start.4) | collective-permute-done | bytes 393248 | tf_op jit(solution)/shard_map/ppermute | solution.py:221
  78.9 0.1 add_convert_fusion
  79.0 0.1 collective-permute-start.5
  79.1 0.0 collective-permute-done.l1
  79.1 0.0 collective-permute-done.3.r1
  79.1 5.1 %collective-permute-done.2.l2 = bf16[96,2048]{1,0:T(8,128)(2,1)S(1)} collective-permute-done((bf16[96,2048]{1,0:T(8,128)(2,1)S(1)}, bf16[96,2048]{1,0:T(8,128)(2,1)S(1)}, u32[]{:S(2)}, u32[]{:S(2)}) %collective-permute-start.2) | collective-permute-done | bytes 393248 | tf_op jit(solution)/shard_map/ppermute | solution.py:221
  84.3 4.4 %collective-permute-done.5.r2 = bf16[96,2048]{1,0:T(8,128)(2,1)S(1)} collective-permute-done((bf16[96,2048]{1,0:T(8,128)(2,1)S(1)}, bf16[96,2048]{1,0:T(8,128)(2,1)S(1)}, u32[]{:S(2)}, u32[]{:S(2)}) %collective-permute-start.5) | collective-permute-done | bytes 393248 | tf_op jit(solution)/shard_map/ppermute | solution.py:221
  88.7 0.9 shard_map.68
  89.6 1.7 %collective-permute-start.6 = (bf16[3,48,512]{2,1,0:T(8,128)(2,1)S(1)}, bf16[3,48,512]{2,1,0:T(8,128)(2,1)S(1)}, u32[]{:S(2)}, u32[]{:S(2)}) collective-permute-start(bf16[3,48,512]{2,1,0:T(8,128)(2,1)S(1)} %get-tuple-element.39), channel_id=1, source_target_pairs={{0,2},{1,3},{2,4},{3,5},{4,6},{5,7},{6,0},{7,1},{8,10},{9,11},{10,... | collective-permute-start | bytes 442376 | tf_op jit(solution)/shard_map/ppermute | solution.py:221
  91.3 2.5 %collective-permute-start.7 = (bf16[3,48,512]{2,1,0:T(8,128)(2,1)S(1)}, bf16[3,48,512]{2,1,0:T(8,128)(2,1)S(1)}, u32[]{:S(2)}, u32[]{:S(2)}) collective-permute-start(bf16[3,48,512]{2,1,0:T(8,128)(2,1)S(1)} %get-tuple-element.40), channel_id=1, source_target_pairs={{0,6},{1,7},{2,0},{3,1},{4,2},{5,3},{6,4},{7,5},{8,14},{9,15},{10,... | collective-permute-start | bytes 442376 | tf_op jit(solution)/shard_map/ppermute | solution.py:221
  93.8 4.2 %collective-permute-done.6.far_up = bf16[3,48,512]{2,1,0:T(8,128)(2,1)S(1)} collective-permute-done((bf16[3,48,512]{2,1,0:T(8,128)(2,1)S(1)}, bf16[3,48,512]{2,1,0:T(8,128)(2,1)S(1)}, u32[]{:S(2)}, u32[]{:S(2)}) %collective-permute-start.6) | collective-permute-done | bytes 147488 | tf_op jit(solution)/shard_map/ppermute | solution.py:221
  98.0 0.5 collective-permute-done.7.far_down
  98.5 0.1 shard_map.69
  98.6 2.6 %collective-permute-start.8 = (bf16[48,1024]{1,0:T(8,128)(2,1)S(1)}, bf16[48,1024]{1,0:T(8,128)(2,1)S(1)}, u32[]{:S(2)}, u32[]{:S(2)}) collective-permute-start(bf16[48,1024]{1,0:T(8,128)(2,1)S(1)} %get-tuple-element.45), channel_id=1, source_target_pairs={{0,1},{1,2},{2,3},{3,4},{4,5},{5,6},{6,7},{7,0},{8,9},{9,10},{10,1... | collective-permute-start | bytes 294920 | tf_op jit(solution)/shard_map/ppermute | solution.py:221
  101.2 4.3 %collective-permute-start.9 = (bf16[48,1024]{1,0:T(8,128)(2,1)S(1)}, bf16[48,1024]{1,0:T(8,128)(2,1)S(1)}, u32[]{:S(2)}, u32[]{:S(2)}) collective-permute-start(bf16[48,1024]{1,0:T(8,128)(2,1)S(1)} %get-tuple-element.46), channel_id=1, source_target_pairs={{0,2},{1,3},{2,4},{3,5},{4,6},{5,7},{6,0},{7,1},{8,10},{9,11},{10,... | collective-permute-start | bytes 294920 | tf_op jit(solution)/shard_map/ppermute | solution.py:221
  105.5 3.1 %collective-permute-start.10 = (bf16[48,1024]{1,0:T(8,128)(2,1)S(1)}, bf16[48,1024]{1,0:T(8,128)(2,1)S(1)}, u32[]{:S(2)}, u32[]{:S(2)}) collective-permute-start(bf16[48,1024]{1,0:T(8,128)(2,1)S(1)} %get-tuple-element.47), channel_id=1, source_target_pairs={{0,7},{1,0},{2,1},{3,2},{4,3},{5,4},{6,5},{7,6},{8,15},{9,8},{10,9... | collective-permute-start | bytes 294920 | tf_op jit(solution)/shard_map/ppermute | solution.py:221
  108.6 0.0 collective-permute-start.11
  108.7 0.0 collective-permute-done.8.refs_1_
  108.7 1.4 %collective-permute-done.9.refs_2_ = bf16[48,1024]{1,0:T(8,128)(2,1)S(1)} collective-permute-done((bf16[48,1024]{1,0:T(8,128)(2,1)S(1)}, bf16[48,1024]{1,0:T(8,128)(2,1)S(1)}, u32[]{:S(2)}, u32[]{:S(2)}) %collective-permute-start.9) | collective-permute-done | bytes 98336 | tf_op jit(solution)/shard_map/ppermute | solution.py:221
  110.1 0.8 collective-permute-done.10.refs_3_
  110.9 3.3 %collective-permute-done.11.refs_4_ = bf16[48,1024]{1,0:T(8,128)(2,1)S(1)} collective-permute-done((bf16[48,1024]{1,0:T(8,128)(2,1)S(1)}, bf16[48,1024]{1,0:T(8,128)(2,1)S(1)}, u32[]{:S(2)}, u32[]{:S(2)}) %collective-permute-start.11) | collective-permute-done | bytes 98336 | tf_op jit(solution)/shard_map/ppermute | solution.py:221
  114.2 0.8 shard_map.70
Async XLA Ops:
  4.6 11.7 %copy-start.1 = (s32[384]{0:T(512)S(1)}, s32[384]{0:T(512)}, u32[]{:S(2)}) copy-start(s32[384]{0:T(512)} %param.10) | copy-start | bytes 4612
  4.6 48.8 %all-to-all-start = ((bf16[32,192,128]{2,1,0:T(8,128)(2,1)}), bf16[32,192,128]{2,1,0:T(8,128)(2,1)S(1)}, u32[]{:S(2)}, u32[]{:S(2)}) async-start(bf16[32,192,128]{2,1,0:T(8,128)(2,1)} %shard_map.64), calls=%async_computation | async-start | bytes 3145728 | tf_op jit(solution)/shard_map/all_to_all | solution.py:297
  53.4 1.0 copy-start
  59.0 11.3 %collective-permute-start.1 = (bf16[96,2048]{1,0:T(8,128)(2,1)S(1)}, bf16[96,2048]{1,0:T(8,128)(2,1)S(1)}, u32[]{:S(2)}, u32[]{:S(2)}) collective-permute-start(bf16[96,2048]{1,0:T(8,128)(2,1)S(1)} %get-tuple-element.32), channel_id=1, source_target_pairs={{0,8},{8,16},{16,24},{24,0},{1,9},{9,17},{17,25},{25,1},{2,10},{10... | collective-permute-start | bytes 1179656 | tf_op jit(solution)/shard_map/ppermute | solution.py:221
  61.5 17.6 %collective-permute-start = (bf16[96,2048]{1,0:T(8,128)(2,1)S(1)}, bf16[96,2048]{1,0:T(8,128)(2,1)S(1)}, u32[]{:S(2)}, u32[]{:S(2)}) collective-permute-start(bf16[96,2048]{1,0:T(8,128)(2,1)S(1)} %get-tuple-element.30), channel_id=1, source_target_pairs={{0,24},{8,0},{16,8},{24,16},{1,25},{9,1},{17,9},{25,17},{2,26},{10... | collective-permute-start | bytes 1179656 | tf_op jit(solution)/shard_map/ppermute | solution.py:221
  65.1 14.0 %collective-permute-start.3 = (bf16[96,2048]{1,0:T(8,128)(2,1)S(1)}, bf16[96,2048]{1,0:T(8,128)(2,1)S(1)}, u32[]{:S(2)}, u32[]{:S(2)}) collective-permute-start(bf16[96,2048]{1,0:T(8,128)(2,1)S(1)} %get-tuple-element.35), channel_id=1, source_target_pairs={{0,8},{8,16},{16,24},{24,0},{1,9},{9,17},{17,25},{25,1},{2,10},{10... | collective-permute-start | bytes 1179656 | tf_op jit(solution)/shard_map/ppermute | solution.py:221
  68.4 10.5 %collective-permute-start.4 = (bf16[96,2048]{1,0:T(8,128)(2,1)S(1)}, bf16[96,2048]{1,0:T(8,128)(2,1)S(1)}, u32[]{:S(2)}, u32[]{:S(2)}) collective-permute-start(bf16[96,2048]{1,0:T(8,128)(2,1)S(1)} %get-tuple-element.37), channel_id=1, source_target_pairs={{0,24},{8,0},{16,8},{24,16},{1,25},{9,1},{17,9},{25,17},{2,26},{10... | collective-permute-start | bytes 1179656 | tf_op jit(solution)/shard_map/ppermute | solution.py:221
  70.4 13.9 %collective-permute-start.2 = (bf16[96,2048]{1,0:T(8,128)(2,1)S(1)}, bf16[96,2048]{1,0:T(8,128)(2,1)S(1)}, u32[]{:S(2)}, u32[]{:S(2)}) collective-permute-start(bf16[96,2048]{1,0:T(8,128)(2,1)S(1)} %add_convert_fusion.1), channel_id=1, source_target_pairs={{0,8},{8,16},{16,24},{24,0},{1,9},{9,17},{17,25},{25,1},{2,10},{10... | collective-permute-start | bytes 1179656 | tf_op jit(solution)/shard_map/ppermute | solution.py:221
  79.0 9.7 %collective-permute-start.5 = (bf16[96,2048]{1,0:T(8,128)(2,1)S(1)}, bf16[96,2048]{1,0:T(8,128)(2,1)S(1)}, u32[]{:S(2)}, u32[]{:S(2)}) collective-permute-start(bf16[96,2048]{1,0:T(8,128)(2,1)S(1)} %add_convert_fusion), channel_id=1, source_target_pairs={{0,24},{8,0},{16,8},{24,16},{1,25},{9,1},{17,9},{25,17},{2,26},{10... | collective-permute-start | bytes 1179656 | tf_op jit(solution)/shard_map/ppermute | solution.py:221
  89.6 8.4 %collective-permute-start.6 = (bf16[3,48,512]{2,1,0:T(8,128)(2,1)S(1)}, bf16[3,48,512]{2,1,0:T(8,128)(2,1)S(1)}, u32[]{:S(2)}, u32[]{:S(2)}) collective-permute-start(bf16[3,48,512]{2,1,0:T(8,128)(2,1)S(1)} %get-tuple-element.39), channel_id=1, source_target_pairs={{0,2},{1,3},{2,4},{3,5},{4,6},{5,7},{6,0},{7,1},{8,10},{9,11},{10,... | collective-permute-start | bytes 442376 | tf_op jit(solution)/shard_map/ppermute | solution.py:221
  91.3 7.2 %collective-permute-start.7 = (bf16[3,48,512]{2,1,0:T(8,128)(2,1)S(1)}, bf16[3,48,512]{2,1,0:T(8,128)(2,1)S(1)}, u32[]{:S(2)}, u32[]{:S(2)}) collective-permute-start(bf16[3,48,512]{2,1,0:T(8,128)(2,1)S(1)} %get-tuple-element.40), channel_id=1, source_target_pairs={{0,6},{1,7},{2,0},{3,1},{4,2},{5,3},{6,4},{7,5},{8,14},{9,15},{10,... | collective-permute-start | bytes 442376 | tf_op jit(solution)/shard_map/ppermute | solution.py:221
  98.6 10.1 %collective-permute-start.8 = (bf16[48,1024]{1,0:T(8,128)(2,1)S(1)}, bf16[48,1024]{1,0:T(8,128)(2,1)S(1)}, u32[]{:S(2)}, u32[]{:S(2)}) collective-permute-start(bf16[48,1024]{1,0:T(8,128)(2,1)S(1)} %get-tuple-element.45), channel_id=1, source_target_pairs={{0,1},{1,2},{2,3},{3,4},{4,5},{5,6},{6,7},{7,0},{8,9},{9,10},{10,1... | collective-permute-start | bytes 294920 | tf_op jit(solution)/shard_map/ppermute | solution.py:221
  101.2 8.9 %collective-permute-start.9 = (bf16[48,1024]{1,0:T(8,128)(2,1)S(1)}, bf16[48,1024]{1,0:T(8,128)(2,1)S(1)}, u32[]{:S(2)}, u32[]{:S(2)}) collective-permute-start(bf16[48,1024]{1,0:T(8,128)(2,1)S(1)} %get-tuple-element.46), channel_id=1, source_target_pairs={{0,2},{1,3},{2,4},{3,5},{4,6},{5,7},{6,0},{7,1},{8,10},{9,11},{10,... | collective-permute-start | bytes 294920 | tf_op jit(solution)/shard_map/ppermute | solution.py:221
  105.5 5.4 %collective-permute-start.10 = (bf16[48,1024]{1,0:T(8,128)(2,1)S(1)}, bf16[48,1024]{1,0:T(8,128)(2,1)S(1)}, u32[]{:S(2)}, u32[]{:S(2)}) collective-permute-start(bf16[48,1024]{1,0:T(8,128)(2,1)S(1)} %get-tuple-element.47), channel_id=1, source_target_pairs={{0,7},{1,0},{2,1},{3,2},{4,3},{5,4},{6,5},{7,6},{8,15},{9,8},{10,9... | collective-permute-start | bytes 294920 | tf_op jit(solution)/shard_map/ppermute | solution.py:221
  108.6 5.5 %collective-permute-start.11 = (bf16[48,1024]{1,0:T(8,128)(2,1)S(1)}, bf16[48,1024]{1,0:T(8,128)(2,1)S(1)}, u32[]{:S(2)}, u32[]{:S(2)}) collective-permute-start(bf16[48,1024]{1,0:T(8,128)(2,1)S(1)} %get-tuple-element.48), channel_id=1, source_target_pairs={{0,6},{1,7},{2,0},{3,1},{4,2},{5,3},{6,4},{7,5},{8,14},{9,15},{10,... | collective-permute-start | bytes 294920 | tf_op jit(solution)/shard_map/ppermute | solution.py:221

commit v7 on v6

--- a/solution.py
+++ b/solution.py
@@ -98,11 +98,11 @@
     )(q_fact.T, p_fact.T, q_cot, p_cot)
 
 
-def prepared(projection, passage_of):
+def permuted(projection):
     steps = 8
     cols = K // steps
 
-    def kernel(passage, proj, out, hot, held, made, order, in_sems, out_sems):
+    def kernel(proj, out, held, made, order, in_sems, out_sems):
         def load(n):
             return pltpu.make_async_copy(proj.at[:, pl.ds(cols * n, cols)], held.at[n], in_sems.at[n])
 
@@ -111,7 +111,6 @@
 
         for n in range(steps):
             load(n).start()
-        hot[...] = ones_where(iota((PAIRS, PAIRS), 1) == passage[...])
         u, v = iota((G, G), 0), iota((G, G), 1)
         order[...] = ones_where(v == (u & 63) * 16 + ((u >> 6) & 1) * 8 + (u >> 7))
         for n in range(steps):
@@ -123,12 +122,12 @@
 
     return call(
         kernel,
-        [array(3 * G, K), array(PAIRS, PAIRS)],
+        array(3 * G, K),
         2 * G * G * K,
         16_000_000,
         vmem=57,
-        in_specs=[WHOLE, HBM],
-        out_specs=[HBM, WHOLE],
+        in_specs=[HBM],
+        out_specs=HBM,
         scratch_shapes=[
             pltpu.VMEM((steps, G, cols), BF),
             pltpu.VMEM((steps, G, cols), BF),
@@ -136,7 +135,7 @@
             pltpu.SemaphoreType.DMA((steps,)),
             pltpu.SemaphoreType.DMA((steps,)),
         ],
-    )(passage_of.reshape(PAIRS, 1), projection)
+    )(projection)
 
 
 def rows_of(recv, kind, at, count):
@@ -149,29 +148,30 @@
     return jnp.concatenate(pieces, axis=0)
 
 
-def fetch(proj, held, sems, first):
+def fetch(proj, held, sems):
     copies = []
-    for n in range(2):
-        at = pl.ds(KV * (first + n), KV)
-        copies.append(pltpu.make_async_copy(proj.at[:G, at], held.at[n], sems.at[n]))
+    for n in range(4):
+        copies.append(pltpu.make_async_copy(proj.at[:G, pl.ds(KV * n, KV)], held.at[n], sems.at[n]))
         copies[n].start()
     return copies
 
 
-def products(pair, copies, held, outs):
-    for n in range(2):
+def products(pair, copies, held, takes):
+    for n in range(4):
         copies[n].wait()
-        part = dot(pair[...], held[n]).astype(BF)
+        first, outs = takes[n // 2]
+        part = dot(pair[ROWS * first : ROWS * (first + len(outs)), :], held[n]).astype(BF)
+        at = KV * (n % 2)
         for d, out in enumerate(outs):
-            out[:, KV * n : KV * n + KV] = part[ROWS * d : ROWS * d + ROWS, :]
-
-
-HELD = [pltpu.VMEM((2, G, KV), BF), pltpu.SemaphoreType.DMA((2,))]
-
-
-def product_left(recv, hot, proj):
-    def kernel(recv, hot, proj, pair, o0, o1, o2, o3, wide_q, wide_p, held, sems):
-        copies = fetch(proj, held, sems, 0)
+            out[:, at : at + KV] = part[ROWS * d : ROWS * d + ROWS, :]
+
+
+HELD = [pltpu.VMEM((4, G, KV), BF), pltpu.SemaphoreType.DMA((4,))]
+
+
+def product_far(recv, passage_of, proj):
+    def kernel(recv, passage, proj, pair, l1, l2, r2, r3, wide_q, wide_p, held, sems):
+        copies = fetch(proj, held, sems)
         x = lax.axis_index("px")
         r, c = iota((256, 256), 0), iota((256, 256), 1)
         swap = ones_where(c == (r & 31) * 8 + (r >> 5))
@@ -181,35 +181,40 @@
             for b in range(8):
                 wide_q[32 * g : 32 * g + 32, 128 * b : 128 * b + 128] = mixed[32 * b : 32 * b + 32, :128]
                 wide_p[32 * g : 32 * g + 32, 128 * b : 128 * b + 128] = mixed[32 * b : 32 * b + 32, 128:]
-        summed = (wide_q[...].astype(F32) + dot(hot[...], wide_p[...])).astype(BF)
+        hot = ones_where(iota((PAIRS, PAIRS), 0) == passage[...])
+        picked = lax.dot_general(hot, wide_p[...], (((0,), (0,)), ((), ())), preferred_element_type=F32)
+        summed = (wide_q[...].astype(F32) + picked).astype(BF)
         for i in range(NX):
             at = pl.multiple_of(((i - x) & 3) * ROWS, 32)
             pair[pl.ds(at, ROWS), :] = summed[ROWS * i : ROWS * i + ROWS, :]
-        products(pair, copies, held, (o0, o1, o2, o3))
+        products(pair, copies, held, ((1, (l1, l2)), (2, (r2, r3))))
 
     return call(
         kernel,
         [array(PAIRS, G)] + [array(ROWS, K // 2)] * 4,
         2_500_000_000,
-        8_000_000,
+        12_000_000,
         vmem=44,
         in_specs=[WHOLE, WHOLE, HBM],
         scratch_shapes=[pltpu.VMEM((PAIRS, G), BF)] * 2 + HELD,
-    )(recv, hot, proj)
-
-
-def product_right(pair, proj):
-    def kernel(pair, proj, o0, o1, o2, o3, held, sems):
-        products(pair, fetch(proj, held, sems, 2), held, (o0, o1, o2, o3))
+    )(recv, passage_of.reshape(1, PAIRS), proj)
+
+
+def product_near(pair, proj):
+    def kernel(pair, proj, l3, l0, r0, r1, turned, held, sems):
+        copies = fetch(proj, held, sems)
+        turned[:ROWS, :] = pair[3 * ROWS :, :]
+        turned[ROWS:, :] = pair[: 3 * ROWS, :]
+        products(turned, copies, held, ((0, (l3, l0)), (1, (r0, r1))))
 
     return call(
         kernel,
         [array(ROWS, K // 2)] * 4,
         1_700_000_000,
-        7_000_000,
+        10_000_000,
         vmem=44,
         in_specs=[WHOLE, HBM],
-        scratch_shapes=HELD,
+        scratch_shapes=[pltpu.VMEM((PAIRS, G), BF)] + HELD,
     )(pair, proj)
 
 
@@ -221,20 +226,20 @@
     return lax.ppermute(x, axis, [(i, (i + by) % size) for i in range(size)])
 
 
-def across_x(left, right):
-    l0, l1, l2, l3 = left
-    r0, r1, r2, r3 = right
+def across_x(recv, passage_of, proj):
+    pair, l1, l2, r2, r3 = product_far(recv, passage_of, proj)
     far_l = shift(l2, "px", NX, 1)
+    far_r = shift(r2, "px", NX, -1)
+    l3, l0, r0, r1 = product_near(pair, proj)
     got_l = shift(l3, "px", NX, -1)
-    far_r = shift(r2, "px", NX, -1)
     got_r = shift(r1, "px", NX, 1)
     sum_l = shift(add(l1, far_l), "px", NX, 1)
     sum_r = shift(add(r3, far_r), "px", NX, -1)
-    return l0, got_l, sum_l, r0, got_r, sum_r
+    return sum_l, sum_r, got_l, got_r, l0, r0
 
 
 def across_z(terms):
-    def kernel(l0, l1, l2, r0, r1, r2, far_up, far_down, own, up1, up2, down1, down2):
+    def kernel(l2, r2, l1, r1, l0, r0, far_up, far_down, own, up1, up2, down1, down2):
         left = (l0[...].astype(F32) + l1[...].astype(F32) + l2[...].astype(F32)).astype(BF)
         right = (r0[...].astype(F32) + r1[...].astype(F32) + r2[...].astype(F32)).astype(BF)
         stacked = jnp.concatenate([left[:, :KV], left[:, KV:], right[:, :KV], right[:, KV:]], axis=0)
@@ -278,7 +283,7 @@
     down2 = shift(down2, "pz", NZ, -2)
     up1 = shift(up1, "pz", NZ, 1)
     down1 = shift(down1, "pz", NZ, -1)
-    return own, up1, up2, down1, down2
+    return own, up2, down2, up1, down1
 
 
 def last_sum(parts):
@@ -295,9 +300,7 @@
 
 def local(q_fact, p_fact, q_cot, p_cot, passage_of, projection):
     recv = lax.all_to_all(grads(q_fact, p_fact, q_cot, p_cot), ("px", "pz"), 0, 0, tiled=True)
-    proj, hot = prepared(projection, passage_of)
-    pair, *left = product_left(recv, hot, proj)
-    return last_sum(across_z(across_x(left, product_right(pair, proj))))
+    return last_sum(across_z(across_x(recv, passage_of, permuted(projection))))
 
 
 def solution(mesh):

time: 115 us -> 110 us (0.957)
  starting transfers between devices: 34.5 us -> 32.7 us
  local copies, waits for them, and re-layouts: 1.76 us -> 0.01 us
    ppermute x12, waiting for transfers between devices: 27.6 us -> 24.5 us  [shift(): return lax.ppermute(x, axis, [(i, (i + by) % size) for i in range(size)])]
    all_to_all x1, waiting for transfers between devices: 22.2 us -> 24.7 us  [local(): lax.all_to_all(grads(q_fact, p_fact, q_cot, p_cot), ('px', 'pz'), 0, 0, t...]
    ppermute x12, starting transfers between devices: 22.8 us -> 21 us  [shift(): return lax.ppermute(x, axis, [(i, (i + by) % size) for i in range(size)])]
  transfers between devices with their start and end apart: 13 -> 13, of which waited for: 10 -> 9; matrix products, arithmetic and copies ran while one was open for 1% -> 0% of each run, Pallas kernels for 15% -> 15%
where the time goes in v7:
time: 110 us
  waiting for transfers between devices  49.2 us (45%)
  starting transfers between devices  32.7 us (30%)
  Pallas kernels  27.9 us (25%)
    all_to_all x1, waiting for transfers between devices, local(): lax.all_to_all(grads(q_fact, p_fact, q_cot, p_cot), ('px', 'pz'), 0, 0, t...  24.7 us
    ppermute x12, waiting for transfers between devices, shift(): return lax.ppermute(x, axis, [(i, (i + by) % size) for i in range(size)])  24.5 us
    ppermute x12, starting transfers between devices, shift(): return lax.ppermute(x, axis, [(i, (i + by) % size) for i in range(size)])  21 us
    pallas_call x1, Pallas kernels, permuted(): call(kernel, array(3 * G, K), 2 * G * G * K, 16000000, vmem=57, in_specs=...  12.3 us
    all_to_all x1, starting transfers between devices, local(): lax.all_to_all(grads(q_fact, p_fact, q_cot, p_cot), ('px', 'pz'), 0, 0, t...  11.7 us
    pallas_call x1, Pallas kernels, product_far(): call(kernel, [array(PAIRS, G)] + [array(ROWS, K // 2)] * 4, 2500000000, 1...  5.15 us
    pallas_call x1, Pallas kernels, grads(): call(kernel, array(N, 2 * ROWS, 128), 800000000, 5500000, vmem=60, grid=(...  4.6 us
    pallas_call x1, Pallas kernels, product_near(): call(kernel, [array(ROWS, K // 2)] * 4, 1700000000, 10000000, vmem=44, in...  4.11 us
  transfers between devices with their start and end apart: 13, of which 9 were waited for; matrix products, arithmetic and copies ran while one was open for 0% of the time, Pallas kernels for 15%

profile of v7, /device:TPU:14, one launch (start us, length us, event | category | flops | bytes accessed | tf_op | source)
XLA Modules:
  0.0 110.1 jit_solution(1677590936612797363)
XLA Ops:
  0.0 4.6 %shard_map.64 = bf16[32,192,128]{2,1,0:T(8,128)(2,1)} custom-call(bf16[32,384]{1,0:T(8,128)(2,1)} %bitcast.3, bf16[32,576]{1,0:T(8,128)(2,1)} %bitcast.2, bf16[384,2048]{1,0:T(8,128)(2,1)} %q_cot.1, bf16[576,2048]{1,0:T(8,128)(2,1)} %p_cot.1), custom_call_target="tpu_custom_call" | custom-call | flops 800000000 | bytes 5500000 | tf_op jit(solution)/shard_map/pallas_call | solution.py:83
  4.6 0.0 copy-start
  4.6 11.7 %all-to-all-start = ((bf16[32,192,128]{2,1,0:T(8,128)(2,1)}), bf16[32,192,128]{2,1,0:T(8,128)(2,1)S(1)}, u32[]{:S(2)}, u32[]{:S(2)}) async-start(bf16[32,192,128]{2,1,0:T(8,128)(2,1)} %shard_map.64), calls=%async_computation | async-start | bytes 3145728 | tf_op jit(solution)/shard_map/all_to_all | solution.py:302
  16.3 0.0 copy-done
  16.4 12.3 %shard_map.65.proj = bf16[3072,4096]{1,0:T(8,128)(2,1)} custom-call(bf16[1024,4096]{1,0:T(8,128)(2,1)} %proj.1), custom_call_target="tpu_custom_call" | custom-call | flops 8589934592 | bytes 16000000 | tf_op jit(solution)/shard_map/pallas_call | solution.py:123
  28.7 24.7 %all-to-all-done.recv = bf16[32,192,128]{2,1,0:T(8,128)(2,1)S(1)} async-done(((bf16[32,192,128]{2,1,0:T(8,128)(2,1)}), bf16[32,192,128]{2,1,0:T(8,128)(2,1)S(1)}, u32[]{:S(2)}, u32[]{:S(2)}) %all-to-all-start) | async-done | bytes 1572896 | tf_op jit(solution)/shard_map/all_to_all | solution.py:302
  53.4 5.1 %shard_map.66 = (bf16[384,1024]{1,0:T(8,128)(2,1)S(1)}, bf16[96,2048]{1,0:T(8,128)(2,1)S(1)}, bf16[96,2048]{1,0:T(8,128)(2,1)S(1)}, bf16[96,2048]{1,0:T(8,128)(2,1)S(1)}, bf16[96,2048]{1,0:T(8,128)(2,1)S(1)}) custom-call(bf16[32,192,128]{2,1,0:T(8,128)(2,1)S(1)} %all-to-all-done.recv, s32[1,384]{1,0:T(1,128)S(1)} %reshape.3.passage, ...), custom_call_target="tpu_custom_call" | custom-call | flops 2500000000 | bytes 12000000 | tf_op jit(solution)/shard_map/pallas_call | solution.py:192
  58.6 2.5 %collective-permute-start = (bf16[96,2048]{1,0:T(8,128)(2,1)S(1)}, bf16[96,2048]{1,0:T(8,128)(2,1)S(1)}, u32[]{:S(2)}, u32[]{:S(2)}) collective-permute-start(bf16[96,2048]{1,0:T(8,128)(2,1)S(1)} %get-tuple-element.26), channel_id=1, source_target_pairs={{0,8},{8,16},{16,24},{24,0},{1,9},{9,17},{17,25},{25,1},{2,10},{10... | collective-permute-start | bytes 1179656 | tf_op jit(solution)/shard_map/ppermute | solution.py:226
  61.1 0.0 collective-permute-start.2
  61.1 4.1 %shard_map.67 = (bf16[96,2048]{1,0:T(8,128)(2,1)S(1)}, bf16[96,2048]{1,0:T(8,128)(2,1)S(1)}, bf16[96,2048]{1,0:T(8,128)(2,1)S(1)}, bf16[96,2048]{1,0:T(8,128)(2,1)S(1)}) custom-call(bf16[384,1024]{1,0:T(8,128)(2,1)S(1)} %get-tuple-element.29.pair, bf16[3072,4096]{1,0:T(8,128)(2,1)} %shard_map.65.proj), custom_call_target="tpu_custom_call" | custom-call | flops 1700000000 | bytes 10000000 | tf_op jit(solution)/shard_map/pallas_call | solution.py:210
  65.2 0.2 collective-permute-start.4
  65.4 3.2 %collective-permute-start.5 = (bf16[96,2048]{1,0:T(8,128)(2,1)S(1)}, bf16[96,2048]{1,0:T(8,128)(2,1)S(1)}, u32[]{:S(2)}, u32[]{:S(2)}) collective-permute-start(bf16[96,2048]{1,0:T(8,128)(2,1)S(1)} %get-tuple-element.31), channel_id=1, source_target_pairs={{0,8},{8,16},{16,24},{24,0},{1,9},{9,17},{17,25},{25,1},{2,10},{10... | collective-permute-start | bytes 1179656 | tf_op jit(solution)/shard_map/ppermute | solution.py:226
  68.6 0.6 collective-permute-done
  69.2 0.1 add_convert_fusion.1
  69.3 2.6 %collective-permute-start.1 = (bf16[96,2048]{1,0:T(8,128)(2,1)S(1)}, bf16[96,2048]{1,0:T(8,128)(2,1)S(1)}, u32[]{:S(2)}, u32[]{:S(2)}) collective-permute-start(bf16[96,2048]{1,0:T(8,128)(2,1)S(1)} %add_convert_fusion.1), channel_id=1, source_target_pairs={{0,8},{8,16},{16,24},{24,0},{1,9},{9,17},{17,25},{25,1},{2,10},{10... | collective-permute-start | bytes 1179656 | tf_op jit(solution)/shard_map/ppermute | solution.py:226
  71.9 2.4 %collective-permute-done.2 = bf16[96,2048]{1,0:T(8,128)(2,1)S(1)} collective-permute-done((bf16[96,2048]{1,0:T(8,128)(2,1)S(1)}, bf16[96,2048]{1,0:T(8,128)(2,1)S(1)}, u32[]{:S(2)}, u32[]{:S(2)}) %collective-permute-start.2) | collective-permute-done | bytes 393248 | tf_op jit(solution)/shard_map/ppermute | solution.py:226
  74.4 0.1 add_convert_fusion
  74.5 0.1 collective-permute-start.3
  74.6 8.2 %collective-permute-done.4.l1 = bf16[96,2048]{1,0:T(8,128)(2,1)S(1)} collective-permute-done((bf16[96,2048]{1,0:T(8,128)(2,1)S(1)}, bf16[96,2048]{1,0:T(8,128)(2,1)S(1)}, u32[]{:S(2)}, u32[]{:S(2)}) %collective-permute-start.4) | collective-permute-done | bytes 393248 | tf_op jit(solution)/shard_map/ppermute | solution.py:226
  82.7 0.0 collective-permute-done.5.r1
  82.7 1.1 %collective-permute-done.1.l2 = bf16[96,2048]{1,0:T(8,128)(2,1)S(1)} collective-permute-done((bf16[96,2048]{1,0:T(8,128)(2,1)S(1)}, bf16[96,2048]{1,0:T(8,128)(2,1)S(1)}, u32[]{:S(2)}, u32[]{:S(2)}) %collective-permute-start.1) | collective-permute-done | bytes 393248 | tf_op jit(solution)/shard_map/ppermute | solution.py:226
  83.9 3.1 %collective-permute-done.3.r2 = bf16[96,2048]{1,0:T(8,128)(2,1)S(1)} collective-permute-done((bf16[96,2048]{1,0:T(8,128)(2,1)S(1)}, bf16[96,2048]{1,0:T(8,128)(2,1)S(1)}, u32[]{:S(2)}, u32[]{:S(2)}) %collective-permute-start.3) | collective-permute-done | bytes 393248 | tf_op jit(solution)/shard_map/ppermute | solution.py:226
  86.9 0.9 shard_map.68
  87.8 1.7 %collective-permute-start.6 = (bf16[3,48,512]{2,1,0:T(8,128)(2,1)S(1)}, bf16[3,48,512]{2,1,0:T(8,128)(2,1)S(1)}, u32[]{:S(2)}, u32[]{:S(2)}) collective-permute-start(bf16[3,48,512]{2,1,0:T(8,128)(2,1)S(1)} %get-tuple-element.35), channel_id=1, source_target_pairs={{0,2},{1,3},{2,4},{3,5},{4,6},{5,7},{6,0},{7,1},{8,10},{9,11},{10,... | collective-permute-start | bytes 442376 | tf_op jit(solution)/shard_map/ppermute | solution.py:226
  89.6 2.5 %collective-permute-start.7 = (bf16[3,48,512]{2,1,0:T(8,128)(2,1)S(1)}, bf16[3,48,512]{2,1,0:T(8,128)(2,1)S(1)}, u32[]{:S(2)}, u32[]{:S(2)}) collective-permute-start(bf16[3,48,512]{2,1,0:T(8,128)(2,1)S(1)} %get-tuple-element.36), channel_id=1, source_target_pairs={{0,6},{1,7},{2,0},{3,1},{4,2},{5,3},{6,4},{7,5},{8,14},{9,15},{10,... | collective-permute-start | bytes 442376 | tf_op jit(solution)/shard_map/ppermute | solution.py:226
  92.1 4.8 %collective-permute-done.6.far_up = bf16[3,48,512]{2,1,0:T(8,128)(2,1)S(1)} collective-permute-done((bf16[3,48,512]{2,1,0:T(8,128)(2,1)S(1)}, bf16[3,48,512]{2,1,0:T(8,128)(2,1)S(1)}, u32[]{:S(2)}, u32[]{:S(2)}) %collective-permute-start.6) | collective-permute-done | bytes 147488 | tf_op jit(solution)/shard_map/ppermute | solution.py:226
  96.8 0.0 collective-permute-done.7.far_down
  96.8 0.1 shard_map.69
  96.9 4.9 %collective-permute-start.8 = (bf16[48,1024]{1,0:T(8,128)(2,1)S(1)}, bf16[48,1024]{1,0:T(8,128)(2,1)S(1)}, u32[]{:S(2)}, u32[]{:S(2)}) collective-permute-start(bf16[48,1024]{1,0:T(8,128)(2,1)S(1)} %get-tuple-element.41), channel_id=1, source_target_pairs={{0,2},{1,3},{2,4},{3,5},{4,6},{5,7},{6,0},{7,1},{8,10},{9,11},{10,... | collective-permute-start | bytes 294920 | tf_op jit(solution)/shard_map/ppermute | solution.py:226
  101.8 0.0 collective-permute-start.9
  101.8 2.3 %collective-permute-start.10 = (bf16[48,1024]{1,0:T(8,128)(2,1)S(1)}, bf16[48,1024]{1,0:T(8,128)(2,1)S(1)}, u32[]{:S(2)}, u32[]{:S(2)}) collective-permute-start(bf16[48,1024]{1,0:T(8,128)(2,1)S(1)} %get-tuple-element.43), channel_id=1, source_target_pairs={{0,1},{1,2},{2,3},{3,4},{4,5},{5,6},{6,7},{7,0},{8,9},{9,10},{10,1... | collective-permute-start | bytes 294920 | tf_op jit(solution)/shard_map/ppermute | solution.py:226
  104.1 0.9 collective-permute-start.11
  105.0 0.0 collective-permute-done.8.refs_1_
  105.0 3.3 %collective-permute-done.9.refs_2_ = bf16[48,1024]{1,0:T(8,128)(2,1)S(1)} collective-permute-done((bf16[48,1024]{1,0:T(8,128)(2,1)S(1)}, bf16[48,1024]{1,0:T(8,128)(2,1)S(1)}, u32[]{:S(2)}, u32[]{:S(2)}) %collective-permute-start.9) | collective-permute-done | bytes 98336 | tf_op jit(solution)/shard_map/ppermute | solution.py:226
  108.3 0.0 collective-permute-done.10.refs_3_
  108.3 1.0 collective-permute-done.11.refs_4_
  109.3 0.8 shard_map.70
  (1 shorter events, 0.0 us)
Async XLA Ops:
  4.6 11.7 %copy-start = (s32[384]{0:T(512)S(1)}, s32[384]{0:T(512)}, u32[]{:S(2)}) copy-start(s32[384]{0:T(512)} %param.10) | copy-start | bytes 4612
  4.6 48.8 %all-to-all-start = ((bf16[32,192,128]{2,1,0:T(8,128)(2,1)}), bf16[32,192,128]{2,1,0:T(8,128)(2,1)S(1)}, u32[]{:S(2)}, u32[]{:S(2)}) async-start(bf16[32,192,128]{2,1,0:T(8,128)(2,1)} %shard_map.64), calls=%async_computation | async-start | bytes 3145728 | tf_op jit(solution)/shard_map/all_to_all | solution.py:302
  58.6 10.6 %collective-permute-start = (bf16[96,2048]{1,0:T(8,128)(2,1)S(1)}, bf16[96,2048]{1,0:T(8,128)(2,1)S(1)}, u32[]{:S(2)}, u32[]{:S(2)}) collective-permute-start(bf16[96,2048]{1,0:T(8,128)(2,1)S(1)} %get-tuple-element.26), channel_id=1, source_target_pairs={{0,8},{8,16},{16,24},{24,0},{1,9},{9,17},{17,25},{25,1},{2,10},{10... | collective-permute-start | bytes 1179656 | tf_op jit(solution)/shard_map/ppermute | solution.py:226
  61.1 13.3 %collective-permute-start.2 = (bf16[96,2048]{1,0:T(8,128)(2,1)S(1)}, bf16[96,2048]{1,0:T(8,128)(2,1)S(1)}, u32[]{:S(2)}, u32[]{:S(2)}) collective-permute-start(bf16[96,2048]{1,0:T(8,128)(2,1)S(1)} %get-tuple-element.28), channel_id=1, source_target_pairs={{0,24},{8,0},{16,8},{24,16},{1,25},{9,1},{17,9},{25,17},{2,26},{10... | collective-permute-start | bytes 1179656 | tf_op jit(solution)/shard_map/ppermute | solution.py:226
  65.2 17.5 %collective-permute-start.4 = (bf16[96,2048]{1,0:T(8,128)(2,1)S(1)}, bf16[96,2048]{1,0:T(8,128)(2,1)S(1)}, u32[]{:S(2)}, u32[]{:S(2)}) collective-permute-start(bf16[96,2048]{1,0:T(8,128)(2,1)S(1)} %get-tuple-element.30), channel_id=1, source_target_pairs={{0,24},{8,0},{16,8},{24,16},{1,25},{9,1},{17,9},{25,17},{2,26},{10... | collective-permute-start | bytes 1179656 | tf_op jit(solution)/shard_map/ppermute | solution.py:226
  65.4 17.3 %collective-permute-start.5 = (bf16[96,2048]{1,0:T(8,128)(2,1)S(1)}, bf16[96,2048]{1,0:T(8,128)(2,1)S(1)}, u32[]{:S(2)}, u32[]{:S(2)}) collective-permute-start(bf16[96,2048]{1,0:T(8,128)(2,1)S(1)} %get-tuple-element.31), channel_id=1, source_target_pairs={{0,8},{8,16},{16,24},{24,0},{1,9},{9,17},{17,25},{25,1},{2,10},{10... | collective-permute-start | bytes 1179656 | tf_op jit(solution)/shard_map/ppermute | solution.py:226
  69.3 14.5 %collective-permute-start.1 = (bf16[96,2048]{1,0:T(8,128)(2,1)S(1)}, bf16[96,2048]{1,0:T(8,128)(2,1)S(1)}, u32[]{:S(2)}, u32[]{:S(2)}) collective-permute-start(bf16[96,2048]{1,0:T(8,128)(2,1)S(1)} %add_convert_fusion.1), channel_id=1, source_target_pairs={{0,8},{8,16},{16,24},{24,0},{1,9},{9,17},{17,25},{25,1},{2,10},{10... | collective-permute-start | bytes 1179656 | tf_op jit(solution)/shard_map/ppermute | solution.py:226
  74.5 12.5 %collective-permute-start.3 = (bf16[96,2048]{1,0:T(8,128)(2,1)S(1)}, bf16[96,2048]{1,0:T(8,128)(2,1)S(1)}, u32[]{:S(2)}, u32[]{:S(2)}) collective-permute-start(bf16[96,2048]{1,0:T(8,128)(2,1)S(1)} %add_convert_fusion), channel_id=1, source_target_pairs={{0,24},{8,0},{16,8},{24,16},{1,25},{9,1},{17,9},{25,17},{2,26},{10... | collective-permute-start | bytes 1179656 | tf_op jit(solution)/shard_map/ppermute | solution.py:226
  87.8 9.0 %collective-permute-start.6 = (bf16[3,48,512]{2,1,0:T(8,128)(2,1)S(1)}, bf16[3,48,512]{2,1,0:T(8,128)(2,1)S(1)}, u32[]{:S(2)}, u32[]{:S(2)}) collective-permute-start(bf16[3,48,512]{2,1,0:T(8,128)(2,1)S(1)} %get-tuple-element.35), channel_id=1, source_target_pairs={{0,2},{1,3},{2,4},{3,5},{4,6},{5,7},{6,0},{7,1},{8,10},{9,11},{10,... | collective-permute-start | bytes 442376 | tf_op jit(solution)/shard_map/ppermute | solution.py:226
  89.6 7.3 %collective-permute-start.7 = (bf16[3,48,512]{2,1,0:T(8,128)(2,1)S(1)}, bf16[3,48,512]{2,1,0:T(8,128)(2,1)S(1)}, u32[]{:S(2)}, u32[]{:S(2)}) collective-permute-start(bf16[3,48,512]{2,1,0:T(8,128)(2,1)S(1)} %get-tuple-element.36), channel_id=1, source_target_pairs={{0,6},{1,7},{2,0},{3,1},{4,2},{5,3},{6,4},{7,5},{8,14},{9,15},{10,... | collective-permute-start | bytes 442376 | tf_op jit(solution)/shard_map/ppermute | solution.py:226
  96.9 8.1 %collective-permute-start.8 = (bf16[48,1024]{1,0:T(8,128)(2,1)S(1)}, bf16[48,1024]{1,0:T(8,128)(2,1)S(1)}, u32[]{:S(2)}, u32[]{:S(2)}) collective-permute-start(bf16[48,1024]{1,0:T(8,128)(2,1)S(1)} %get-tuple-element.41), channel_id=1, source_target_pairs={{0,2},{1,3},{2,4},{3,5},{4,6},{5,7},{6,0},{7,1},{8,10},{9,11},{10,... | collective-permute-start | bytes 294920 | tf_op jit(solution)/shard_map/ppermute | solution.py:226
  101.8 6.5 %collective-permute-start.9 = (bf16[48,1024]{1,0:T(8,128)(2,1)S(1)}, bf16[48,1024]{1,0:T(8,128)(2,1)S(1)}, u32[]{:S(2)}, u32[]{:S(2)}) collective-permute-start(bf16[48,1024]{1,0:T(8,128)(2,1)S(1)} %get-tuple-element.42), channel_id=1, source_target_pairs={{0,6},{1,7},{2,0},{3,1},{4,2},{5,3},{6,4},{7,5},{8,14},{9,15},{10,... | collective-permute-start | bytes 294920 | tf_op jit(solution)/shard_map/ppermute | solution.py:226
  101.8 6.5 %collective-permute-start.10 = (bf16[48,1024]{1,0:T(8,128)(2,1)S(1)}, bf16[48,1024]{1,0:T(8,128)(2,1)S(1)}, u32[]{:S(2)}, u32[]{:S(2)}) collective-permute-start(bf16[48,1024]{1,0:T(8,128)(2,1)S(1)} %get-tuple-element.43), channel_id=1, source_target_pairs={{0,1},{1,2},{2,3},{3,4},{4,5},{5,6},{6,7},{7,0},{8,9},{9,10},{10,1... | collective-permute-start | bytes 294920 | tf_op jit(solution)/shard_map/ppermute | solution.py:226
  104.1 5.2 %collective-permute-start.11 = (bf16[48,1024]{1,0:T(8,128)(2,1)S(1)}, bf16[48,1024]{1,0:T(8,128)(2,1)S(1)}, u32[]{:S(2)}, u32[]{:S(2)}) collective-permute-start(bf16[48,1024]{1,0:T(8,128)(2,1)S(1)} %get-tuple-element.44), channel_id=1, source_target_pairs={{0,7},{1,0},{2,1},{3,2},{4,3},{5,4},{6,5},{7,6},{8,15},{9,8},{10,9... | collective-permute-start | bytes 294920 | tf_op jit(solution)/shard_map/ppermute | solution.py:226

commit v8 on v7

--- a/solution.py
+++ b/solution.py
@@ -99,7 +99,7 @@
 
 
 def permuted(projection):
-    steps = 8
+    steps = 4
     cols = K // steps
 
     def kernel(proj, out, held, made, order, in_sems, out_sems):
@@ -107,7 +107,7 @@
             return pltpu.make_async_copy(proj.at[:, pl.ds(cols * n, cols)], held.at[n], in_sems.at[n])
 
         def store(n):
-            return pltpu.make_async_copy(made.at[n], out.at[:G, pl.ds(cols * n, cols)], out_sems.at[n])
+            return pltpu.make_async_copy(made.at[n], out.at[n], out_sems.at[n])
 
         for n in range(steps):
             load(n).start()
@@ -122,7 +122,7 @@
 
     return call(
         kernel,
-        array(3 * G, K),
+        array(12, G, KV),
         2 * G * G * K,
         16_000_000,
         vmem=57,
@@ -151,7 +151,7 @@
 def fetch(proj, held, sems):
     copies = []
     for n in range(4):
-        copies.append(pltpu.make_async_copy(proj.at[:G, pl.ds(KV * n, KV)], held.at[n], sems.at[n]))
+        copies.append(pltpu.make_async_copy(proj.at[n], held.at[n], sems.at[n]))
         copies[n].start()
     return copies
 
@@ -239,7 +239,7 @@
 
 
 def across_z(terms):
-    def kernel(l2, r2, l1, r1, l0, r0, far_up, far_down, own, up1, up2, down1, down2):
+    def kernel(l2, r2, l1, r1, l0, r0, odd_up, odd_down, own, up, down, across):
         left = (l0[...].astype(F32) + l1[...].astype(F32) + l2[...].astype(F32)).astype(BF)
         right = (r0[...].astype(F32) + r1[...].astype(F32) + r2[...].astype(F32)).astype(BF)
         stacked = jnp.concatenate([left[:, :KV], left[:, KV:], right[:, :KV], right[:, KV:]], axis=0)
@@ -250,48 +250,25 @@
         z = (block + lax.axis_index("pz")) & (NZ - 1)
         hot = ones_where(c == quarter * ROWS + z * MINE + item)
         rows = dot(hot, stacked).astype(BF)
-        for k, out in ((0, own), (1, up1), (2, up2), (6, down2), (7, down1)):
+        outs = (own, odd_up.at[0], up, odd_up.at[1], across, odd_down.at[1], down, odd_down.at[0])
+        for k, out in enumerate(outs):
             out[...] = rows[48 * k : 48 * k + 48, :]
-        half = KV // 2
-        far_up[0] = rows[48 * 3 : 48 * 4, :half]
-        far_up[1] = rows[48 * 3 : 48 * 4, half:]
-        far_up[2] = rows[48 * 4 : 48 * 5, :half]
-        far_down[0] = rows[48 * 5 : 48 * 6, :half]
-        far_down[1] = rows[48 * 5 : 48 * 6, half:]
-        far_down[2] = rows[48 * 4 : 48 * 5, half:]
-
-    outs = [array(3, 48, KV // 2)] * 2 + [array(48, KV)] * 5
-    far_up, far_down, *near = call(kernel, outs, 300_000_000, 4_000_000)(*terms)
-    far_up = shift(far_up, "pz", NZ, 2)
-    far_down = shift(far_down, "pz", NZ, -2)
-
-    def add_kernel(far_up, far_down, up1, up2, down1, down2, *outs):
-        half = KV // 2
-        for far, near1, near2, out1, out2, side in (
-            (far_up, up1, up2, outs[0], outs[1], 0),
-            (far_down, down1, down2, outs[2], outs[3], 1),
-        ):
-            out1[:, :half] = add(near1[:, :half], far[0])
-            out1[:, half:] = add(near1[:, half:], far[1])
-            for i in range(2):
-                at = slice(half * i, half * i + half)
-                out2[:, at] = add(near2[:, at], far[2]) if i == side else near2[:, at]
-
-    own, *near = near
-    up1, up2, down1, down2 = call(add_kernel, [array(48, KV)] * 4, 1_000_000, 1_000_000)(far_up, far_down, *near)
-    up2 = shift(up2, "pz", NZ, 2)
-    down2 = shift(down2, "pz", NZ, -2)
-    up1 = shift(up1, "pz", NZ, 1)
-    down1 = shift(down1, "pz", NZ, -1)
-    return own, up2, down2, up1, down1
+
+    outs = [array(2, 48, KV)] * 2 + [array(48, KV)] * 4
+    odd_up, odd_down, own, up, down, across = call(kernel, outs, 300_000_000, 4_000_000)(*terms)
+    odd_up = shift(odd_up, "pz", NZ, 1)
+    odd_down = shift(odd_down, "pz", NZ, -1)
+    across = shift(across, "pz", NZ, 4)
+    up = shift(add(up, odd_up[1]), "pz", NZ, 2)
+    down = shift(add(down, odd_down[1]), "pz", NZ, -2)
+    return up, down, odd_up, odd_down, across, own
 
 
 def last_sum(parts):
-    def kernel(*refs):
-        *terms, out = refs
-        total = terms[0][...].astype(F32)
-        for term in terms[1:]:
-            total = total + term[...].astype(F32)
+    def kernel(up, down, odd_up, odd_down, across, own, out):
+        total = own[...].astype(F32)
+        for term in (odd_up[0], odd_down[0], across[...], up[...], down[...]):
+            total = total + term.astype(F32)
         for q in range(4):
             out[:, KV * q : KV * q + KV] = total[MINE * q : MINE * q + MINE, :]
 

time: 110 us -> 110 us (level); the launches traced: 110 us -> 109 us
  starting transfers between devices: 32.7 us -> 30.6 us
    ppermute x12 -> x11, starting transfers between devices: 21 us -> 18.8 us  [shift(): return lax.ppermute(x, axis, [(i, (i + by) % size) for i in range(size)])]
    ppermute x12 -> x11, waiting for transfers between devices: 24.5 us -> 25.4 us  [shift(): return lax.ppermute(x, axis, [(i, (i + by) % size) for i in range(size)])]
    pallas_call x3 -> x2, Pallas kernels: 13.3 us -> 13.2 us  [the longest x1 12.3 us: permuted(): call(kernel, array(12, G, KV), 2 * G * G * K, 16000000, vmem=57, in_specs...]
  transfers between devices with their start and end apart: 13 -> 12, of which waited for: 9 -> 10; matrix products, arithmetic and copies ran while one was open for 0% -> 0% of each run, Pallas kernels for 15% -> 15%
where the time goes in v8:
time: 110 us; the launch traced here: 109 us
  waiting for transfers between devices  50.1 us (46%)
  starting transfers between devices  30.6 us (28%)
  Pallas kernels  27.9 us (25%)
    ppermute x11, waiting for transfers between devices, shift(): return lax.ppermute(x, axis, [(i, (i + by) % size) for i in range(size)])  25.4 us
    all_to_all x1, waiting for transfers between devices, local(): lax.all_to_all(grads(q_fact, p_fact, q_cot, p_cot), ('px', 'pz'), 0, 0, t...  24.7 us
    ppermute x11, starting transfers between devices, shift(): return lax.ppermute(x, axis, [(i, (i + by) % size) for i in range(size)])  18.8 us
    pallas_call x1, Pallas kernels, permuted(): call(kernel, array(12, G, KV), 2 * G * G * K, 16000000, vmem=57, in_specs...  12.3 us
    all_to_all x1, starting transfers between devices, local(): lax.all_to_all(grads(q_fact, p_fact, q_cot, p_cot), ('px', 'pz'), 0, 0, t...  11.7 us
    pallas_call x1, Pallas kernels, product_far(): call(kernel, [array(PAIRS, G)] + [array(ROWS, K // 2)] * 4, 2500000000, 1...  5.12 us
    pallas_call x1, Pallas kernels, grads(): call(kernel, array(N, 2 * ROWS, 128), 800000000, 5500000, vmem=60, grid=(...  4.62 us
    pallas_call x1, Pallas kernels, product_near(): call(kernel, [array(ROWS, K // 2)] * 4, 1700000000, 10000000, vmem=44, in...  4.08 us
  transfers between devices with their start and end apart: 12, of which 10 were waited for; matrix products, arithmetic and copies ran while one was open for 0% of the time, Pallas kernels for 15%

profile of v8, /device:TPU:14, one launch (start us, length us, event | category | flops | bytes accessed | tf_op | source)
XLA Modules:
  0.0 108.9 jit_solution(17257275191165810623)
XLA Ops:
  0.0 4.6 %shard_map.64 = bf16[32,192,128]{2,1,0:T(8,128)(2,1)} custom-call(bf16[32,384]{1,0:T(8,128)(2,1)} %bitcast.13, bf16[32,576]{1,0:T(8,128)(2,1)} %bitcast.12, bf16[384,2048]{1,0:T(8,128)(2,1)} %q_cot.1, bf16[576,2048]{1,0:T(8,128)(2,1)} %p_cot.1), custom_call_target="tpu_custom_call" | custom-call | flops 800000000 | bytes 5500000 | tf_op jit(solution)/shard_map/pallas_call | solution.py:83
  4.6 0.0 copy-start
  4.6 11.7 %all-to-all-start = ((bf16[32,192,128]{2,1,0:T(8,128)(2,1)}), bf16[32,192,128]{2,1,0:T(8,128)(2,1)S(1)}, u32[]{:S(2)}, u32[]{:S(2)}) async-start(bf16[32,192,128]{2,1,0:T(8,128)(2,1)} %shard_map.64), calls=%async_computation | async-start | bytes 3145728 | tf_op jit(solution)/shard_map/all_to_all | solution.py:279
  16.4 0.0 copy-done
  16.4 12.3 %shard_map.65.proj = bf16[12,1024,1024]{2,1,0:T(8,128)(2,1)} custom-call(bf16[1024,4096]{1,0:T(8,128)(2,1)} %proj.1), custom_call_target="tpu_custom_call" | custom-call | flops 8589934592 | bytes 16000000 | tf_op jit(solution)/shard_map/pallas_call | solution.py:123
  28.7 24.7 %all-to-all-done.recv = bf16[32,192,128]{2,1,0:T(8,128)(2,1)S(1)} async-done(((bf16[32,192,128]{2,1,0:T(8,128)(2,1)}), bf16[32,192,128]{2,1,0:T(8,128)(2,1)S(1)}, u32[]{:S(2)}, u32[]{:S(2)}) %all-to-all-start) | async-done | bytes 1572896 | tf_op jit(solution)/shard_map/all_to_all | solution.py:279
  53.5 5.1 %shard_map.66 = (bf16[384,1024]{1,0:T(8,128)(2,1)S(1)}, bf16[96,2048]{1,0:T(8,128)(2,1)S(1)}, bf16[96,2048]{1,0:T(8,128)(2,1)S(1)}, bf16[96,2048]{1,0:T(8,128)(2,1)S(1)}, bf16[96,2048]{1,0:T(8,128)(2,1)S(1)}) custom-call(bf16[32,192,128]{2,1,0:T(8,128)(2,1)S(1)} %all-to-all-done.recv, s32[1,384]{1,0:T(1,128)S(1)} %reshape.7.passage, ...), custom_call_target="tpu_custom_call" | custom-call | flops 2500000000 | bytes 12000000 | tf_op jit(solution)/shard_map/pallas_call | solution.py:192
  58.6 2.5 %collective-permute-start = (bf16[96,2048]{1,0:T(8,128)(2,1)S(1)}, bf16[96,2048]{1,0:T(8,128)(2,1)S(1)}, u32[]{:S(2)}, u32[]{:S(2)}) collective-permute-start(bf16[96,2048]{1,0:T(8,128)(2,1)S(1)} %get-tuple-element.21), channel_id=1, source_target_pairs={{0,8},{8,16},{16,24},{24,0},{1,9},{9,17},{17,25},{25,1},{2,10},{10... | collective-permute-start | bytes 1179656 | tf_op jit(solution)/shard_map/ppermute | solution.py:226
  61.1 0.0 collective-permute-start.2
  61.1 4.1 %shard_map.67 = (bf16[96,2048]{1,0:T(8,128)(2,1)S(1)}, bf16[96,2048]{1,0:T(8,128)(2,1)S(1)}, bf16[96,2048]{1,0:T(8,128)(2,1)S(1)}, bf16[96,2048]{1,0:T(8,128)(2,1)S(1)}) custom-call(bf16[384,1024]{1,0:T(8,128)(2,1)S(1)} %get-tuple-element.24.pair, bf16[12,1024,1024]{2,1,0:T(8,128)(2,1)} %shard_map.65.proj), custom_call_target="tpu_custom_call" | custom-call | flops 1700000000 | bytes 10000000 | tf_op jit(solution)/shard_map/pallas_call | solution.py:210
  65.2 0.2 collective-permute-start.4
  65.4 3.2 %collective-permute-start.5 = (bf16[96,2048]{1,0:T(8,128)(2,1)S(1)}, bf16[96,2048]{1,0:T(8,128)(2,1)S(1)}, u32[]{:S(2)}, u32[]{:S(2)}) collective-permute-start(bf16[96,2048]{1,0:T(8,128)(2,1)S(1)} %get-tuple-element.26), channel_id=1, source_target_pairs={{0,8},{8,16},{16,24},{24,0},{1,9},{9,17},{17,25},{25,1},{2,10},{10... | collective-permute-start | bytes 1179656 | tf_op jit(solution)/shard_map/ppermute | solution.py:226
  68.6 0.7 collective-permute-done
  69.3 0.1 add_convert_fusion.1
  69.4 2.6 %collective-permute-start.1 = (bf16[96,2048]{1,0:T(8,128)(2,1)S(1)}, bf16[96,2048]{1,0:T(8,128)(2,1)S(1)}, u32[]{:S(2)}, u32[]{:S(2)}) collective-permute-start(bf16[96,2048]{1,0:T(8,128)(2,1)S(1)} %add_convert_fusion.1), channel_id=1, source_target_pairs={{0,8},{8,16},{16,24},{24,0},{1,9},{9,17},{17,25},{25,1},{2,10},{10... | collective-permute-start | bytes 1179656 | tf_op jit(solution)/shard_map/ppermute | solution.py:226
  72.0 2.4 %collective-permute-done.2 = bf16[96,2048]{1,0:T(8,128)(2,1)S(1)} collective-permute-done((bf16[96,2048]{1,0:T(8,128)(2,1)S(1)}, bf16[96,2048]{1,0:T(8,128)(2,1)S(1)}, u32[]{:S(2)}, u32[]{:S(2)}) %collective-permute-start.2) | collective-permute-done | bytes 393248 | tf_op jit(solution)/shard_map/ppermute | solution.py:226
  74.4 0.1 add_convert_fusion
  74.5 0.1 collective-permute-start.3
  74.6 8.2 %collective-permute-done.4.l1 = bf16[96,2048]{1,0:T(8,128)(2,1)S(1)} collective-permute-done((bf16[96,2048]{1,0:T(8,128)(2,1)S(1)}, bf16[96,2048]{1,0:T(8,128)(2,1)S(1)}, u32[]{:S(2)}, u32[]{:S(2)}) %collective-permute-start.4) | collective-permute-done | bytes 393248 | tf_op jit(solution)/shard_map/ppermute | solution.py:226
  82.7 0.0 collective-permute-done.5.r1
  82.7 1.1 %collective-permute-done.1.l2 = bf16[96,2048]{1,0:T(8,128)(2,1)S(1)} collective-permute-done((bf16[96,2048]{1,0:T(8,128)(2,1)S(1)}, bf16[96,2048]{1,0:T(8,128)(2,1)S(1)}, u32[]{:S(2)}, u32[]{:S(2)}) %collective-permute-start.1) | collective-permute-done | bytes 393248 | tf_op jit(solution)/shard_map/ppermute | solution.py:226
  83.9 3.1 %collective-permute-done.3.r2 = bf16[96,2048]{1,0:T(8,128)(2,1)S(1)} collective-permute-done((bf16[96,2048]{1,0:T(8,128)(2,1)S(1)}, bf16[96,2048]{1,0:T(8,128)(2,1)S(1)}, u32[]{:S(2)}, u32[]{:S(2)}) %collective-permute-start.3) | collective-permute-done | bytes 393248 | tf_op jit(solution)/shard_map/ppermute | solution.py:226
  86.9 0.9 shard_map.68
  87.8 3.4 %collective-permute-start.6 = (bf16[2,48,1024]{2,1,0:T(8,128)(2,1)S(1)}, bf16[2,48,1024]{2,1,0:T(8,128)(2,1)S(1)}, u32[]{:S(2)}, u32[]{:S(2)}) collective-permute-start(bf16[2,48,1024]{2,1,0:T(8,128)(2,1)S(1)} %get-tuple-element.30), channel_id=1, source_target_pairs={{0,1},{1,2},{2,3},{3,4},{4,5},{5,6},{6,7},{7,0},{8,9},{9,10},{10,1... | collective-permute-start | bytes 589832 | tf_op jit(solution)/shard_map/ppermute | solution.py:226
  91.3 2.0 %collective-permute-start.10 = (bf16[48,1024]{1,0:T(8,128)(2,1)S(1)}, bf16[48,1024]{1,0:T(8,128)(2,1)S(1)}, u32[]{:S(2)}, u32[]{:S(2)}) collective-permute-start(bf16[48,1024]{1,0:T(8,128)(2,1)S(1)} %get-tuple-element.33), channel_id=1, source_target_pairs={{0,4},{1,5},{2,6},{3,7},{4,0},{5,1},{6,2},{7,3},{8,12},{9,13},{10,... | collective-permute-start | bytes 294920 | tf_op jit(solution)/shard_map/ppermute | solution.py:226
  93.3 1.7 %collective-permute-start.8 = (bf16[2,48,1024]{2,1,0:T(8,128)(2,1)S(1)}, bf16[2,48,1024]{2,1,0:T(8,128)(2,1)S(1)}, u32[]{:S(2)}, u32[]{:S(2)}) collective-permute-start(bf16[2,48,1024]{2,1,0:T(8,128)(2,1)S(1)} %get-tuple-element.32), channel_id=1, source_target_pairs={{0,7},{1,0},{2,1},{3,2},{4,3},{5,4},{6,5},{7,6},{8,15},{9,8},{10,9... | collective-permute-start | bytes 589832 | tf_op jit(solution)/shard_map/ppermute | solution.py:226
  95.0 3.7 %collective-permute-done.6.odd_up = bf16[2,48,1024]{2,1,0:T(8,128)(2,1)S(1)} collective-permute-done((bf16[2,48,1024]{2,1,0:T(8,128)(2,1)S(1)}, bf16[2,48,1024]{2,1,0:T(8,128)(2,1)S(1)}, u32[]{:S(2)}, u32[]{:S(2)}) %collective-permute-start.6) | collective-permute-done | bytes 196640 | tf_op jit(solution)/shard_map/ppermute | solution.py:226
  98.7 0.7 collective-permute-start.7
  99.4 2.0 %collective-permute-done.8.odd_down = bf16[2,48,1024]{2,1,0:T(8,128)(2,1)S(1)} collective-permute-done((bf16[2,48,1024]{2,1,0:T(8,128)(2,1)S(1)}, bf16[2,48,1024]{2,1,0:T(8,128)(2,1)S(1)}, u32[]{:S(2)}, u32[]{:S(2)}) %collective-permute-start.8) | collective-permute-done | bytes 196640 | tf_op jit(solution)/shard_map/ppermute | solution.py:226
  101.5 2.4 %collective-permute-start.9 = (bf16[48,1024]{1,0:T(8,128)(2,1)S(1)}, bf16[48,1024]{1,0:T(8,128)(2,1)S(1)}, u32[]{:S(2)}, u32[]{:S(2)}) collective-permute-start(bf16[48,1024]{1,0:T(8,128)(2,1)S(1)} %fusion), channel_id=1, source_target_pairs={{0,6},{1,7},{2,0},{3,1},{4,2},{5,3},{6,4},{7,5},{8,14},{9,15},{10,... | collective-permute-start | bytes 294920 | tf_op jit(solution)/shard_map/ppermute | solution.py:226
  103.9 0.0 collective-permute-done.10.across
  103.9 2.8 %collective-permute-done.7.up = bf16[48,1024]{1,0:T(8,128)(2,1)S(1)} collective-permute-done((bf16[48,1024]{1,0:T(8,128)(2,1)S(1)}, bf16[48,1024]{1,0:T(8,128)(2,1)S(1)}, u32[]{:S(2)}, u32[]{:S(2)}) %collective-permute-start.7) | collective-permute-done | bytes 98336 | tf_op jit(solution)/shard_map/ppermute | solution.py:226
  106.7 1.5 %collective-permute-done.9.down = bf16[48,1024]{1,0:T(8,128)(2,1)S(1)} collective-permute-done((bf16[48,1024]{1,0:T(8,128)(2,1)S(1)}, bf16[48,1024]{1,0:T(8,128)(2,1)S(1)}, u32[]{:S(2)}, u32[]{:S(2)}) %collective-permute-start.9) | collective-permute-done | bytes 98336 | tf_op jit(solution)/shard_map/ppermute | solution.py:226
  108.1 0.8 shard_map.69
  (3 shorter events, 0.1 us)
Async XLA Ops:
  4.6 11.7 %copy-start = (s32[384]{0:T(512)S(1)}, s32[384]{0:T(512)}, u32[]{:S(2)}) copy-start(s32[384]{0:T(512)} %param.10) | copy-start | bytes 4612
  4.6 48.8 %all-to-all-start = ((bf16[32,192,128]{2,1,0:T(8,128)(2,1)}), bf16[32,192,128]{2,1,0:T(8,128)(2,1)S(1)}, u32[]{:S(2)}, u32[]{:S(2)}) async-start(bf16[32,192,128]{2,1,0:T(8,128)(2,1)} %shard_map.64), calls=%async_computation | async-start | bytes 3145728 | tf_op jit(solution)/shard_map/all_to_all | solution.py:279
  58.6 10.7 %collective-permute-start = (bf16[96,2048]{1,0:T(8,128)(2,1)S(1)}, bf16[96,2048]{1,0:T(8,128)(2,1)S(1)}, u32[]{:S(2)}, u32[]{:S(2)}) collective-permute-start(bf16[96,2048]{1,0:T(8,128)(2,1)S(1)} %get-tuple-element.21), channel_id=1, source_target_pairs={{0,8},{8,16},{16,24},{24,0},{1,9},{9,17},{17,25},{25,1},{2,10},{10... | collective-permute-start | bytes 1179656 | tf_op jit(solution)/shard_map/ppermute | solution.py:226
  61.1 13.3 %collective-permute-start.2 = (bf16[96,2048]{1,0:T(8,128)(2,1)S(1)}, bf16[96,2048]{1,0:T(8,128)(2,1)S(1)}, u32[]{:S(2)}, u32[]{:S(2)}) collective-permute-start(bf16[96,2048]{1,0:T(8,128)(2,1)S(1)} %get-tuple-element.23), channel_id=1, source_target_pairs={{0,24},{8,0},{16,8},{24,16},{1,25},{9,1},{17,9},{25,17},{2,26},{10... | collective-permute-start | bytes 1179656 | tf_op jit(solution)/shard_map/ppermute | solution.py:226
  65.2 17.5 %collective-permute-start.4 = (bf16[96,2048]{1,0:T(8,128)(2,1)S(1)}, bf16[96,2048]{1,0:T(8,128)(2,1)S(1)}, u32[]{:S(2)}, u32[]{:S(2)}) collective-permute-start(bf16[96,2048]{1,0:T(8,128)(2,1)S(1)} %get-tuple-element.25), channel_id=1, source_target_pairs={{0,24},{8,0},{16,8},{24,16},{1,25},{9,1},{17,9},{25,17},{2,26},{10... | collective-permute-start | bytes 1179656 | tf_op jit(solution)/shard_map/ppermute | solution.py:226
  65.4 17.3 %collective-permute-start.5 = (bf16[96,2048]{1,0:T(8,128)(2,1)S(1)}, bf16[96,2048]{1,0:T(8,128)(2,1)S(1)}, u32[]{:S(2)}, u32[]{:S(2)}) collective-permute-start(bf16[96,2048]{1,0:T(8,128)(2,1)S(1)} %get-tuple-element.26), channel_id=1, source_target_pairs={{0,8},{8,16},{16,24},{24,0},{1,9},{9,17},{17,25},{25,1},{2,10},{10... | collective-permute-start | bytes 1179656 | tf_op jit(solution)/shard_map/ppermute | solution.py:226
  69.4 14.5 %collective-permute-start.1 = (bf16[96,2048]{1,0:T(8,128)(2,1)S(1)}, bf16[96,2048]{1,0:T(8,128)(2,1)S(1)}, u32[]{:S(2)}, u32[]{:S(2)}) collective-permute-start(bf16[96,2048]{1,0:T(8,128)(2,1)S(1)} %add_convert_fusion.1), channel_id=1, source_target_pairs={{0,8},{8,16},{16,24},{24,0},{1,9},{9,17},{17,25},{25,1},{2,10},{10... | collective-permute-start | bytes 1179656 | tf_op jit(solution)/shard_map/ppermute | solution.py:226
  74.5 12.5 %collective-permute-start.3 = (bf16[96,2048]{1,0:T(8,128)(2,1)S(1)}, bf16[96,2048]{1,0:T(8,128)(2,1)S(1)}, u32[]{:S(2)}, u32[]{:S(2)}) collective-permute-start(bf16[96,2048]{1,0:T(8,128)(2,1)S(1)} %add_convert_fusion), channel_id=1, source_target_pairs={{0,24},{8,0},{16,8},{24,16},{1,25},{9,1},{17,9},{25,17},{2,26},{10... | collective-permute-start | bytes 1179656 | tf_op jit(solution)/shard_map/ppermute | solution.py:226
  87.8 10.9 %collective-permute-start.6 = (bf16[2,48,1024]{2,1,0:T(8,128)(2,1)S(1)}, bf16[2,48,1024]{2,1,0:T(8,128)(2,1)S(1)}, u32[]{:S(2)}, u32[]{:S(2)}) collective-permute-start(bf16[2,48,1024]{2,1,0:T(8,128)(2,1)S(1)} %get-tuple-element.30), channel_id=1, source_target_pairs={{0,1},{1,2},{2,3},{3,4},{4,5},{5,6},{6,7},{7,0},{8,9},{9,10},{10,1... | collective-permute-start | bytes 589832 | tf_op jit(solution)/shard_map/ppermute | solution.py:226
  91.3 12.6 %collective-permute-start.10 = (bf16[48,1024]{1,0:T(8,128)(2,1)S(1)}, bf16[48,1024]{1,0:T(8,128)(2,1)S(1)}, u32[]{:S(2)}, u32[]{:S(2)}) collective-permute-start(bf16[48,1024]{1,0:T(8,128)(2,1)S(1)} %get-tuple-element.33), channel_id=1, source_target_pairs={{0,4},{1,5},{2,6},{3,7},{4,0},{5,1},{6,2},{7,3},{8,12},{9,13},{10,... | collective-permute-start | bytes 294920 | tf_op jit(solution)/shard_map/ppermute | solution.py:226
  93.3 8.2 %collective-permute-start.8 = (bf16[2,48,1024]{2,1,0:T(8,128)(2,1)S(1)}, bf16[2,48,1024]{2,1,0:T(8,128)(2,1)S(1)}, u32[]{:S(2)}, u32[]{:S(2)}) collective-permute-start(bf16[2,48,1024]{2,1,0:T(8,128)(2,1)S(1)} %get-tuple-element.32), channel_id=1, source_target_pairs={{0,7},{1,0},{2,1},{3,2},{4,3},{5,4},{6,5},{7,6},{8,15},{9,8},{10,9... | collective-permute-start | bytes 589832 | tf_op jit(solution)/shard_map/ppermute | solution.py:226
  98.7 8.0 %collective-permute-start.7 = (bf16[48,1024]{1,0:T(8,128)(2,1)S(1)}, bf16[48,1024]{1,0:T(8,128)(2,1)S(1)}, u32[]{:S(2)}, u32[]{:S(2)}) collective-permute-start(bf16[48,1024]{1,0:T(8,128)(2,1)S(1)} %fusion.1), channel_id=1, source_target_pairs={{0,2},{1,3},{2,4},{3,5},{4,6},{5,7},{6,0},{7,1},{8,10},{9,11},{10,... | collective-permute-start | bytes 294920 | tf_op jit(solution)/shard_map/ppermute | solution.py:226
  101.5 6.7 %collective-permute-start.9 = (bf16[48,1024]{1,0:T(8,128)(2,1)S(1)}, bf16[48,1024]{1,0:T(8,128)(2,1)S(1)}, u32[]{:S(2)}, u32[]{:S(2)}) collective-permute-start(bf16[48,1024]{1,0:T(8,128)(2,1)S(1)} %fusion), channel_id=1, source_target_pairs={{0,6},{1,7},{2,0},{3,1},{4,2},{5,3},{6,4},{7,5},{8,14},{9,15},{10,... | collective-permute-start | bytes 294920 | tf_op jit(solution)/shard_map/ppermute | solution.py:226

commit v9 on v8

--- a/solution.py
+++ b/solution.py
@@ -259,6 +259,7 @@
     odd_up = shift(odd_up, "pz", NZ, 1)
     odd_down = shift(odd_down, "pz", NZ, -1)
     across = shift(across, "pz", NZ, 4)
+    odd_up, odd_down = lax.optimization_barrier((odd_up, odd_down))
     up = shift(add(up, odd_up[1]), "pz", NZ, 2)
     down = shift(add(down, odd_down[1]), "pz", NZ, -2)
     return up, down, odd_up, odd_down, across, own

time: 110 us -> 110 us (level)
  no operation moved by 1% of the time
where the time goes in v9:
time: 110 us; the launch traced here: 108 us
  waiting for transfers between devices  49.7 us (45%)
  starting transfers between devices  30.5 us (28%)
  Pallas kernels  27.9 us (25%)
    ppermute x11, waiting for transfers between devices, shift(): return lax.ppermute(x, axis, [(i, (i + by) % size) for i in range(size)])  25 us
    all_to_all x1, waiting for transfers between devices, local(): lax.all_to_all(grads(q_fact, p_fact, q_cot, p_cot), ('px', 'pz'), 0, 0, t...  24.7 us
    ppermute x11, starting transfers between devices, shift(): return lax.ppermute(x, axis, [(i, (i + by) % size) for i in range(size)])  18.8 us
    pallas_call x1, Pallas kernels, permuted(): call(kernel, array(12, G, KV), 2 * G * G * K, 16000000, vmem=57, in_specs...  12.3 us
    all_to_all x1, starting transfers between devices, local(): lax.all_to_all(grads(q_fact, p_fact, q_cot, p_cot), ('px', 'pz'), 0, 0, t...  11.7 us
    pallas_call x1, Pallas kernels, product_far(): call(kernel, [array(PAIRS, G)] + [array(ROWS, K // 2)] * 4, 2500000000, 1...  5.12 us
    pallas_call x1, Pallas kernels, grads(): call(kernel, array(N, 2 * ROWS, 128), 800000000, 5500000, vmem=60, grid=(...  4.62 us
    pallas_call x1, Pallas kernels, product_near(): call(kernel, [array(ROWS, K // 2)] * 4, 1700000000, 10000000, vmem=44, in...  4.08 us
  transfers between devices with their start and end apart: 12, of which 10 were waited for; matrix products, arithmetic and copies ran while one was open for 0% of the time, Pallas kernels for 15%

profile of v9, /device:TPU:14, one launch (start us, length us, event | category | flops | bytes accessed | tf_op | source)
XLA Modules:
  0.0 108.5 jit_solution(14821943658993100864)
XLA Ops:
  0.0 4.6 %shard_map.64 = bf16[32,192,128]{2,1,0:T(8,128)(2,1)} custom-call(bf16[32,384]{1,0:T(8,128)(2,1)} %bitcast.9, bf16[32,576]{1,0:T(8,128)(2,1)} %bitcast.8, bf16[384,2048]{1,0:T(8,128)(2,1)} %q_cot.1, bf16[576,2048]{1,0:T(8,128)(2,1)} %p_cot.1), custom_call_target="tpu_custom_call" | custom-call | flops 800000000 | bytes 5500000 | tf_op jit(solution)/shard_map/pallas_call | solution.py:83
  4.6 0.0 copy-start
  4.6 11.7 %all-to-all-start = ((bf16[32,192,128]{2,1,0:T(8,128)(2,1)}), bf16[32,192,128]{2,1,0:T(8,128)(2,1)S(1)}, u32[]{:S(2)}, u32[]{:S(2)}) async-start(bf16[32,192,128]{2,1,0:T(8,128)(2,1)} %shard_map.64), calls=%async_computation | async-start | bytes 3145728 | tf_op jit(solution)/shard_map/all_to_all | solution.py:280
  16.4 0.0 copy-done
  16.4 12.3 %shard_map.65.proj = bf16[12,1024,1024]{2,1,0:T(8,128)(2,1)} custom-call(bf16[1024,4096]{1,0:T(8,128)(2,1)} %proj.1), custom_call_target="tpu_custom_call" | custom-call | flops 8589934592 | bytes 16000000 | tf_op jit(solution)/shard_map/pallas_call | solution.py:123
  28.7 24.7 %all-to-all-done.recv = bf16[32,192,128]{2,1,0:T(8,128)(2,1)S(1)} async-done(((bf16[32,192,128]{2,1,0:T(8,128)(2,1)}), bf16[32,192,128]{2,1,0:T(8,128)(2,1)S(1)}, u32[]{:S(2)}, u32[]{:S(2)}) %all-to-all-start) | async-done | bytes 1572896 | tf_op jit(solution)/shard_map/all_to_all | solution.py:280
  53.5 5.1 %shard_map.66 = (bf16[384,1024]{1,0:T(8,128)(2,1)S(1)}, bf16[96,2048]{1,0:T(8,128)(2,1)S(1)}, bf16[96,2048]{1,0:T(8,128)(2,1)S(1)}, bf16[96,2048]{1,0:T(8,128)(2,1)S(1)}, bf16[96,2048]{1,0:T(8,128)(2,1)S(1)}) custom-call(bf16[32,192,128]{2,1,0:T(8,128)(2,1)S(1)} %all-to-all-done.recv, s32[1,384]{1,0:T(1,128)S(1)} %reshape.7.passage, ...), custom_call_target="tpu_custom_call" | custom-call | flops 2500000000 | bytes 12000000 | tf_op jit(solution)/shard_map/pallas_call | solution.py:192
  58.6 2.5 %collective-permute-start = (bf16[96,2048]{1,0:T(8,128)(2,1)S(1)}, bf16[96,2048]{1,0:T(8,128)(2,1)S(1)}, u32[]{:S(2)}, u32[]{:S(2)}) collective-permute-start(bf16[96,2048]{1,0:T(8,128)(2,1)S(1)} %get-tuple-element.23), channel_id=1, source_target_pairs={{0,8},{8,16},{16,24},{24,0},{1,9},{9,17},{17,25},{25,1},{2,10},{10... | collective-permute-start | bytes 1179656 | tf_op jit(solution)/shard_map/ppermute | solution.py:226
  61.1 0.0 collective-permute-start.2
  61.1 4.1 %shard_map.67 = (bf16[96,2048]{1,0:T(8,128)(2,1)S(1)}, bf16[96,2048]{1,0:T(8,128)(2,1)S(1)}, bf16[96,2048]{1,0:T(8,128)(2,1)S(1)}, bf16[96,2048]{1,0:T(8,128)(2,1)S(1)}) custom-call(bf16[384,1024]{1,0:T(8,128)(2,1)S(1)} %get-tuple-element.26.pair, bf16[12,1024,1024]{2,1,0:T(8,128)(2,1)} %shard_map.65.proj), custom_call_target="tpu_custom_call" | custom-call | flops 1700000000 | bytes 10000000 | tf_op jit(solution)/shard_map/pallas_call | solution.py:210
  65.2 0.2 collective-permute-start.4
  65.4 3.2 %collective-permute-start.5 = (bf16[96,2048]{1,0:T(8,128)(2,1)S(1)}, bf16[96,2048]{1,0:T(8,128)(2,1)S(1)}, u32[]{:S(2)}, u32[]{:S(2)}) collective-permute-start(bf16[96,2048]{1,0:T(8,128)(2,1)S(1)} %get-tuple-element.28), channel_id=1, source_target_pairs={{0,8},{8,16},{16,24},{24,0},{1,9},{9,17},{17,25},{25,1},{2,10},{10... | collective-permute-start | bytes 1179656 | tf_op jit(solution)/shard_map/ppermute | solution.py:226
  68.6 0.7 collective-permute-done
  69.3 0.1 add_convert_fusion.1
  69.4 2.6 %collective-permute-start.1 = (bf16[96,2048]{1,0:T(8,128)(2,1)S(1)}, bf16[96,2048]{1,0:T(8,128)(2,1)S(1)}, u32[]{:S(2)}, u32[]{:S(2)}) collective-permute-start(bf16[96,2048]{1,0:T(8,128)(2,1)S(1)} %add_convert_fusion.1), channel_id=1, source_target_pairs={{0,8},{8,16},{16,24},{24,0},{1,9},{9,17},{17,25},{25,1},{2,10},{10... | collective-permute-start | bytes 1179656 | tf_op jit(solution)/shard_map/ppermute | solution.py:226
  72.0 2.4 %collective-permute-done.2 = bf16[96,2048]{1,0:T(8,128)(2,1)S(1)} collective-permute-done((bf16[96,2048]{1,0:T(8,128)(2,1)S(1)}, bf16[96,2048]{1,0:T(8,128)(2,1)S(1)}, u32[]{:S(2)}, u32[]{:S(2)}) %collective-permute-start.2) | collective-permute-done | bytes 393248 | tf_op jit(solution)/shard_map/ppermute | solution.py:226
  74.4 0.1 add_convert_fusion
  74.5 0.1 collective-permute-start.3
  74.6 8.2 %collective-permute-done.4.l1 = bf16[96,2048]{1,0:T(8,128)(2,1)S(1)} collective-permute-done((bf16[96,2048]{1,0:T(8,128)(2,1)S(1)}, bf16[96,2048]{1,0:T(8,128)(2,1)S(1)}, u32[]{:S(2)}, u32[]{:S(2)}) %collective-permute-start.4) | collective-permute-done | bytes 393248 | tf_op jit(solution)/shard_map/ppermute | solution.py:226
  82.7 0.0 collective-permute-done.5.r1
  82.7 1.1 %collective-permute-done.1.l2 = bf16[96,2048]{1,0:T(8,128)(2,1)S(1)} collective-permute-done((bf16[96,2048]{1,0:T(8,128)(2,1)S(1)}, bf16[96,2048]{1,0:T(8,128)(2,1)S(1)}, u32[]{:S(2)}, u32[]{:S(2)}) %collective-permute-start.1) | collective-permute-done | bytes 393248 | tf_op jit(solution)/shard_map/ppermute | solution.py:226
  83.9 3.1 %collective-permute-done.3.r2 = bf16[96,2048]{1,0:T(8,128)(2,1)S(1)} collective-permute-done((bf16[96,2048]{1,0:T(8,128)(2,1)S(1)}, bf16[96,2048]{1,0:T(8,128)(2,1)S(1)}, u32[]{:S(2)}, u32[]{:S(2)}) %collective-permute-start.3) | collective-permute-done | bytes 393248 | tf_op jit(solution)/shard_map/ppermute | solution.py:226
  86.9 0.9 shard_map.68
  87.8 3.4 %collective-permute-start.6 = (bf16[2,48,1024]{2,1,0:T(8,128)(2,1)S(1)}, bf16[2,48,1024]{2,1,0:T(8,128)(2,1)S(1)}, u32[]{:S(2)}, u32[]{:S(2)}) collective-permute-start(bf16[2,48,1024]{2,1,0:T(8,128)(2,1)S(1)} %get-tuple-element.32), channel_id=1, source_target_pairs={{0,1},{1,2},{2,3},{3,4},{4,5},{5,6},{6,7},{7,0},{8,9},{9,10},{10,1... | collective-permute-start | bytes 589832 | tf_op jit(solution)/shard_map/ppermute | solution.py:226
  91.3 0.1 collective-permute-start.7
  91.4 3.6 %collective-permute-start.10 = (bf16[48,1024]{1,0:T(8,128)(2,1)S(1)}, bf16[48,1024]{1,0:T(8,128)(2,1)S(1)}, u32[]{:S(2)}, u32[]{:S(2)}) collective-permute-start(bf16[48,1024]{1,0:T(8,128)(2,1)S(1)} %get-tuple-element.37), channel_id=1, source_target_pairs={{0,4},{1,5},{2,6},{3,7},{4,0},{5,1},{6,2},{7,3},{8,12},{9,13},{10,... | collective-permute-start | bytes 294920 | tf_op jit(solution)/shard_map/ppermute | solution.py:226
  95.0 1.7 %collective-permute-done.6.odd_up = bf16[2,48,1024]{2,1,0:T(8,128)(2,1)S(1)} collective-permute-done((bf16[2,48,1024]{2,1,0:T(8,128)(2,1)S(1)}, bf16[2,48,1024]{2,1,0:T(8,128)(2,1)S(1)}, u32[]{:S(2)}, u32[]{:S(2)}) %collective-permute-start.6) | collective-permute-done | bytes 196640 | tf_op jit(solution)/shard_map/ppermute | solution.py:226
  96.7 4.0 %collective-permute-done.7.odd_down = bf16[2,48,1024]{2,1,0:T(8,128)(2,1)S(1)} collective-permute-done((bf16[2,48,1024]{2,1,0:T(8,128)(2,1)S(1)}, bf16[2,48,1024]{2,1,0:T(8,128)(2,1)S(1)}, u32[]{:S(2)}, u32[]{:S(2)}) %collective-permute-start.7) | collective-permute-done | bytes 196640 | tf_op jit(solution)/shard_map/ppermute | solution.py:226
  100.7 0.1 collective-permute-start.9
  100.9 3.0 %collective-permute-start.8 = (bf16[48,1024]{1,0:T(8,128)(2,1)S(1)}, bf16[48,1024]{1,0:T(8,128)(2,1)S(1)}, u32[]{:S(2)}, u32[]{:S(2)}) collective-permute-start(bf16[48,1024]{1,0:T(8,128)(2,1)S(1)} %fusion.1), channel_id=1, source_target_pairs={{0,2},{1,3},{2,4},{3,5},{4,6},{5,7},{6,0},{7,1},{8,10},{9,11},{10,... | collective-permute-start | bytes 294920 | tf_op jit(solution)/shard_map/ppermute | solution.py:226
  103.8 0.0 collective-permute-done.10.across
  103.8 2.6 %collective-permute-done.9.down = bf16[48,1024]{1,0:T(8,128)(2,1)S(1)} collective-permute-done((bf16[48,1024]{1,0:T(8,128)(2,1)S(1)}, bf16[48,1024]{1,0:T(8,128)(2,1)S(1)}, u32[]{:S(2)}, u32[]{:S(2)}) %collective-permute-start.9) | collective-permute-done | bytes 98336 | tf_op jit(solution)/shard_map/ppermute | solution.py:226
  106.4 1.3 %collective-permute-done.8.up = bf16[48,1024]{1,0:T(8,128)(2,1)S(1)} collective-permute-done((bf16[48,1024]{1,0:T(8,128)(2,1)S(1)}, bf16[48,1024]{1,0:T(8,128)(2,1)S(1)}, u32[]{:S(2)}, u32[]{:S(2)}) %collective-permute-start.8) | collective-permute-done | bytes 98336 | tf_op jit(solution)/shard_map/ppermute | solution.py:226
  107.7 0.8 shard_map.69
  (3 shorter events, 0.1 us)
Async XLA Ops:
  4.6 11.7 %copy-start = (s32[384]{0:T(512)S(1)}, s32[384]{0:T(512)}, u32[]{:S(2)}) copy-start(s32[384]{0:T(512)} %param.10) | copy-start | bytes 4612
  4.6 48.8 %all-to-all-start = ((bf16[32,192,128]{2,1,0:T(8,128)(2,1)}), bf16[32,192,128]{2,1,0:T(8,128)(2,1)S(1)}, u32[]{:S(2)}, u32[]{:S(2)}) async-start(bf16[32,192,128]{2,1,0:T(8,128)(2,1)} %shard_map.64), calls=%async_computation | async-start | bytes 3145728 | tf_op jit(solution)/shard_map/all_to_all | solution.py:280
  58.6 10.7 %collective-permute-start = (bf16[96,2048]{1,0:T(8,128)(2,1)S(1)}, bf16[96,2048]{1,0:T(8,128)(2,1)S(1)}, u32[]{:S(2)}, u32[]{:S(2)}) collective-permute-start(bf16[96,2048]{1,0:T(8,128)(2,1)S(1)} %get-tuple-element.23), channel_id=1, source_target_pairs={{0,8},{8,16},{16,24},{24,0},{1,9},{9,17},{17,25},{25,1},{2,10},{10... | collective-permute-start | bytes 1179656 | tf_op jit(solution)/shard_map/ppermute | solution.py:226
  61.1 13.3 %collective-permute-start.2 = (bf16[96,2048]{1,0:T(8,128)(2,1)S(1)}, bf16[96,2048]{1,0:T(8,128)(2,1)S(1)}, u32[]{:S(2)}, u32[]{:S(2)}) collective-permute-start(bf16[96,2048]{1,0:T(8,128)(2,1)S(1)} %get-tuple-element.25), channel_id=1, source_target_pairs={{0,24},{8,0},{16,8},{24,16},{1,25},{9,1},{17,9},{25,17},{2,26},{10... | collective-permute-start | bytes 1179656 | tf_op jit(solution)/shard_map/ppermute | solution.py:226
  65.2 17.5 %collective-permute-start.4 = (bf16[96,2048]{1,0:T(8,128)(2,1)S(1)}, bf16[96,2048]{1,0:T(8,128)(2,1)S(1)}, u32[]{:S(2)}, u32[]{:S(2)}) collective-permute-start(bf16[96,2048]{1,0:T(8,128)(2,1)S(1)} %get-tuple-element.27), channel_id=1, source_target_pairs={{0,24},{8,0},{16,8},{24,16},{1,25},{9,1},{17,9},{25,17},{2,26},{10... | collective-permute-start | bytes 1179656 | tf_op jit(solution)/shard_map/ppermute | solution.py:226
  65.4 17.3 %collective-permute-start.5 = (bf16[96,2048]{1,0:T(8,128)(2,1)S(1)}, bf16[96,2048]{1,0:T(8,128)(2,1)S(1)}, u32[]{:S(2)}, u32[]{:S(2)}) collective-permute-start(bf16[96,2048]{1,0:T(8,128)(2,1)S(1)} %get-tuple-element.28), channel_id=1, source_target_pairs={{0,8},{8,16},{16,24},{24,0},{1,9},{9,17},{17,25},{25,1},{2,10},{10... | collective-permute-start | bytes 1179656 | tf_op jit(solution)/shard_map/ppermute | solution.py:226
  69.4 14.5 %collective-permute-start.1 = (bf16[96,2048]{1,0:T(8,128)(2,1)S(1)}, bf16[96,2048]{1,0:T(8,128)(2,1)S(1)}, u32[]{:S(2)}, u32[]{:S(2)}) collective-permute-start(bf16[96,2048]{1,0:T(8,128)(2,1)S(1)} %add_convert_fusion.1), channel_id=1, source_target_pairs={{0,8},{8,16},{16,24},{24,0},{1,9},{9,17},{17,25},{25,1},{2,10},{10... | collective-permute-start | bytes 1179656 | tf_op jit(solution)/shard_map/ppermute | solution.py:226
  74.5 12.5 %collective-permute-start.3 = (bf16[96,2048]{1,0:T(8,128)(2,1)S(1)}, bf16[96,2048]{1,0:T(8,128)(2,1)S(1)}, u32[]{:S(2)}, u32[]{:S(2)}) collective-permute-start(bf16[96,2048]{1,0:T(8,128)(2,1)S(1)} %add_convert_fusion), channel_id=1, source_target_pairs={{0,24},{8,0},{16,8},{24,16},{1,25},{9,1},{17,9},{25,17},{2,26},{10... | collective-permute-start | bytes 1179656 | tf_op jit(solution)/shard_map/ppermute | solution.py:226
  87.8 8.8 %collective-permute-start.6 = (bf16[2,48,1024]{2,1,0:T(8,128)(2,1)S(1)}, bf16[2,48,1024]{2,1,0:T(8,128)(2,1)S(1)}, u32[]{:S(2)}, u32[]{:S(2)}) collective-permute-start(bf16[2,48,1024]{2,1,0:T(8,128)(2,1)S(1)} %get-tuple-element.32), channel_id=1, source_target_pairs={{0,1},{1,2},{2,3},{3,4},{4,5},{5,6},{6,7},{7,0},{8,9},{9,10},{10,1... | collective-permute-start | bytes 589832 | tf_op jit(solution)/shard_map/ppermute | solution.py:226
  91.3 9.4 %collective-permute-start.7 = (bf16[2,48,1024]{2,1,0:T(8,128)(2,1)S(1)}, bf16[2,48,1024]{2,1,0:T(8,128)(2,1)S(1)}, u32[]{:S(2)}, u32[]{:S(2)}) collective-permute-start(bf16[2,48,1024]{2,1,0:T(8,128)(2,1)S(1)} %get-tuple-element.33), channel_id=1, source_target_pairs={{0,7},{1,0},{2,1},{3,2},{4,3},{5,4},{6,5},{7,6},{8,15},{9,8},{10,9... | collective-permute-start | bytes 589832 | tf_op jit(solution)/shard_map/ppermute | solution.py:226
  91.4 12.5 %collective-permute-start.10 = (bf16[48,1024]{1,0:T(8,128)(2,1)S(1)}, bf16[48,1024]{1,0:T(8,128)(2,1)S(1)}, u32[]{:S(2)}, u32[]{:S(2)}) collective-permute-start(bf16[48,1024]{1,0:T(8,128)(2,1)S(1)} %get-tuple-element.37), channel_id=1, source_target_pairs={{0,4},{1,5},{2,6},{3,7},{4,0},{5,1},{6,2},{7,3},{8,12},{9,13},{10,... | collective-permute-start | bytes 294920 | tf_op jit(solution)/shard_map/ppermute | solution.py:226
  100.7 5.7 %collective-permute-start.9 = (bf16[48,1024]{1,0:T(8,128)(2,1)S(1)}, bf16[48,1024]{1,0:T(8,128)(2,1)S(1)}, u32[]{:S(2)}, u32[]{:S(2)}) collective-permute-start(bf16[48,1024]{1,0:T(8,128)(2,1)S(1)} %fusion), channel_id=1, source_target_pairs={{0,6},{1,7},{2,0},{3,1},{4,2},{5,3},{6,4},{7,5},{8,14},{9,15},{10,... | collective-permute-start | bytes 294920 | tf_op jit(solution)/shard_map/ppermute | solution.py:226
  100.9 6.9 %collective-permute-start.8 = (bf16[48,1024]{1,0:T(8,128)(2,1)S(1)}, bf16[48,1024]{1,0:T(8,128)(2,1)S(1)}, u32[]{:S(2)}, u32[]{:S(2)}) collective-permute-start(bf16[48,1024]{1,0:T(8,128)(2,1)S(1)} %fusion.1), channel_id=1, source_target_pairs={{0,2},{1,3},{2,4},{3,5},{4,6},{5,7},{6,0},{7,1},{8,10},{9,11},{10,... | collective-permute-start | bytes 294920 | tf_op jit(solution)/shard_map/ppermute | solution.py:226

commit v10 on v8

--- a/solution.py
+++ b/solution.py
@@ -239,7 +239,7 @@
 
 
 def across_z(terms):
-    def kernel(l2, r2, l1, r1, l0, r0, odd_up, odd_down, own, up, down, across):
+    def kernel(l2, r2, l1, r1, l0, r0, odd_up, odd_down, own, up, down, far_up, far_down):
         left = (l0[...].astype(F32) + l1[...].astype(F32) + l2[...].astype(F32)).astype(BF)
         right = (r0[...].astype(F32) + r1[...].astype(F32) + r2[...].astype(F32)).astype(BF)
         stacked = jnp.concatenate([left[:, :KV], left[:, KV:], right[:, :KV], right[:, KV:]], axis=0)
@@ -250,24 +250,39 @@
         z = (block + lax.axis_index("pz")) & (NZ - 1)
         hot = ones_where(c == quarter * ROWS + z * MINE + item)
         rows = dot(hot, stacked).astype(BF)
-        outs = (own, odd_up.at[0], up, odd_up.at[1], across, odd_down.at[1], down, odd_down.at[0])
+        outs = (own, odd_up.at[0], up, odd_up.at[1], None, odd_down.at[1], down, odd_down.at[0])
         for k, out in enumerate(outs):
-            out[...] = rows[48 * k : 48 * k + 48, :]
-
-    outs = [array(2, 48, KV)] * 2 + [array(48, KV)] * 4
-    odd_up, odd_down, own, up, down, across = call(kernel, outs, 300_000_000, 4_000_000)(*terms)
+            if k != 4:
+                out[...] = rows[48 * k : 48 * k + 48, :]
+        far_up[...] = rows[48 * 4 : 48 * 5, : KV // 2]
+        far_down[...] = rows[48 * 4 : 48 * 5, KV // 2 :]
+
+    outs = [array(2, 48, KV)] * 2 + [array(48, KV)] * 3 + [array(48, KV // 2)] * 2
+    odd_up, odd_down, own, up, down, far_up, far_down = call(kernel, outs, 300_000_000, 4_000_000)(*terms)
     odd_up = shift(odd_up, "pz", NZ, 1)
     odd_down = shift(odd_down, "pz", NZ, -1)
-    across = shift(across, "pz", NZ, 4)
-    up = shift(add(up, odd_up[1]), "pz", NZ, 2)
-    down = shift(add(down, odd_down[1]), "pz", NZ, -2)
-    return up, down, odd_up, odd_down, across, own
+    far_up = shift(far_up, "pz", NZ, 2)
+    far_down = shift(far_down, "pz", NZ, -2)
+
+    def add_kernel(odd_up, odd_down, far_up, far_down, up, down, up_out, down_out):
+        half = KV // 2
+        for near, odd, far, out, first in ((up, odd_up, far_up, up_out, 0), (down, odd_down, far_down, down_out, half)):
+            total = near[...].astype(F32) + odd[1].astype(F32)
+            at, rest = slice(first, first + half), slice(half - first, KV - first)
+            out[:, at] = (total[:, at] + far[...].astype(F32)).astype(BF)
+            out[:, rest] = total[:, rest].astype(BF)
+
+    inputs = (odd_up, odd_down, far_up, far_down, up, down)
+    up, down = call(add_kernel, [array(48, KV)] * 2, 1_000_000, 1_000_000)(*inputs)
+    up = shift(up, "pz", NZ, 2)
+    down = shift(down, "pz", NZ, -2)
+    return up, down, odd_up, odd_down, own
 
 
 def last_sum(parts):
-    def kernel(up, down, odd_up, odd_down, across, own, out):
+    def kernel(up, down, odd_up, odd_down, own, out):
         total = own[...].astype(F32)
-        for term in (odd_up[0], odd_down[0], across[...], up[...], down[...]):
+        for term in (odd_up[0], odd_down[0], up[...], down[...]):
             total = total + term.astype(F32)
         for q in range(4):
             out[:, KV * q : KV * q + KV] = total[MINE * q : MINE * q + MINE, :]

time: 110 us -> 109 us (level)
  starting transfers between devices: 30.6 us -> 32.2 us
  waiting for transfers between devices: 50.1 us -> 48.6 us
    ppermute x11 -> x12, starting transfers between devices: 18.8 us -> 20.5 us  [shift(): return lax.ppermute(x, axis, [(i, (i + by) % size) for i in range(size)])]
    ppermute x11 -> x12, waiting for transfers between devices: 25.4 us -> 23.9 us  [shift(): return lax.ppermute(x, axis, [(i, (i + by) % size) for i in range(size)])]
  transfers between devices with their start and end apart: 12 -> 13, of which waited for: 10 -> 9; matrix products, arithmetic and copies ran while one was open for 0% -> 0% of each run, Pallas kernels for 15% -> 15%
where the time goes in v10:
time: 109 us
  waiting for transfers between devices  48.6 us (45%)
  starting transfers between devices  32.2 us (30%)
  Pallas kernels  27.9 us (26%)
    all_to_all x1, waiting for transfers between devices, local(): lax.all_to_all(grads(q_fact, p_fact, q_cot, p_cot), ('px', 'pz'), 0, 0, t...  24.7 us
    ppermute x12, waiting for transfers between devices, shift(): return lax.ppermute(x, axis, [(i, (i + by) % size) for i in range(size)])  23.9 us
    ppermute x12, starting transfers between devices, shift(): return lax.ppermute(x, axis, [(i, (i + by) % size) for i in range(size)])  20.5 us
    pallas_call x1, Pallas kernels, permuted(): call(kernel, array(12, G, KV), 2 * G * G * K, 16000000, vmem=57, in_specs...  12.4 us
    all_to_all x1, starting transfers between devices, local(): lax.all_to_all(grads(q_fact, p_fact, q_cot, p_cot), ('px', 'pz'), 0, 0, t...  11.7 us
    pallas_call x1, Pallas kernels, product_far(): call(kernel, [array(PAIRS, G)] + [array(ROWS, K // 2)] * 4, 2500000000, 1...  5.12 us
    pallas_call x1, Pallas kernels, grads(): call(kernel, array(N, 2 * ROWS, 128), 800000000, 5500000, vmem=60, grid=(...  4.6 us
    pallas_call x1, Pallas kernels, product_near(): call(kernel, [array(ROWS, K // 2)] * 4, 1700000000, 10000000, vmem=44, in...  4.08 us
  transfers between devices with their start and end apart: 13, of which 9 were waited for; matrix products, arithmetic and copies ran while one was open for 0% of the time, Pallas kernels for 15%

profile of v10, /device:TPU:14, one launch (start us, length us, event | category | flops | bytes accessed | tf_op | source)
XLA Modules:
  0.0 109.0 jit_solution(17719310840506442673)
XLA Ops:
  0.0 4.6 %shard_map.64 = bf16[32,192,128]{2,1,0:T(8,128)(2,1)} custom-call(bf16[32,384]{1,0:T(8,128)(2,1)} %bitcast.3, bf16[32,576]{1,0:T(8,128)(2,1)} %bitcast.2, bf16[384,2048]{1,0:T(8,128)(2,1)} %q_cot.1, bf16[576,2048]{1,0:T(8,128)(2,1)} %p_cot.1), custom_call_target="tpu_custom_call" | custom-call | flops 800000000 | bytes 5500000 | tf_op jit(solution)/shard_map/pallas_call | solution.py:83
  4.6 0.0 copy-start
  4.6 11.7 %all-to-all-start = ((bf16[32,192,128]{2,1,0:T(8,128)(2,1)}), bf16[32,192,128]{2,1,0:T(8,128)(2,1)S(1)}, u32[]{:S(2)}, u32[]{:S(2)}) async-start(bf16[32,192,128]{2,1,0:T(8,128)(2,1)} %shard_map.64), calls=%async_computation | async-start | bytes 3145728 | tf_op jit(solution)/shard_map/all_to_all | solution.py:294
  16.3 0.0 copy-done
  16.4 12.4 %shard_map.65.proj = bf16[12,1024,1024]{2,1,0:T(8,128)(2,1)} custom-call(bf16[1024,4096]{1,0:T(8,128)(2,1)} %proj.1), custom_call_target="tpu_custom_call" | custom-call | flops 8589934592 | bytes 16000000 | tf_op jit(solution)/shard_map/pallas_call | solution.py:123
  28.7 24.7 %all-to-all-done.recv = bf16[32,192,128]{2,1,0:T(8,128)(2,1)S(1)} async-done(((bf16[32,192,128]{2,1,0:T(8,128)(2,1)}), bf16[32,192,128]{2,1,0:T(8,128)(2,1)S(1)}, u32[]{:S(2)}, u32[]{:S(2)}) %all-to-all-start) | async-done | bytes 1572896 | tf_op jit(solution)/shard_map/all_to_all | solution.py:294
  53.4 5.1 %shard_map.66 = (bf16[384,1024]{1,0:T(8,128)(2,1)S(1)}, bf16[96,2048]{1,0:T(8,128)(2,1)S(1)}, bf16[96,2048]{1,0:T(8,128)(2,1)S(1)}, bf16[96,2048]{1,0:T(8,128)(2,1)S(1)}, bf16[96,2048]{1,0:T(8,128)(2,1)S(1)}) custom-call(bf16[32,192,128]{2,1,0:T(8,128)(2,1)S(1)} %all-to-all-done.recv, s32[1,384]{1,0:T(1,128)S(1)} %reshape.3.passage, ...), custom_call_target="tpu_custom_call" | custom-call | flops 2500000000 | bytes 12000000 | tf_op jit(solution)/shard_map/pallas_call | solution.py:192
  58.6 2.5 %collective-permute-start = (bf16[96,2048]{1,0:T(8,128)(2,1)S(1)}, bf16[96,2048]{1,0:T(8,128)(2,1)S(1)}, u32[]{:S(2)}, u32[]{:S(2)}) collective-permute-start(bf16[96,2048]{1,0:T(8,128)(2,1)S(1)} %get-tuple-element.24), channel_id=1, source_target_pairs={{0,8},{8,16},{16,24},{24,0},{1,9},{9,17},{17,25},{25,1},{2,10},{10... | collective-permute-start | bytes 1179656 | tf_op jit(solution)/shard_map/ppermute | solution.py:226
  61.1 0.0 collective-permute-start.2
  61.1 4.1 %shard_map.67 = (bf16[96,2048]{1,0:T(8,128)(2,1)S(1)}, bf16[96,2048]{1,0:T(8,128)(2,1)S(1)}, bf16[96,2048]{1,0:T(8,128)(2,1)S(1)}, bf16[96,2048]{1,0:T(8,128)(2,1)S(1)}) custom-call(bf16[384,1024]{1,0:T(8,128)(2,1)S(1)} %get-tuple-element.27.pair, bf16[12,1024,1024]{2,1,0:T(8,128)(2,1)} %shard_map.65.proj), custom_call_target="tpu_custom_call" | custom-call | flops 1700000000 | bytes 10000000 | tf_op jit(solution)/shard_map/pallas_call | solution.py:210
  65.2 0.2 collective-permute-start.4
  65.4 3.2 %collective-permute-start.5 = (bf16[96,2048]{1,0:T(8,128)(2,1)S(1)}, bf16[96,2048]{1,0:T(8,128)(2,1)S(1)}, u32[]{:S(2)}, u32[]{:S(2)}) collective-permute-start(bf16[96,2048]{1,0:T(8,128)(2,1)S(1)} %get-tuple-element.29), channel_id=1, source_target_pairs={{0,8},{8,16},{16,24},{24,0},{1,9},{9,17},{17,25},{25,1},{2,10},{10... | collective-permute-start | bytes 1179656 | tf_op jit(solution)/shard_map/ppermute | solution.py:226
  68.6 0.7 collective-permute-done
  69.2 0.1 add_convert_fusion.1
  69.4 2.6 %collective-permute-start.1 = (bf16[96,2048]{1,0:T(8,128)(2,1)S(1)}, bf16[96,2048]{1,0:T(8,128)(2,1)S(1)}, u32[]{:S(2)}, u32[]{:S(2)}) collective-permute-start(bf16[96,2048]{1,0:T(8,128)(2,1)S(1)} %add_convert_fusion.1), channel_id=1, source_target_pairs={{0,8},{8,16},{16,24},{24,0},{1,9},{9,17},{17,25},{25,1},{2,10},{10... | collective-permute-start | bytes 1179656 | tf_op jit(solution)/shard_map/ppermute | solution.py:226
  71.9 2.4 %collective-permute-done.2 = bf16[96,2048]{1,0:T(8,128)(2,1)S(1)} collective-permute-done((bf16[96,2048]{1,0:T(8,128)(2,1)S(1)}, bf16[96,2048]{1,0:T(8,128)(2,1)S(1)}, u32[]{:S(2)}, u32[]{:S(2)}) %collective-permute-start.2) | collective-permute-done | bytes 393248 | tf_op jit(solution)/shard_map/ppermute | solution.py:226
  74.3 0.1 add_convert_fusion
  74.4 0.1 collective-permute-start.3
  74.5 8.2 %collective-permute-done.4.l1 = bf16[96,2048]{1,0:T(8,128)(2,1)S(1)} collective-permute-done((bf16[96,2048]{1,0:T(8,128)(2,1)S(1)}, bf16[96,2048]{1,0:T(8,128)(2,1)S(1)}, u32[]{:S(2)}, u32[]{:S(2)}) %collective-permute-start.4) | collective-permute-done | bytes 393248 | tf_op jit(solution)/shard_map/ppermute | solution.py:226
  82.7 0.0 collective-permute-done.5.r1
  82.7 1.2 %collective-permute-done.1.l2 = bf16[96,2048]{1,0:T(8,128)(2,1)S(1)} collective-permute-done((bf16[96,2048]{1,0:T(8,128)(2,1)S(1)}, bf16[96,2048]{1,0:T(8,128)(2,1)S(1)}, u32[]{:S(2)}, u32[]{:S(2)}) %collective-permute-start.1) | collective-permute-done | bytes 393248 | tf_op jit(solution)/shard_map/ppermute | solution.py:226
  83.9 3.1 %collective-permute-done.3.r2 = bf16[96,2048]{1,0:T(8,128)(2,1)S(1)} collective-permute-done((bf16[96,2048]{1,0:T(8,128)(2,1)S(1)}, bf16[96,2048]{1,0:T(8,128)(2,1)S(1)}, u32[]{:S(2)}, u32[]{:S(2)}) %collective-permute-start.3) | collective-permute-done | bytes 393248 | tf_op jit(solution)/shard_map/ppermute | solution.py:226
  86.9 0.9 shard_map.68
  87.8 3.4 %collective-permute-start.6 = (bf16[2,48,1024]{2,1,0:T(8,128)(2,1)S(1)}, bf16[2,48,1024]{2,1,0:T(8,128)(2,1)S(1)}, u32[]{:S(2)}, u32[]{:S(2)}) collective-permute-start(bf16[2,48,1024]{2,1,0:T(8,128)(2,1)S(1)} %get-tuple-element.32), channel_id=1, source_target_pairs={{0,1},{1,2},{2,3},{3,4},{4,5},{5,6},{6,7},{7,0},{8,9},{9,10},{10,1... | collective-permute-start | bytes 589832 | tf_op jit(solution)/shard_map/ppermute | solution.py:226
  91.3 0.1 collective-permute-start.7
  91.3 1.5 %collective-permute-start.8 = (bf16[48,512]{1,0:T(8,128)(2,1)S(1)}, bf16[48,512]{1,0:T(8,128)(2,1)S(1)}, u32[]{:S(2)}, u32[]{:S(2)}) collective-permute-start(bf16[48,512]{1,0:T(8,128)(2,1)S(1)} %get-tuple-element.34), channel_id=1, source_target_pairs={{0,2},{1,3},{2,4},{3,5},{4,6},{5,7},{6,0},{7,1},{8,10},{9,11},{10,... | collective-permute-start | bytes 147464 | tf_op jit(solution)/shard_map/ppermute | solution.py:226
  92.8 2.6 %collective-permute-start.9 = (bf16[48,512]{1,0:T(8,128)(2,1)S(1)}, bf16[48,512]{1,0:T(8,128)(2,1)S(1)}, u32[]{:S(2)}, u32[]{:S(2)}) collective-permute-start(bf16[48,512]{1,0:T(8,128)(2,1)S(1)} %get-tuple-element.35), channel_id=1, source_target_pairs={{0,6},{1,7},{2,0},{3,1},{4,2},{5,3},{6,4},{7,5},{8,14},{9,15},{10,... | collective-permute-start | bytes 147464 | tf_op jit(solution)/shard_map/ppermute | solution.py:226
  95.5 3.0 %collective-permute-done.8.far_up = bf16[48,512]{1,0:T(8,128)(2,1)S(1)} collective-permute-done((bf16[48,512]{1,0:T(8,128)(2,1)S(1)}, bf16[48,512]{1,0:T(8,128)(2,1)S(1)}, u32[]{:S(2)}, u32[]{:S(2)}) %collective-permute-start.8) | collective-permute-done | bytes 49184 | tf_op jit(solution)/shard_map/ppermute | solution.py:226
  98.4 0.0 collective-permute-done.9.far_down
  98.4 0.0 collective-permute-done.6.odd_up
  98.4 0.0 collective-permute-done.7.odd_down
  98.4 0.1 shard_map.69
  98.5 3.6 %collective-permute-start.10 = (bf16[48,1024]{1,0:T(8,128)(2,1)S(1)}, bf16[48,1024]{1,0:T(8,128)(2,1)S(1)}, u32[]{:S(2)}, u32[]{:S(2)}) collective-permute-start(bf16[48,1024]{1,0:T(8,128)(2,1)S(1)} %get-tuple-element.38), channel_id=1, source_target_pairs={{0,2},{1,3},{2,4},{3,5},{4,6},{5,7},{6,0},{7,1},{8,10},{9,11},{10,... | collective-permute-start | bytes 294920 | tf_op jit(solution)/shard_map/ppermute | solution.py:226
  102.1 0.6 collective-permute-start.11
  102.7 2.7 %collective-permute-done.10.up = bf16[48,1024]{1,0:T(8,128)(2,1)S(1)} collective-permute-done((bf16[48,1024]{1,0:T(8,128)(2,1)S(1)}, bf16[48,1024]{1,0:T(8,128)(2,1)S(1)}, u32[]{:S(2)}, u32[]{:S(2)}) %collective-permute-start.10) | collective-permute-done | bytes 98336 | tf_op jit(solution)/shard_map/ppermute | solution.py:226
  105.4 2.8 %collective-permute-done.11.down = bf16[48,1024]{1,0:T(8,128)(2,1)S(1)} collective-permute-done((bf16[48,1024]{1,0:T(8,128)(2,1)S(1)}, bf16[48,1024]{1,0:T(8,128)(2,1)S(1)}, u32[]{:S(2)}, u32[]{:S(2)}) %collective-permute-start.11) | collective-permute-done | bytes 98336 | tf_op jit(solution)/shard_map/ppermute | solution.py:226
  108.2 0.8 shard_map.70
  (1 shorter events, 0.0 us)
Async XLA Ops:
  4.6 11.7 %copy-start = (s32[384]{0:T(512)S(1)}, s32[384]{0:T(512)}, u32[]{:S(2)}) copy-start(s32[384]{0:T(512)} %param.10) | copy-start | bytes 4612
  4.6 48.8 %all-to-all-start = ((bf16[32,192,128]{2,1,0:T(8,128)(2,1)}), bf16[32,192,128]{2,1,0:T(8,128)(2,1)S(1)}, u32[]{:S(2)}, u32[]{:S(2)}) async-start(bf16[32,192,128]{2,1,0:T(8,128)(2,1)} %shard_map.64), calls=%async_computation | async-start | bytes 3145728 | tf_op jit(solution)/shard_map/all_to_all | solution.py:294
  58.6 10.7 %collective-permute-start = (bf16[96,2048]{1,0:T(8,128)(2,1)S(1)}, bf16[96,2048]{1,0:T(8,128)(2,1)S(1)}, u32[]{:S(2)}, u32[]{:S(2)}) collective-permute-start(bf16[96,2048]{1,0:T(8,128)(2,1)S(1)} %get-tuple-element.24), channel_id=1, source_target_pairs={{0,8},{8,16},{16,24},{24,0},{1,9},{9,17},{17,25},{25,1},{2,10},{10... | collective-permute-start | bytes 1179656 | tf_op jit(solution)/shard_map/ppermute | solution.py:226
  61.1 13.3 %collective-permute-start.2 = (bf16[96,2048]{1,0:T(8,128)(2,1)S(1)}, bf16[96,2048]{1,0:T(8,128)(2,1)S(1)}, u32[]{:S(2)}, u32[]{:S(2)}) collective-permute-start(bf16[96,2048]{1,0:T(8,128)(2,1)S(1)} %get-tuple-element.26), channel_id=1, source_target_pairs={{0,24},{8,0},{16,8},{24,16},{1,25},{9,1},{17,9},{25,17},{2,26},{10... | collective-permute-start | bytes 1179656 | tf_op jit(solution)/shard_map/ppermute | solution.py:226
  65.2 17.5 %collective-permute-start.4 = (bf16[96,2048]{1,0:T(8,128)(2,1)S(1)}, bf16[96,2048]{1,0:T(8,128)(2,1)S(1)}, u32[]{:S(2)}, u32[]{:S(2)}) collective-permute-start(bf16[96,2048]{1,0:T(8,128)(2,1)S(1)} %get-tuple-element.28), channel_id=1, source_target_pairs={{0,24},{8,0},{16,8},{24,16},{1,25},{9,1},{17,9},{25,17},{2,26},{10... | collective-permute-start | bytes 1179656 | tf_op jit(solution)/shard_map/ppermute | solution.py:226
  65.4 17.3 %collective-permute-start.5 = (bf16[96,2048]{1,0:T(8,128)(2,1)S(1)}, bf16[96,2048]{1,0:T(8,128)(2,1)S(1)}, u32[]{:S(2)}, u32[]{:S(2)}) collective-permute-start(bf16[96,2048]{1,0:T(8,128)(2,1)S(1)} %get-tuple-element.29), channel_id=1, source_target_pairs={{0,8},{8,16},{16,24},{24,0},{1,9},{9,17},{17,25},{25,1},{2,10},{10... | collective-permute-start | bytes 1179656 | tf_op jit(solution)/shard_map/ppermute | solution.py:226
  69.4 14.5 %collective-permute-start.1 = (bf16[96,2048]{1,0:T(8,128)(2,1)S(1)}, bf16[96,2048]{1,0:T(8,128)(2,1)S(1)}, u32[]{:S(2)}, u32[]{:S(2)}) collective-permute-start(bf16[96,2048]{1,0:T(8,128)(2,1)S(1)} %add_convert_fusion.1), channel_id=1, source_target_pairs={{0,8},{8,16},{16,24},{24,0},{1,9},{9,17},{17,25},{25,1},{2,10},{10... | collective-permute-start | bytes 1179656 | tf_op jit(solution)/shard_map/ppermute | solution.py:226
  74.4 12.5 %collective-permute-start.3 = (bf16[96,2048]{1,0:T(8,128)(2,1)S(1)}, bf16[96,2048]{1,0:T(8,128)(2,1)S(1)}, u32[]{:S(2)}, u32[]{:S(2)}) collective-permute-start(bf16[96,2048]{1,0:T(8,128)(2,1)S(1)} %add_convert_fusion), channel_id=1, source_target_pairs={{0,24},{8,0},{16,8},{24,16},{1,25},{9,1},{17,9},{25,17},{2,26},{10... | collective-permute-start | bytes 1179656 | tf_op jit(solution)/shard_map/ppermute | solution.py:226
  87.8 10.6 %collective-permute-start.6 = (bf16[2,48,1024]{2,1,0:T(8,128)(2,1)S(1)}, bf16[2,48,1024]{2,1,0:T(8,128)(2,1)S(1)}, u32[]{:S(2)}, u32[]{:S(2)}) collective-permute-start(bf16[2,48,1024]{2,1,0:T(8,128)(2,1)S(1)} %get-tuple-element.32), channel_id=1, source_target_pairs={{0,1},{1,2},{2,3},{3,4},{4,5},{5,6},{6,7},{7,0},{8,9},{9,10},{10,1... | collective-permute-start | bytes 589832 | tf_op jit(solution)/shard_map/ppermute | solution.py:226
  91.3 7.2 %collective-permute-start.7 = (bf16[2,48,1024]{2,1,0:T(8,128)(2,1)S(1)}, bf16[2,48,1024]{2,1,0:T(8,128)(2,1)S(1)}, u32[]{:S(2)}, u32[]{:S(2)}) collective-permute-start(bf16[2,48,1024]{2,1,0:T(8,128)(2,1)S(1)} %get-tuple-element.33), channel_id=1, source_target_pairs={{0,7},{1,0},{2,1},{3,2},{4,3},{5,4},{6,5},{7,6},{8,15},{9,8},{10,9... | collective-permute-start | bytes 589832 | tf_op jit(solution)/shard_map/ppermute | solution.py:226
  91.3 7.1 %collective-permute-start.8 = (bf16[48,512]{1,0:T(8,128)(2,1)S(1)}, bf16[48,512]{1,0:T(8,128)(2,1)S(1)}, u32[]{:S(2)}, u32[]{:S(2)}) collective-permute-start(bf16[48,512]{1,0:T(8,128)(2,1)S(1)} %get-tuple-element.34), channel_id=1, source_target_pairs={{0,2},{1,3},{2,4},{3,5},{4,6},{5,7},{6,0},{7,1},{8,10},{9,11},{10,... | collective-permute-start | bytes 147464 | tf_op jit(solution)/shard_map/ppermute | solution.py:226
  92.8 5.6 %collective-permute-start.9 = (bf16[48,512]{1,0:T(8,128)(2,1)S(1)}, bf16[48,512]{1,0:T(8,128)(2,1)S(1)}, u32[]{:S(2)}, u32[]{:S(2)}) collective-permute-start(bf16[48,512]{1,0:T(8,128)(2,1)S(1)} %get-tuple-element.35), channel_id=1, source_target_pairs={{0,6},{1,7},{2,0},{3,1},{4,2},{5,3},{6,4},{7,5},{8,14},{9,15},{10,... | collective-permute-start | bytes 147464 | tf_op jit(solution)/shard_map/ppermute | solution.py:226
  98.5 6.9 %collective-permute-start.10 = (bf16[48,1024]{1,0:T(8,128)(2,1)S(1)}, bf16[48,1024]{1,0:T(8,128)(2,1)S(1)}, u32[]{:S(2)}, u32[]{:S(2)}) collective-permute-start(bf16[48,1024]{1,0:T(8,128)(2,1)S(1)} %get-tuple-element.38), channel_id=1, source_target_pairs={{0,2},{1,3},{2,4},{3,5},{4,6},{5,7},{6,0},{7,1},{8,10},{9,11},{10,... | collective-permute-start | bytes 294920 | tf_op jit(solution)/shard_map/ppermute | solution.py:226
  102.1 6.1 %collective-permute-start.11 = (bf16[48,1024]{1,0:T(8,128)(2,1)S(1)}, bf16[48,1024]{1,0:T(8,128)(2,1)S(1)}, u32[]{:S(2)}, u32[]{:S(2)}) collective-permute-start(bf16[48,1024]{1,0:T(8,128)(2,1)S(1)} %get-tuple-element.39), channel_id=1, source_target_pairs={{0,6},{1,7},{2,0},{3,1},{4,2},{5,3},{6,4},{7,5},{8,14},{9,15},{10,... | collective-permute-start | bytes 294920 | tf_op jit(solution)/shard_map/ppermute | solution.py:226

commit v11 on v10

--- a/solution.py
+++ b/solution.py
@@ -156,21 +156,8 @@
     return copies
 
 
-def products(pair, copies, held, takes):
-    for n in range(4):
-        copies[n].wait()
-        first, outs = takes[n // 2]
-        part = dot(pair[ROWS * first : ROWS * (first + len(outs)), :], held[n]).astype(BF)
-        at = KV * (n % 2)
-        for d, out in enumerate(outs):
-            out[:, at : at + KV] = part[ROWS * d : ROWS * d + ROWS, :]
-
-
-HELD = [pltpu.VMEM((4, G, KV), BF), pltpu.SemaphoreType.DMA((4,))]
-
-
-def product_far(recv, passage_of, proj):
-    def kernel(recv, passage, proj, pair, l1, l2, r2, r3, wide_q, wide_p, held, sems):
+def product(recv, passage_of, proj):
+    def kernel(recv, passage, proj, l0, l1, l2, l3, r0, r1, r2, r3, wide_q, wide_p, pair, held, sems):
         copies = fetch(proj, held, sems)
         x = lax.axis_index("px")
         r, c = iota((256, 256), 0), iota((256, 256), 1)
@@ -187,35 +174,23 @@
         for i in range(NX):
             at = pl.multiple_of(((i - x) & 3) * ROWS, 32)
             pair[pl.ds(at, ROWS), :] = summed[ROWS * i : ROWS * i + ROWS, :]
-        products(pair, copies, held, ((1, (l1, l2)), (2, (r2, r3))))
+        for n in range(4):
+            copies[n].wait()
+            part = dot(pair[...], held[n]).astype(BF)
+            at = KV * (n % 2)
+            for d, out in enumerate(((l0, l1, l2, l3), (r0, r1, r2, r3))[n // 2]):
+                out[:, at : at + KV] = part[ROWS * d : ROWS * d + ROWS, :]
 
     return call(
         kernel,
-        [array(PAIRS, G)] + [array(ROWS, K // 2)] * 4,
-        2_500_000_000,
+        [array(ROWS, K // 2)] * 8,
+        4_000_000_000,
         12_000_000,
         vmem=44,
         in_specs=[WHOLE, WHOLE, HBM],
-        scratch_shapes=[pltpu.VMEM((PAIRS, G), BF)] * 2 + HELD,
+        scratch_shapes=[pltpu.VMEM((PAIRS, G), BF)] * 3
+        + [pltpu.VMEM((4, G, KV), BF), pltpu.SemaphoreType.DMA((4,))],
     )(recv, passage_of.reshape(1, PAIRS), proj)
-
-
-def product_near(pair, proj):
-    def kernel(pair, proj, l3, l0, r0, r1, turned, held, sems):
-        copies = fetch(proj, held, sems)
-        turned[:ROWS, :] = pair[3 * ROWS :, :]
-        turned[ROWS:, :] = pair[: 3 * ROWS, :]
-        products(turned, copies, held, ((0, (l3, l0)), (1, (r0, r1))))
-
-    return call(
-        kernel,
-        [array(ROWS, K // 2)] * 4,
-        1_700_000_000,
-        10_000_000,
-        vmem=44,
-        in_specs=[WHOLE, HBM],
-        scratch_shapes=[pltpu.VMEM((PAIRS, G), BF)] + HELD,
-    )(pair, proj)
 
 
 def add(a, b):
@@ -227,10 +202,9 @@
 
 
 def across_x(recv, passage_of, proj):
-    pair, l1, l2, r2, r3 = product_far(recv, passage_of, proj)
+    l0, l1, l2, l3, r0, r1, r2, r3 = product(recv, passage_of, proj)
     far_l = shift(l2, "px", NX, 1)
     far_r = shift(r2, "px", NX, -1)
-    l3, l0, r0, r1 = product_near(pair, proj)
     got_l = shift(l3, "px", NX, -1)
     got_r = shift(r1, "px", NX, 1)
     sum_l = shift(add(l1, far_l), "px", NX, 1)

time: 109 us -> 110 us (level)
  Pallas kernels: 27.9 us -> 24.9 us
  waiting for transfers between devices: 48.6 us -> 51.6 us
    pallas_call x2 -> x1, Pallas kernels: 9.2 us -> 6.18 us  [product(): call(kernel, [array(ROWS, K // 2)] * 8, 4000000000, 12000000, vmem=44, in...]
    ppermute x12, waiting for transfers between devices: 23.9 us -> 26.8 us  [shift(): return lax.ppermute(x, axis, [(i, (i + by) % size) for i in range(size)])]
    ppermute x12, starting transfers between devices: 20.5 us -> 21.6 us  [shift(): return lax.ppermute(x, axis, [(i, (i + by) % size) for i in range(size)])]
  transfers between devices with their start and end apart: 13 -> 13, of which waited for: 9 -> 9; matrix products, arithmetic and copies ran while one was open for 0% -> 0% of each run, Pallas kernels for 15% -> 11%
where the time goes in v11:
time: 110 us
  waiting for transfers between devices  51.6 us (47%)
  starting transfers between devices  33.3 us (30%)
  Pallas kernels  24.9 us (23%)
    ppermute x12, waiting for transfers between devices, shift(): return lax.ppermute(x, axis, [(i, (i + by) % size) for i in range(size)])  26.8 us
    all_to_all x1, waiting for transfers between devices, local(): lax.all_to_all(grads(q_fact, p_fact, q_cot, p_cot), ('px', 'pz'), 0, 0, t...  24.7 us
    ppermute x12, starting transfers between devices, shift(): return lax.ppermute(x, axis, [(i, (i + by) % size) for i in range(size)])  21.6 us
    pallas_call x1, Pallas kernels, permuted(): call(kernel, array(12, G, KV), 2 * G * G * K, 16000000, vmem=57, in_specs...  12.3 us
    all_to_all x1, starting transfers between devices, local(): lax.all_to_all(grads(q_fact, p_fact, q_cot, p_cot), ('px', 'pz'), 0, 0, t...  11.7 us
    pallas_call x1, Pallas kernels, product(): call(kernel, [array(ROWS, K // 2)] * 8, 4000000000, 12000000, vmem=44, in...  6.18 us
    pallas_call x1, Pallas kernels, grads(): call(kernel, array(N, 2 * ROWS, 128), 800000000, 5500000, vmem=60, grid=(...  4.61 us
  transfers between devices with their start and end apart: 13, of which 9 were waited for; matrix products, arithmetic and copies ran while one was open for 0% of the time, Pallas kernels for 11%

profile of v11, /device:TPU:14, one launch (start us, length us, event | category | flops | bytes accessed | tf_op | source)
XLA Modules:
  0.0 110.0 jit_solution(3698355177149840988)
XLA Ops:
  0.0 4.6 %shard_map.64 = bf16[32,192,128]{2,1,0:T(8,128)(2,1)} custom-call(bf16[32,384]{1,0:T(8,128)(2,1)} %bitcast.3, bf16[32,576]{1,0:T(8,128)(2,1)} %bitcast.2, bf16[384,2048]{1,0:T(8,128)(2,1)} %q_cot.1, bf16[576,2048]{1,0:T(8,128)(2,1)} %p_cot.1), custom_call_target="tpu_custom_call" | custom-call | flops 800000000 | bytes 5500000 | tf_op jit(solution)/shard_map/pallas_call | solution.py:83
  4.6 0.0 copy-start
  4.6 11.7 %all-to-all-start = ((bf16[32,192,128]{2,1,0:T(8,128)(2,1)}), bf16[32,192,128]{2,1,0:T(8,128)(2,1)S(1)}, u32[]{:S(2)}, u32[]{:S(2)}) async-start(bf16[32,192,128]{2,1,0:T(8,128)(2,1)} %shard_map.64), calls=%async_computation | async-start | bytes 3145728 | tf_op jit(solution)/shard_map/all_to_all | solution.py:268
  16.3 0.0 copy-done
  16.4 12.3 %shard_map.65.proj = bf16[12,1024,1024]{2,1,0:T(8,128)(2,1)} custom-call(bf16[1024,4096]{1,0:T(8,128)(2,1)} %proj.1), custom_call_target="tpu_custom_call" | custom-call | flops 8589934592 | bytes 16000000 | tf_op jit(solution)/shard_map/pallas_call | solution.py:123
  28.7 24.7 %all-to-all-done.recv = bf16[32,192,128]{2,1,0:T(8,128)(2,1)S(1)} async-done(((bf16[32,192,128]{2,1,0:T(8,128)(2,1)}), bf16[32,192,128]{2,1,0:T(8,128)(2,1)S(1)}, u32[]{:S(2)}, u32[]{:S(2)}) %all-to-all-start) | async-done | bytes 1572896 | tf_op jit(solution)/shard_map/all_to_all | solution.py:268
  53.4 6.2 %shard_map.66 = (bf16[96,2048]{1,0:T(8,128)(2,1)S(1)}, bf16[96,2048]{1,0:T(8,128)(2,1)S(1)}, bf16[96,2048]{1,0:T(8,128)(2,1)S(1)}, bf16[96,2048]{1,0:T(8,128)(2,...) custom-call(bf16[32,192,128]{2,1,0:T(8,128)(2,1)S(1)} %all-to-all-do, ...), custom_call_target="tpu_custom_call" | custom-call | flops 4000000000 | bytes 12000000 | tf_op jit(solution)/shard_map/pallas_call | solution.py:184
  59.6 2.7 %collective-permute-start = (bf16[96,2048]{1,0:T(8,128)(2,1)S(1)}, bf16[96,2048]{1,0:T(8,128)(2,1)S(1)}, u32[]{:S(2)}, u32[]{:S(2)}) collective-permute-start(bf16[96,2048]{1,0:T(8,128)(2,1)S(1)} %get-tuple-element.23), channel_id=1, source_target_pairs={{0,8},{8,16},{16,24},{24,0},{1,9},{9,17},{17,25},{25,1},{2,10},{10... | collective-permute-start | bytes 1179656 | tf_op jit(solution)/shard_map/ppermute | solution.py:201
  62.3 0.0 collective-permute-start.2
  62.3 0.1 collective-permute-start.4
  62.5 3.1 %collective-permute-start.5 = (bf16[96,2048]{1,0:T(8,128)(2,1)S(1)}, bf16[96,2048]{1,0:T(8,128)(2,1)S(1)}, u32[]{:S(2)}, u32[]{:S(2)}) collective-permute-start(bf16[96,2048]{1,0:T(8,128)(2,1)S(1)} %get-tuple-element.27), channel_id=1, source_target_pairs={{0,8},{8,16},{16,24},{24,0},{1,9},{9,17},{17,25},{25,1},{2,10},{10... | collective-permute-start | bytes 1179656 | tf_op jit(solution)/shard_map/ppermute | solution.py:201
  65.6 6.3 %collective-permute-done = bf16[96,2048]{1,0:T(8,128)(2,1)S(1)} collective-permute-done((bf16[96,2048]{1,0:T(8,128)(2,1)S(1)}, bf16[96,2048]{1,0:T(8,128)(2,1)S(1)}, u32[]{:S(2)}, u32[]{:S(2)}) %collective-permute-start) | collective-permute-done | bytes 393248 | tf_op jit(solution)/shard_map/ppermute | solution.py:201
  71.9 0.1 add_convert_fusion.1
  72.0 3.7 %collective-permute-start.1 = (bf16[96,2048]{1,0:T(8,128)(2,1)S(1)}, bf16[96,2048]{1,0:T(8,128)(2,1)S(1)}, u32[]{:S(2)}, u32[]{:S(2)}) collective-permute-start(bf16[96,2048]{1,0:T(8,128)(2,1)S(1)} %add_convert_fusion.1), channel_id=1, source_target_pairs={{0,8},{8,16},{16,24},{24,0},{1,9},{9,17},{17,25},{25,1},{2,10},{10... | collective-permute-start | bytes 1179656 | tf_op jit(solution)/shard_map/ppermute | solution.py:201
  75.8 0.0 collective-permute-done.2
  75.8 0.1 add_convert_fusion
  75.9 0.1 collective-permute-start.3
  76.0 8.0 %collective-permute-done.4.l1 = bf16[96,2048]{1,0:T(8,128)(2,1)S(1)} collective-permute-done((bf16[96,2048]{1,0:T(8,128)(2,1)S(1)}, bf16[96,2048]{1,0:T(8,128)(2,1)S(1)}, u32[]{:S(2)}, u32[]{:S(2)}) %collective-permute-start.4) | collective-permute-done | bytes 393248 | tf_op jit(solution)/shard_map/ppermute | solution.py:201
  83.9 0.0 collective-permute-done.5.r1
  83.9 1.1 %collective-permute-done.1.l2 = bf16[96,2048]{1,0:T(8,128)(2,1)S(1)} collective-permute-done((bf16[96,2048]{1,0:T(8,128)(2,1)S(1)}, bf16[96,2048]{1,0:T(8,128)(2,1)S(1)}, u32[]{:S(2)}, u32[]{:S(2)}) %collective-permute-start.1) | collective-permute-done | bytes 393248 | tf_op jit(solution)/shard_map/ppermute | solution.py:201
  85.1 3.1 %collective-permute-done.3.r2 = bf16[96,2048]{1,0:T(8,128)(2,1)S(1)} collective-permute-done((bf16[96,2048]{1,0:T(8,128)(2,1)S(1)}, bf16[96,2048]{1,0:T(8,128)(2,1)S(1)}, u32[]{:S(2)}, u32[]{:S(2)}) %collective-permute-start.3) | collective-permute-done | bytes 393248 | tf_op jit(solution)/shard_map/ppermute | solution.py:201
  88.2 0.9 shard_map.67
  89.1 3.4 %collective-permute-start.6 = (bf16[2,48,1024]{2,1,0:T(8,128)(2,1)S(1)}, bf16[2,48,1024]{2,1,0:T(8,128)(2,1)S(1)}, u32[]{:S(2)}, u32[]{:S(2)}) collective-permute-start(bf16[2,48,1024]{2,1,0:T(8,128)(2,1)S(1)} %get-tuple-element.30), channel_id=1, source_target_pairs={{0,1},{1,2},{2,3},{3,4},{4,5},{5,6},{6,7},{7,0},{8,9},{9,10},{10,1... | collective-permute-start | bytes 589832 | tf_op jit(solution)/shard_map/ppermute | solution.py:201
  92.5 0.0 collective-permute-start.7
  92.5 1.5 %collective-permute-start.8 = (bf16[48,512]{1,0:T(8,128)(2,1)S(1)}, bf16[48,512]{1,0:T(8,128)(2,1)S(1)}, u32[]{:S(2)}, u32[]{:S(2)}) collective-permute-start(bf16[48,512]{1,0:T(8,128)(2,1)S(1)} %get-tuple-element.32), channel_id=1, source_target_pairs={{0,2},{1,3},{2,4},{3,5},{4,6},{5,7},{6,0},{7,1},{8,10},{9,11},{10,... | collective-permute-start | bytes 147464 | tf_op jit(solution)/shard_map/ppermute | solution.py:201
  94.1 2.6 %collective-permute-start.9 = (bf16[48,512]{1,0:T(8,128)(2,1)S(1)}, bf16[48,512]{1,0:T(8,128)(2,1)S(1)}, u32[]{:S(2)}, u32[]{:S(2)}) collective-permute-start(bf16[48,512]{1,0:T(8,128)(2,1)S(1)} %get-tuple-element.33), channel_id=1, source_target_pairs={{0,6},{1,7},{2,0},{3,1},{4,2},{5,3},{6,4},{7,5},{8,14},{9,15},{10,... | collective-permute-start | bytes 147464 | tf_op jit(solution)/shard_map/ppermute | solution.py:201
  96.6 2.7 %collective-permute-done.8.far_up = bf16[48,512]{1,0:T(8,128)(2,1)S(1)} collective-permute-done((bf16[48,512]{1,0:T(8,128)(2,1)S(1)}, bf16[48,512]{1,0:T(8,128)(2,1)S(1)}, u32[]{:S(2)}, u32[]{:S(2)}) %collective-permute-start.8) | collective-permute-done | bytes 49184 | tf_op jit(solution)/shard_map/ppermute | solution.py:201
  99.3 0.0 collective-permute-done.9.far_down
  99.3 0.0 collective-permute-done.6.odd_up
  99.3 0.2 collective-permute-done.7.odd_down
  99.6 0.1 shard_map.68
  99.6 3.6 %collective-permute-start.10 = (bf16[48,1024]{1,0:T(8,128)(2,1)S(1)}, bf16[48,1024]{1,0:T(8,128)(2,1)S(1)}, u32[]{:S(2)}, u32[]{:S(2)}) collective-permute-start(bf16[48,1024]{1,0:T(8,128)(2,1)S(1)} %get-tuple-element.36), channel_id=1, source_target_pairs={{0,2},{1,3},{2,4},{3,5},{4,6},{5,7},{6,0},{7,1},{8,10},{9,11},{10,... | collective-permute-start | bytes 294920 | tf_op jit(solution)/shard_map/ppermute | solution.py:201
  103.2 0.6 collective-permute-start.11
  103.8 2.7 %collective-permute-done.10.up = bf16[48,1024]{1,0:T(8,128)(2,1)S(1)} collective-permute-done((bf16[48,1024]{1,0:T(8,128)(2,1)S(1)}, bf16[48,1024]{1,0:T(8,128)(2,1)S(1)}, u32[]{:S(2)}, u32[]{:S(2)}) %collective-permute-start.10) | collective-permute-done | bytes 98336 | tf_op jit(solution)/shard_map/ppermute | solution.py:201
  106.5 2.7 %collective-permute-done.11.down = bf16[48,1024]{1,0:T(8,128)(2,1)S(1)} collective-permute-done((bf16[48,1024]{1,0:T(8,128)(2,1)S(1)}, bf16[48,1024]{1,0:T(8,128)(2,1)S(1)}, u32[]{:S(2)}, u32[]{:S(2)}) %collective-permute-start.11) | collective-permute-done | bytes 98336 | tf_op jit(solution)/shard_map/ppermute | solution.py:201
  109.2 0.8 shard_map.69
  (1 shorter events, 0.0 us)
Async XLA Ops:
  4.6 11.7 %copy-start = (s32[384]{0:T(512)S(1)}, s32[384]{0:T(512)}, u32[]{:S(2)}) copy-start(s32[384]{0:T(512)} %param.10) | copy-start | bytes 4612
  4.6 48.8 %all-to-all-start = ((bf16[32,192,128]{2,1,0:T(8,128)(2,1)}), bf16[32,192,128]{2,1,0:T(8,128)(2,1)S(1)}, u32[]{:S(2)}, u32[]{:S(2)}) async-start(bf16[32,192,128]{2,1,0:T(8,128)(2,1)} %shard_map.64), calls=%async_computation | async-start | bytes 3145728 | tf_op jit(solution)/shard_map/all_to_all | solution.py:268
  59.6 12.3 %collective-permute-start = (bf16[96,2048]{1,0:T(8,128)(2,1)S(1)}, bf16[96,2048]{1,0:T(8,128)(2,1)S(1)}, u32[]{:S(2)}, u32[]{:S(2)}) collective-permute-start(bf16[96,2048]{1,0:T(8,128)(2,1)S(1)} %get-tuple-element.23), channel_id=1, source_target_pairs={{0,8},{8,16},{16,24},{24,0},{1,9},{9,17},{17,25},{25,1},{2,10},{10... | collective-permute-start | bytes 1179656 | tf_op jit(solution)/shard_map/ppermute | solution.py:201
  62.3 13.5 %collective-permute-start.2 = (bf16[96,2048]{1,0:T(8,128)(2,1)S(1)}, bf16[96,2048]{1,0:T(8,128)(2,1)S(1)}, u32[]{:S(2)}, u32[]{:S(2)}) collective-permute-start(bf16[96,2048]{1,0:T(8,128)(2,1)S(1)} %get-tuple-element.25), channel_id=1, source_target_pairs={{0,24},{8,0},{16,8},{24,16},{1,25},{9,1},{17,9},{25,17},{2,26},{10... | collective-permute-start | bytes 1179656 | tf_op jit(solution)/shard_map/ppermute | solution.py:201
  62.3 21.6 %collective-permute-start.4 = (bf16[96,2048]{1,0:T(8,128)(2,1)S(1)}, bf16[96,2048]{1,0:T(8,128)(2,1)S(1)}, u32[]{:S(2)}, u32[]{:S(2)}) collective-permute-start(bf16[96,2048]{1,0:T(8,128)(2,1)S(1)} %get-tuple-element.26), channel_id=1, source_target_pairs={{0,24},{8,0},{16,8},{24,16},{1,25},{9,1},{17,9},{25,17},{2,26},{10... | collective-permute-start | bytes 1179656 | tf_op jit(solution)/shard_map/ppermute | solution.py:201
  62.5 21.5 %collective-permute-start.5 = (bf16[96,2048]{1,0:T(8,128)(2,1)S(1)}, bf16[96,2048]{1,0:T(8,128)(2,1)S(1)}, u32[]{:S(2)}, u32[]{:S(2)}) collective-permute-start(bf16[96,2048]{1,0:T(8,128)(2,1)S(1)} %get-tuple-element.27), channel_id=1, source_target_pairs={{0,8},{8,16},{16,24},{24,0},{1,9},{9,17},{17,25},{25,1},{2,10},{10... | collective-permute-start | bytes 1179656 | tf_op jit(solution)/shard_map/ppermute | solution.py:201
  72.0 13.0 %collective-permute-start.1 = (bf16[96,2048]{1,0:T(8,128)(2,1)S(1)}, bf16[96,2048]{1,0:T(8,128)(2,1)S(1)}, u32[]{:S(2)}, u32[]{:S(2)}) collective-permute-start(bf16[96,2048]{1,0:T(8,128)(2,1)S(1)} %add_convert_fusion.1), channel_id=1, source_target_pairs={{0,8},{8,16},{16,24},{24,0},{1,9},{9,17},{17,25},{25,1},{2,10},{10... | collective-permute-start | bytes 1179656 | tf_op jit(solution)/shard_map/ppermute | solution.py:201
  75.9 12.3 %collective-permute-start.3 = (bf16[96,2048]{1,0:T(8,128)(2,1)S(1)}, bf16[96,2048]{1,0:T(8,128)(2,1)S(1)}, u32[]{:S(2)}, u32[]{:S(2)}) collective-permute-start(bf16[96,2048]{1,0:T(8,128)(2,1)S(1)} %add_convert_fusion), channel_id=1, source_target_pairs={{0,24},{8,0},{16,8},{24,16},{1,25},{9,1},{17,9},{25,17},{2,26},{10... | collective-permute-start | bytes 1179656 | tf_op jit(solution)/shard_map/ppermute | solution.py:201
  89.1 10.3 %collective-permute-start.6 = (bf16[2,48,1024]{2,1,0:T(8,128)(2,1)S(1)}, bf16[2,48,1024]{2,1,0:T(8,128)(2,1)S(1)}, u32[]{:S(2)}, u32[]{:S(2)}) collective-permute-start(bf16[2,48,1024]{2,1,0:T(8,128)(2,1)S(1)} %get-tuple-element.30), channel_id=1, source_target_pairs={{0,1},{1,2},{2,3},{3,4},{4,5},{5,6},{6,7},{7,0},{8,9},{9,10},{10,1... | collective-permute-start | bytes 589832 | tf_op jit(solution)/shard_map/ppermute | solution.py:201
  92.5 7.1 %collective-permute-start.7 = (bf16[2,48,1024]{2,1,0:T(8,128)(2,1)S(1)}, bf16[2,48,1024]{2,1,0:T(8,128)(2,1)S(1)}, u32[]{:S(2)}, u32[]{:S(2)}) collective-permute-start(bf16[2,48,1024]{2,1,0:T(8,128)(2,1)S(1)} %get-tuple-element.31), channel_id=1, source_target_pairs={{0,7},{1,0},{2,1},{3,2},{4,3},{5,4},{6,5},{7,6},{8,15},{9,8},{10,9... | collective-permute-start | bytes 589832 | tf_op jit(solution)/shard_map/ppermute | solution.py:201
  92.5 6.8 %collective-permute-start.8 = (bf16[48,512]{1,0:T(8,128)(2,1)S(1)}, bf16[48,512]{1,0:T(8,128)(2,1)S(1)}, u32[]{:S(2)}, u32[]{:S(2)}) collective-permute-start(bf16[48,512]{1,0:T(8,128)(2,1)S(1)} %get-tuple-element.32), channel_id=1, source_target_pairs={{0,2},{1,3},{2,4},{3,5},{4,6},{5,7},{6,0},{7,1},{8,10},{9,11},{10,... | collective-permute-start | bytes 147464 | tf_op jit(solution)/shard_map/ppermute | solution.py:201
  94.1 5.3 %collective-permute-start.9 = (bf16[48,512]{1,0:T(8,128)(2,1)S(1)}, bf16[48,512]{1,0:T(8,128)(2,1)S(1)}, u32[]{:S(2)}, u32[]{:S(2)}) collective-permute-start(bf16[48,512]{1,0:T(8,128)(2,1)S(1)} %get-tuple-element.33), channel_id=1, source_target_pairs={{0,6},{1,7},{2,0},{3,1},{4,2},{5,3},{6,4},{7,5},{8,14},{9,15},{10,... | collective-permute-start | bytes 147464 | tf_op jit(solution)/shard_map/ppermute | solution.py:201
  99.6 6.9 %collective-permute-start.10 = (bf16[48,1024]{1,0:T(8,128)(2,1)S(1)}, bf16[48,1024]{1,0:T(8,128)(2,1)S(1)}, u32[]{:S(2)}, u32[]{:S(2)}) collective-permute-start(bf16[48,1024]{1,0:T(8,128)(2,1)S(1)} %get-tuple-element.36), channel_id=1, source_target_pairs={{0,2},{1,3},{2,4},{3,5},{4,6},{5,7},{6,0},{7,1},{8,10},{9,11},{10,... | collective-permute-start | bytes 294920 | tf_op jit(solution)/shard_map/ppermute | solution.py:201
  103.2 6.0 %collective-permute-start.11 = (bf16[48,1024]{1,0:T(8,128)(2,1)S(1)}, bf16[48,1024]{1,0:T(8,128)(2,1)S(1)}, u32[]{:S(2)}, u32[]{:S(2)}) collective-permute-start(bf16[48,1024]{1,0:T(8,128)(2,1)S(1)} %get-tuple-element.37), channel_id=1, source_target_pairs={{0,6},{1,7},{2,0},{3,1},{4,2},{5,3},{6,4},{7,5},{8,14},{9,15},{10,... | collective-permute-start | bytes 294920 | tf_op jit(solution)/shard_map/ppermute | solution.py:201

commit v12 on v10

--- a/solution.py
+++ b/solution.py
@@ -170,7 +170,7 @@
 
 
 def product_far(recv, passage_of, proj):
-    def kernel(recv, passage, proj, pair, l1, l2, r2, r3, wide_q, wide_p, held, sems):
+    def kernel(recv, passage, proj, pair, l2, r2, wide_q, wide_p, held, sems):
         copies = fetch(proj, held, sems)
         x = lax.axis_index("px")
         r, c = iota((256, 256), 0), iota((256, 256), 1)
@@ -187,12 +187,12 @@
         for i in range(NX):
             at = pl.multiple_of(((i - x) & 3) * ROWS, 32)
             pair[pl.ds(at, ROWS), :] = summed[ROWS * i : ROWS * i + ROWS, :]
-        products(pair, copies, held, ((1, (l1, l2)), (2, (r2, r3))))
+        products(pair, copies, held, ((2, (l2,)), (2, (r2,))))
 
     return call(
         kernel,
-        [array(PAIRS, G)] + [array(ROWS, K // 2)] * 4,
-        2_500_000_000,
+        [array(PAIRS, G)] + [array(ROWS, K // 2)] * 2,
+        2_000_000_000,
         12_000_000,
         vmem=44,
         in_specs=[WHOLE, WHOLE, HBM],
@@ -201,16 +201,16 @@
 
 
 def product_near(pair, proj):
-    def kernel(pair, proj, l3, l0, r0, r1, turned, held, sems):
+    def kernel(pair, proj, l3, l0, l1, r3, r0, r1, turned, held, sems):
         copies = fetch(proj, held, sems)
         turned[:ROWS, :] = pair[3 * ROWS :, :]
         turned[ROWS:, :] = pair[: 3 * ROWS, :]
-        products(turned, copies, held, ((0, (l3, l0)), (1, (r0, r1))))
+        products(turned, copies, held, ((0, (l3, l0, l1)), (0, (r3, r0, r1))))
 
     return call(
         kernel,
-        [array(ROWS, K // 2)] * 4,
-        1_700_000_000,
+        [array(ROWS, K // 2)] * 6,
+        2_500_000_000,
         10_000_000,
         vmem=44,
         in_specs=[WHOLE, HBM],
@@ -227,12 +227,13 @@
 
 
 def across_x(recv, passage_of, proj):
-    pair, l1, l2, r2, r3 = product_far(recv, passage_of, proj)
+    pair, l2, r2 = product_far(recv, passage_of, proj)
     far_l = shift(l2, "px", NX, 1)
     far_r = shift(r2, "px", NX, -1)
-    l3, l0, r0, r1 = product_near(pair, proj)
+    l3, l0, l1, r3, r0, r1 = product_near(pair, proj)
     got_l = shift(l3, "px", NX, -1)
     got_r = shift(r1, "px", NX, 1)
+    far_l, far_r = lax.optimization_barrier((far_l, far_r))
     sum_l = shift(add(l1, far_l), "px", NX, 1)
     sum_r = shift(add(r3, far_r), "px", NX, -1)
     return sum_l, sum_r, got_l, got_r, l0, r0

time: 109 us -> 109 us (level)
  waiting for transfers between devices: 48.6 us -> 47.2 us
    ppermute x12, waiting for transfers between devices: 23.9 us -> 22.5 us  [shift(): return lax.ppermute(x, axis, [(i, (i + by) % size) for i in range(size)])]
  transfers between devices with their start and end apart: 13 -> 13, of which waited for: 9 -> 7; matrix products, arithmetic and copies ran while one was open for 0% -> 0% of each run, Pallas kernels for 15% -> 16%
where the time goes in v12:
time: 109 us; the launch traced here: 108 us
  waiting for transfers between devices  47.2 us (43%)
  starting transfers between devices  32.9 us (30%)
  Pallas kernels  27.9 us (26%)
    all_to_all x1, waiting for transfers between devices, local(): lax.all_to_all(grads(q_fact, p_fact, q_cot, p_cot), ('px', 'pz'), 0, 0, t...  24.7 us
    ppermute x12, waiting for transfers between devices, shift(): return lax.ppermute(x, axis, [(i, (i + by) % size) for i in range(size)])  22.5 us
    ppermute x12, starting transfers between devices, shift(): return lax.ppermute(x, axis, [(i, (i + by) % size) for i in range(size)])  21.2 us
    pallas_call x1, Pallas kernels, permuted(): call(kernel, array(12, G, KV), 2 * G * G * K, 16000000, vmem=57, in_specs...  12.4 us
    all_to_all x1, starting transfers between devices, local(): lax.all_to_all(grads(q_fact, p_fact, q_cot, p_cot), ('px', 'pz'), 0, 0, t...  11.7 us
    pallas_call x1, Pallas kernels, product_near(): call(kernel, [array(ROWS, K // 2)] * 6, 2500000000, 10000000, vmem=44, in...  4.74 us
    pallas_call x1, Pallas kernels, grads(): call(kernel, array(N, 2 * ROWS, 128), 800000000, 5500000, vmem=60, grid=(...  4.6 us
    pallas_call x1, Pallas kernels, product_far(): call(kernel, [array(PAIRS, G)] + [array(ROWS, K // 2)] * 2, 2000000000, 1...  4.44 us
  transfers between devices with their start and end apart: 13, of which 7 were waited for; matrix products, arithmetic and copies ran while one was open for 0% of the time, Pallas kernels for 16%

profile of v12, /device:TPU:14, one launch (start us, length us, event | category | flops | bytes accessed | tf_op | source)
XLA Modules:
  0.0 108.3 jit_solution(12114752024637501325)
XLA Ops:
  0.0 4.6 %shard_map.64 = bf16[32,192,128]{2,1,0:T(8,128)(2,1)} custom-call(bf16[32,384]{1,0:T(8,128)(2,1)} %bitcast.3, bf16[32,576]{1,0:T(8,128)(2,1)} %bitcast.2, bf16[384,2048]{1,0:T(8,128)(2,1)} %q_cot.1, bf16[576,2048]{1,0:T(8,128)(2,1)} %p_cot.1), custom_call_target="tpu_custom_call" | custom-call | flops 800000000 | bytes 5500000 | tf_op jit(solution)/shard_map/pallas_call | solution.py:83
  4.6 0.0 copy-start
  4.6 11.7 %all-to-all-start = ((bf16[32,192,128]{2,1,0:T(8,128)(2,1)}), bf16[32,192,128]{2,1,0:T(8,128)(2,1)S(1)}, u32[]{:S(2)}, u32[]{:S(2)}) async-start(bf16[32,192,128]{2,1,0:T(8,128)(2,1)} %shard_map.64), calls=%async_computation | async-start | bytes 3145728 | tf_op jit(solution)/shard_map/all_to_all | solution.py:295
  16.3 0.0 copy-done
  16.4 12.4 %shard_map.65.proj = bf16[12,1024,1024]{2,1,0:T(8,128)(2,1)} custom-call(bf16[1024,4096]{1,0:T(8,128)(2,1)} %proj.1), custom_call_target="tpu_custom_call" | custom-call | flops 8589934592 | bytes 16000000 | tf_op jit(solution)/shard_map/pallas_call | solution.py:123
  28.7 24.7 %all-to-all-done.recv = bf16[32,192,128]{2,1,0:T(8,128)(2,1)S(1)} async-done(((bf16[32,192,128]{2,1,0:T(8,128)(2,1)}), bf16[32,192,128]{2,1,0:T(8,128)(2,1)S(1)}, u32[]{:S(2)}, u32[]{:S(2)}) %all-to-all-start) | async-done | bytes 1572896 | tf_op jit(solution)/shard_map/all_to_all | solution.py:295
  53.4 4.4 %shard_map.66 = (bf16[384,1024]{1,0:T(8,128)(2,1)S(1)}, bf16[96,2048]{1,0:T(8,128)(2,1)S(1)}, bf16[96,2048]{1,0:T(8,128)(2,1)S(1)}) custom-call(bf16[32,192,128]{2,1,0:T(8,128)(2,1)S(1)} %all-to-all-done.recv, s32[1,384]{1,0:T(1,128)S(1)} %reshape.3.passage, bf16[12,1024,1024]{2,1,0:T(8,128)(2,1)} %shard_map.65.proj), custom_call_target="tpu_custom_call" | custom-call | flops 2000000000 | bytes 12000000 | tf_op jit(solution)/shard_map/pallas_call | solution.py:192
  57.9 2.5 %collective-permute-start = (bf16[96,2048]{1,0:T(8,128)(2,1)S(1)}, bf16[96,2048]{1,0:T(8,128)(2,1)S(1)}, u32[]{:S(2)}, u32[]{:S(2)}) collective-permute-start(bf16[96,2048]{1,0:T(8,128)(2,1)S(1)} %get-tuple-element.27), channel_id=1, source_target_pairs={{0,8},{8,16},{16,24},{24,0},{1,9},{9,17},{17,25},{25,1},{2,10},{10... | collective-permute-start | bytes 1179656 | tf_op jit(solution)/shard_map/ppermute | solution.py:226
  60.4 0.0 collective-permute-start.1
  60.4 4.7 %shard_map.67 = (bf16[96,2048]{1,0:T(8,128)(2,1)S(1)}, bf16[96,2048]{1,0:T(8,128)(2,1)S(1)}, bf16[96,2048]{1,0:T(8,128)(2,1)S(1)}, bf16[96,2048]{1,0:T(8,128)(2,...) custom-call(bf16[384,1024]{1,0:T(8,128)(2,1)S(1)} %get-tuple-element.25.pair, ...), custom_call_target="tpu_custom_call" | custom-call | flops 2500000000 | bytes 10000000 | tf_op jit(solution)/shard_map/pallas_call | solution.py:210
  65.2 0.2 collective-permute-start.4
  65.4 3.2 %collective-permute-start.5 = (bf16[96,2048]{1,0:T(8,128)(2,1)S(1)}, bf16[96,2048]{1,0:T(8,128)(2,1)S(1)}, u32[]{:S(2)}, u32[]{:S(2)}) collective-permute-start(bf16[96,2048]{1,0:T(8,128)(2,1)S(1)} %get-tuple-element.33), channel_id=1, source_target_pairs={{0,8},{8,16},{16,24},{24,0},{1,9},{9,17},{17,25},{25,1},{2,10},{10... | collective-permute-start | bytes 1179656 | tf_op jit(solution)/shard_map/ppermute | solution.py:226
  68.6 0.0 collective-permute-done
  68.6 4.5 %collective-permute-done.1 = bf16[96,2048]{1,0:T(8,128)(2,1)S(1)} collective-permute-done((bf16[96,2048]{1,0:T(8,128)(2,1)S(1)}, bf16[96,2048]{1,0:T(8,128)(2,1)S(1)}, u32[]{:S(2)}, u32[]{:S(2)}) %collective-permute-start.1) | collective-permute-done | bytes 393248 | tf_op jit(solution)/shard_map/ppermute | solution.py:226
  73.0 0.1 add_convert_fusion
  73.1 0.1 collective-permute-start.3
  73.2 0.1 add_convert_fusion.1
  73.3 3.3 %collective-permute-start.2 = (bf16[96,2048]{1,0:T(8,128)(2,1)S(1)}, bf16[96,2048]{1,0:T(8,128)(2,1)S(1)}, u32[]{:S(2)}, u32[]{:S(2)}) collective-permute-start(bf16[96,2048]{1,0:T(8,128)(2,1)S(1)} %add_convert_fusion.1), channel_id=1, source_target_pairs={{0,8},{8,16},{16,24},{24,0},{1,9},{9,17},{17,25},{25,1},{2,10},{10... | collective-permute-start | bytes 1179656 | tf_op jit(solution)/shard_map/ppermute | solution.py:226
  76.6 4.8 %collective-permute-done.4.l1 = bf16[96,2048]{1,0:T(8,128)(2,1)S(1)} collective-permute-done((bf16[96,2048]{1,0:T(8,128)(2,1)S(1)}, bf16[96,2048]{1,0:T(8,128)(2,1)S(1)}, u32[]{:S(2)}, u32[]{:S(2)}) %collective-permute-start.4) | collective-permute-done | bytes 393248 | tf_op jit(solution)/shard_map/ppermute | solution.py:226
  81.5 0.0 collective-permute-done.5.r1
  81.5 4.8 %collective-permute-done.3.r2 = bf16[96,2048]{1,0:T(8,128)(2,1)S(1)} collective-permute-done((bf16[96,2048]{1,0:T(8,128)(2,1)S(1)}, bf16[96,2048]{1,0:T(8,128)(2,1)S(1)}, u32[]{:S(2)}, u32[]{:S(2)}) %collective-permute-start.3) | collective-permute-done | bytes 393248 | tf_op jit(solution)/shard_map/ppermute | solution.py:226
  86.2 0.0 collective-permute-done.2.l2
  86.2 0.9 shard_map.68
  87.1 3.4 %collective-permute-start.6 = (bf16[2,48,1024]{2,1,0:T(8,128)(2,1)S(1)}, bf16[2,48,1024]{2,1,0:T(8,128)(2,1)S(1)}, u32[]{:S(2)}, u32[]{:S(2)}) collective-permute-start(bf16[2,48,1024]{2,1,0:T(8,128)(2,1)S(1)} %get-tuple-element.36), channel_id=1, source_target_pairs={{0,1},{1,2},{2,3},{3,4},{4,5},{5,6},{6,7},{7,0},{8,9},{9,10},{10,1... | collective-permute-start | bytes 589832 | tf_op jit(solution)/shard_map/ppermute | solution.py:226
  90.6 0.1 collective-permute-start.7
  90.6 1.5 %collective-permute-start.8 = (bf16[48,512]{1,0:T(8,128)(2,1)S(1)}, bf16[48,512]{1,0:T(8,128)(2,1)S(1)}, u32[]{:S(2)}, u32[]{:S(2)}) collective-permute-start(bf16[48,512]{1,0:T(8,128)(2,1)S(1)} %get-tuple-element.38), channel_id=1, source_target_pairs={{0,2},{1,3},{2,4},{3,5},{4,6},{5,7},{6,0},{7,1},{8,10},{9,11},{10,... | collective-permute-start | bytes 147464 | tf_op jit(solution)/shard_map/ppermute | solution.py:226
  92.1 2.6 %collective-permute-start.9 = (bf16[48,512]{1,0:T(8,128)(2,1)S(1)}, bf16[48,512]{1,0:T(8,128)(2,1)S(1)}, u32[]{:S(2)}, u32[]{:S(2)}) collective-permute-start(bf16[48,512]{1,0:T(8,128)(2,1)S(1)} %get-tuple-element.39), channel_id=1, source_target_pairs={{0,6},{1,7},{2,0},{3,1},{4,2},{5,3},{6,4},{7,5},{8,14},{9,15},{10,... | collective-permute-start | bytes 147464 | tf_op jit(solution)/shard_map/ppermute | solution.py:226
  94.8 3.0 %collective-permute-done.8.far_up = bf16[48,512]{1,0:T(8,128)(2,1)S(1)} collective-permute-done((bf16[48,512]{1,0:T(8,128)(2,1)S(1)}, bf16[48,512]{1,0:T(8,128)(2,1)S(1)}, u32[]{:S(2)}, u32[]{:S(2)}) %collective-permute-start.8) | collective-permute-done | bytes 49184 | tf_op jit(solution)/shard_map/ppermute | solution.py:226
  97.8 0.0 collective-permute-done.9.far_down
  97.8 0.0 collective-permute-done.6.odd_up
  97.8 0.0 collective-permute-done.7.odd_down
  97.8 0.1 shard_map.69
  97.8 3.6 %collective-permute-start.10 = (bf16[48,1024]{1,0:T(8,128)(2,1)S(1)}, bf16[48,1024]{1,0:T(8,128)(2,1)S(1)}, u32[]{:S(2)}, u32[]{:S(2)}) collective-permute-start(bf16[48,1024]{1,0:T(8,128)(2,1)S(1)} %get-tuple-element.42), channel_id=1, source_target_pairs={{0,2},{1,3},{2,4},{3,5},{4,6},{5,7},{6,0},{7,1},{8,10},{9,11},{10,... | collective-permute-start | bytes 294920 | tf_op jit(solution)/shard_map/ppermute | solution.py:226
  101.5 0.6 collective-permute-start.11
  102.0 2.7 %collective-permute-done.10.up = bf16[48,1024]{1,0:T(8,128)(2,1)S(1)} collective-permute-done((bf16[48,1024]{1,0:T(8,128)(2,1)S(1)}, bf16[48,1024]{1,0:T(8,128)(2,1)S(1)}, u32[]{:S(2)}, u32[]{:S(2)}) %collective-permute-start.10) | collective-permute-done | bytes 98336 | tf_op jit(solution)/shard_map/ppermute | solution.py:226
  104.7 2.8 %collective-permute-done.11.down = bf16[48,1024]{1,0:T(8,128)(2,1)S(1)} collective-permute-done((bf16[48,1024]{1,0:T(8,128)(2,1)S(1)}, bf16[48,1024]{1,0:T(8,128)(2,1)S(1)}, u32[]{:S(2)}, u32[]{:S(2)}) %collective-permute-start.11) | collective-permute-done | bytes 98336 | tf_op jit(solution)/shard_map/ppermute | solution.py:226
  107.5 0.8 shard_map.70
  (1 shorter events, 0.0 us)
Async XLA Ops:
  4.6 11.7 %copy-start = (s32[384]{0:T(512)S(1)}, s32[384]{0:T(512)}, u32[]{:S(2)}) copy-start(s32[384]{0:T(512)} %param.10) | copy-start | bytes 4612
  4.6 48.8 %all-to-all-start = ((bf16[32,192,128]{2,1,0:T(8,128)(2,1)}), bf16[32,192,128]{2,1,0:T(8,128)(2,1)S(1)}, u32[]{:S(2)}, u32[]{:S(2)}) async-start(bf16[32,192,128]{2,1,0:T(8,128)(2,1)} %shard_map.64), calls=%async_computation | async-start | bytes 3145728 | tf_op jit(solution)/shard_map/all_to_all | solution.py:295
  57.9 10.7 %collective-permute-start = (bf16[96,2048]{1,0:T(8,128)(2,1)S(1)}, bf16[96,2048]{1,0:T(8,128)(2,1)S(1)}, u32[]{:S(2)}, u32[]{:S(2)}) collective-permute-start(bf16[96,2048]{1,0:T(8,128)(2,1)S(1)} %get-tuple-element.27), channel_id=1, source_target_pairs={{0,8},{8,16},{16,24},{24,0},{1,9},{9,17},{17,25},{25,1},{2,10},{10... | collective-permute-start | bytes 1179656 | tf_op jit(solution)/shard_map/ppermute | solution.py:226
  60.4 12.6 %collective-permute-start.1 = (bf16[96,2048]{1,0:T(8,128)(2,1)S(1)}, bf16[96,2048]{1,0:T(8,128)(2,1)S(1)}, u32[]{:S(2)}, u32[]{:S(2)}) collective-permute-start(bf16[96,2048]{1,0:T(8,128)(2,1)S(1)} %get-tuple-element.28), channel_id=1, source_target_pairs={{0,24},{8,0},{16,8},{24,16},{1,25},{9,1},{17,9},{25,17},{2,26},{10... | collective-permute-start | bytes 1179656 | tf_op jit(solution)/shard_map/ppermute | solution.py:226
  65.2 16.3 %collective-permute-start.4 = (bf16[96,2048]{1,0:T(8,128)(2,1)S(1)}, bf16[96,2048]{1,0:T(8,128)(2,1)S(1)}, u32[]{:S(2)}, u32[]{:S(2)}) collective-permute-start(bf16[96,2048]{1,0:T(8,128)(2,1)S(1)} %get-tuple-element.32), channel_id=1, source_target_pairs={{0,24},{8,0},{16,8},{24,16},{1,25},{9,1},{17,9},{25,17},{2,26},{10... | collective-permute-start | bytes 1179656 | tf_op jit(solution)/shard_map/ppermute | solution.py:226
  65.4 16.1 %collective-permute-start.5 = (bf16[96,2048]{1,0:T(8,128)(2,1)S(1)}, bf16[96,2048]{1,0:T(8,128)(2,1)S(1)}, u32[]{:S(2)}, u32[]{:S(2)}) collective-permute-start(bf16[96,2048]{1,0:T(8,128)(2,1)S(1)} %get-tuple-element.33), channel_id=1, source_target_pairs={{0,8},{8,16},{16,24},{24,0},{1,9},{9,17},{17,25},{25,1},{2,10},{10... | collective-permute-start | bytes 1179656 | tf_op jit(solution)/shard_map/ppermute | solution.py:226
  73.1 13.1 %collective-permute-start.3 = (bf16[96,2048]{1,0:T(8,128)(2,1)S(1)}, bf16[96,2048]{1,0:T(8,128)(2,1)S(1)}, u32[]{:S(2)}, u32[]{:S(2)}) collective-permute-start(bf16[96,2048]{1,0:T(8,128)(2,1)S(1)} %add_convert_fusion), channel_id=1, source_target_pairs={{0,24},{8,0},{16,8},{24,16},{1,25},{9,1},{17,9},{25,17},{2,26},{10... | collective-permute-start | bytes 1179656 | tf_op jit(solution)/shard_map/ppermute | solution.py:226
  73.3 12.9 %collective-permute-start.2 = (bf16[96,2048]{1,0:T(8,128)(2,1)S(1)}, bf16[96,2048]{1,0:T(8,128)(2,1)S(1)}, u32[]{:S(2)}, u32[]{:S(2)}) collective-permute-start(bf16[96,2048]{1,0:T(8,128)(2,1)S(1)} %add_convert_fusion.1), channel_id=1, source_target_pairs={{0,8},{8,16},{16,24},{24,0},{1,9},{9,17},{17,25},{25,1},{2,10},{10... | collective-permute-start | bytes 1179656 | tf_op jit(solution)/shard_map/ppermute | solution.py:226
  87.1 10.6 %collective-permute-start.6 = (bf16[2,48,1024]{2,1,0:T(8,128)(2,1)S(1)}, bf16[2,48,1024]{2,1,0:T(8,128)(2,1)S(1)}, u32[]{:S(2)}, u32[]{:S(2)}) collective-permute-start(bf16[2,48,1024]{2,1,0:T(8,128)(2,1)S(1)} %get-tuple-element.36), channel_id=1, source_target_pairs={{0,1},{1,2},{2,3},{3,4},{4,5},{5,6},{6,7},{7,0},{8,9},{9,10},{10,1... | collective-permute-start | bytes 589832 | tf_op jit(solution)/shard_map/ppermute | solution.py:226
  90.6 7.2 %collective-permute-start.7 = (bf16[2,48,1024]{2,1,0:T(8,128)(2,1)S(1)}, bf16[2,48,1024]{2,1,0:T(8,128)(2,1)S(1)}, u32[]{:S(2)}, u32[]{:S(2)}) collective-permute-start(bf16[2,48,1024]{2,1,0:T(8,128)(2,1)S(1)} %get-tuple-element.37), channel_id=1, source_target_pairs={{0,7},{1,0},{2,1},{3,2},{4,3},{5,4},{6,5},{7,6},{8,15},{9,8},{10,9... | collective-permute-start | bytes 589832 | tf_op jit(solution)/shard_map/ppermute | solution.py:226
  90.6 7.1 %collective-permute-start.8 = (bf16[48,512]{1,0:T(8,128)(2,1)S(1)}, bf16[48,512]{1,0:T(8,128)(2,1)S(1)}, u32[]{:S(2)}, u32[]{:S(2)}) collective-permute-start(bf16[48,512]{1,0:T(8,128)(2,1)S(1)} %get-tuple-element.38), channel_id=1, source_target_pairs={{0,2},{1,3},{2,4},{3,5},{4,6},{5,7},{6,0},{7,1},{8,10},{9,11},{10,... | collective-permute-start | bytes 147464 | tf_op jit(solution)/shard_map/ppermute | solution.py:226
  92.1 5.6 %collective-permute-start.9 = (bf16[48,512]{1,0:T(8,128)(2,1)S(1)}, bf16[48,512]{1,0:T(8,128)(2,1)S(1)}, u32[]{:S(2)}, u32[]{:S(2)}) collective-permute-start(bf16[48,512]{1,0:T(8,128)(2,1)S(1)} %get-tuple-element.39), channel_id=1, source_target_pairs={{0,6},{1,7},{2,0},{3,1},{4,2},{5,3},{6,4},{7,5},{8,14},{9,15},{10,... | collective-permute-start | bytes 147464 | tf_op jit(solution)/shard_map/ppermute | solution.py:226
  97.8 6.9 %collective-permute-start.10 = (bf16[48,1024]{1,0:T(8,128)(2,1)S(1)}, bf16[48,1024]{1,0:T(8,128)(2,1)S(1)}, u32[]{:S(2)}, u32[]{:S(2)}) collective-permute-start(bf16[48,1024]{1,0:T(8,128)(2,1)S(1)} %get-tuple-element.42), channel_id=1, source_target_pairs={{0,2},{1,3},{2,4},{3,5},{4,6},{5,7},{6,0},{7,1},{8,10},{9,11},{10,... | collective-permute-start | bytes 294920 | tf_op jit(solution)/shard_map/ppermute | solution.py:226
  101.5 6.1 %collective-permute-start.11 = (bf16[48,1024]{1,0:T(8,128)(2,1)S(1)}, bf16[48,1024]{1,0:T(8,128)(2,1)S(1)}, u32[]{:S(2)}, u32[]{:S(2)}) collective-permute-start(bf16[48,1024]{1,0:T(8,128)(2,1)S(1)} %get-tuple-element.43), channel_id=1, source_target_pairs={{0,6},{1,7},{2,0},{3,1},{4,2},{5,3},{6,4},{7,5},{8,14},{9,15},{10,... | collective-permute-start | bytes 294920 | tf_op jit(solution)/shard_map/ppermute | solution.py:226
